TPU v7x, 32 devices: a whole 2x2x4 slice. The times are simulated.
32 devices in a mesh: fsdp: 4 (over y, x), ctx: 2 (over core), tp: 4 (over z).
Axes of the slice: x: 2, y: 2, z: 4, core: 2. Of those that a mesh axis runs over, the one named last changes fastest.
Arguments:
- tokens: bfloat16 [16384, 1024], P(('fsdp', 'ctx')), may hold values from -6 to 6
- norm_gain: bfloat16 [1024], P(('fsdp', 'ctx')), may hold values from 0.5 to 1.5
- inner_weight: bfloat16 [2, 1024, 2048], P(None, ('fsdp', 'ctx'), 'tp'), may hold values from -0.1875 to 0.1875
- state_weight: bfloat16 [1024, 256], P(('fsdp', 'ctx')), may hold values from -0.1875 to 0.1875
- step_weight: bfloat16 [1024, 32], P(('fsdp', 'ctx'), 'tp'), may hold values from -0.1875 to 0.1875
- inner_taps: float32 [5, 2048], P(None, 'tp'), may hold values from -3 to 3
- state_taps: float32 [5, 256], replicated, may hold values from -3 to 3
- step_bias: float32 [32], P('tp'), may hold values from -4 to -1
- log_rate: float32 [32], P('tp'), may hold values from -2.5 to 1.5
- skip_gain: float32 [32], P('tp'), may hold values from 0.5 to 1.5
- gated_gain: float32 [2048], P('tp'), may hold values from 0.5 to 1.5
- out_weight: bfloat16 [2048, 1024], P('tp', ('fsdp', 'ctx')), may hold values from -0.125 to 0.125
- out_grad: bfloat16 [16384, 1024], P(('fsdp', 'ctx')), may hold values from -6 to 6
- positions: int32 [16384], P(('fsdp', 'ctx')), may hold values from -1 to 4095, as said below
Outputs:
- mixed_out: bfloat16 [16384, 1024], P(('fsdp', 'ctx'))
- tokens_grad: float32 [16384, 1024], P(('fsdp', 'ctx'))
- norm_gain_grad: float32 [1024], P(('fsdp', 'ctx'))
- inner_weight_grad: float32 [2, 1024, 2048], P(None, ('fsdp', 'ctx'), 'tp')
- state_weight_grad: float32 [1024, 256], P(('fsdp', 'ctx'))
- step_weight_grad: float32 [1024, 32], P(('fsdp', 'ctx'), 'tp')
- inner_taps_grad: float32 [5, 2048], P(None, 'tp')
- state_taps_grad: float32 [5, 256], replicated
- step_bias_grad: float32 [32], P('tp')
- log_rate_grad: float32 [32], P('tp')
- skip_gain_grad: float32 [32], P('tp')
- gated_gain_grad: float32 [2048], P('tp')
- out_weight_grad: float32 [2048, 1024], P('tp', ('fsdp', 'ctx'))
Inputs may be any that keep to these rules, and one draw needn't show every extreme that they name: `positions`: within each fsdp index's 4096 rows whole sequences lie end to end from the first row, each row holding its position in its sequence (0, 1, 2, ...); rows after the last sequence hold -1. Some fsdp index holds one sequence of 4096 rows and some has unused rows. In every fsdp index one sequence covers rows 2047 and 2048.
All inputs are finite; a program needn't handle non-finite values.
Results may differ from a plain program's by a relative error of at most 0.02.
Values may be sent and summed in bfloat16 or wider, within the bound.
No kernel may reach another device: no remote copies, remote signals or barrier semaphores. Data moves between devices by JAX's collectives and lax.ppermute only.
A program may use at most 192 MiB of HBM per device.

v0:
```python
import jax
import jax.numpy as jnp
from jax import lax
from jax.sharding import PartitionSpec as P

CONV = 4
STRETCH = 256
INNER = 2048


epsilon = 1e-05
highest = lax.Precision.HIGHEST


def shifted(x, axis, by):
    devices = lax.axis_size(axis)
    pairs = [(i, i + by) for i in range(devices) if 0 <= i + by < devices]
    return lax.ppermute(x, axis, pairs)


def entering(x, axis, join, neutral, backward):
    count = lax.axis_size(axis)
    place = lax.axis_index(axis)
    ahead = count - 1 - place if backward else place
    gathered = jax.tree.map(
        lambda a, kind: lax.all_gather(a.astype(kind), axis), x, (jnp.bfloat16, jnp.bfloat16)
    )
    state = jax.tree.map(lambda a, e: jnp.zeros_like(a) + jnp.asarray(e, a.dtype), x, neutral)

    def one(hop, state):
        source = count - 1 - hop if backward else hop
        return join(
            state,
            jax.tree.map(
                lambda a, own: lax.dynamic_index_in_dim(a, source, 0, False).astype(own.dtype),
                gathered,
                x,
            ),
        )

    return lax.fori_loop(0, ahead, one, state)


def chain_join(earlier, later):
    return (earlier[0] * later[0], earlier[1] * later[0][:, None, None] + later[1])


def per_device(
    tokens,
    norm_gain,
    inner_weight,
    state_weight,
    step_weight,
    inner_taps,
    state_taps,
    step_bias,
    log_rate,
    skip_gain,
    gated_gain,
    out_weight,
    out_grad,
    positions,
):
    fetched = (
        lax.all_gather(inner_weight, ("fsdp", "ctx"), axis=1, tiled=True),
        lax.all_gather(state_weight, ("fsdp", "ctx"), axis=0, tiled=True),
        lax.all_gather(step_weight, ("fsdp", "ctx"), axis=0, tiled=True),
        lax.all_gather(norm_gain, ("fsdp", "ctx"), axis=0, tiled=True),
        lax.all_gather(out_weight, ("fsdp", "ctx"), axis=1, tiled=True),
    )
    full_inner, full_state, full_step, full_gain, full_out = fetched
    row_count = tokens.shape[0]
    local_heads = step_bias.shape[0]
    local_inner = gated_gain.shape[0]
    head_size = local_inner // local_heads
    state_size = state_weight.shape[1] // 2
    stretch_count = row_count // STRETCH
    carry_rows = CONV - 1
    valid_rows = (positions >= 0).astype(jnp.float32)
    tok_float = tokens.astype(jnp.float32)
    scaling = lax.rsqrt(jnp.mean(tok_float * tok_float, axis=-1, keepdims=True) + epsilon)
    unit_rows = tok_float * scaling
    normed = (unit_rows * full_gain.astype(jnp.float32)[None, :]).astype(jnp.bfloat16)
    gate_pre = jnp.dot(normed, full_inner[0], preferred_element_type=jnp.float32)
    inner_in = jnp.dot(normed, full_inner[1], preferred_element_type=jnp.float32)
    state_in = jnp.dot(normed, full_state, preferred_element_type=jnp.float32)
    step_raw = jnp.dot(normed, full_step, preferred_element_type=jnp.float32)
    mixed_in = jnp.concatenate([inner_in, state_in], axis=1).astype(jnp.bfloat16)
    before = shifted(mixed_in[row_count - carry_rows :], "ctx", 1)
    extended = jnp.concatenate([before, mixed_in], axis=0).astype(jnp.float32)
    conv_taps = jnp.concatenate([inner_taps, state_taps], axis=1)
    lag_masks = [jnp.ones((row_count, 1), jnp.float32)] + [
        (positions >= offset).astype(jnp.float32)[:, None] for offset in range(1, CONV)
    ]
    conv_pre = jnp.broadcast_to(conv_taps[CONV][None, :], (row_count, conv_taps.shape[1]))
    for offset in range(CONV):
        window = extended[carry_rows - offset : carry_rows - offset + row_count]
        conv_pre = conv_pre + conv_taps[CONV - 1 - offset][None, :] * window * lag_masks[offset]
    convolved = jax.nn.silu(conv_pre)
    values = convolved[:, :local_inner].astype(jnp.bfloat16)
    state_keys = convolved[:, local_inner : local_inner + state_size].astype(jnp.bfloat16)
    state_queries = convolved[:, local_inner + state_size :].astype(jnp.bfloat16)
    steps_dt = jax.nn.softplus(step_raw + step_bias[None, :]) * valid_rows[:, None]
    decay_rate = -jnp.exp(log_rate)
    stretch_values = values.reshape(stretch_count, STRETCH, local_heads, head_size)
    stretch_keys = state_keys.reshape(stretch_count, STRETCH, state_size)
    stretch_queries = state_queries.reshape(stretch_count, STRETCH, state_size)
    stretch_dt = jnp.swapaxes(steps_dt.reshape(stretch_count, STRETCH, local_heads), 1, 2)
    stretch_pos = positions.reshape(stretch_count, STRETCH)
    places = jnp.arange(STRETCH)
    log_decay = jnp.cumsum(stretch_dt * decay_rate[None, :, None], axis=2)
    same_seq = (places[None, None, :] <= places[None, :, None]) & (
        places[None, :, None] - places[None, None, :] <= stretch_pos[:, :, None]
    )
    gram_matrix = jnp.einsum(
        "cin,cjn->cij", stretch_queries, stretch_keys, preferred_element_type=jnp.float32
    )
    log_spans = log_decay[:, :, :, None] - log_decay[:, :, None, :]
    mask_heads = same_seq[:, None, :, :]
    decays = jnp.where(mask_heads, jnp.exp(jnp.where(mask_heads, log_spans, 0.0)), 0.0)
    raw_mixing = gram_matrix[:, None] * decays * stretch_dt[:, :, None, :]
    mixing = raw_mixing.astype(jnp.bfloat16)
    within = jnp.einsum(
        "chij,cjhp->cihp", mixing, stretch_values, preferred_element_type=jnp.float32
    )
    last_pos = stretch_pos[:, STRETCH - 1]
    ending = (places[None, :] >= STRETCH - 1 - last_pos[:, None]).astype(jnp.float32)
    end_decay = jnp.exp(log_decay[:, :, STRETCH - 1 :] - log_decay)
    weight_end = ending[:, None, :] * end_decay * stretch_dt
    value_float = stretch_values.astype(jnp.float32)
    keys_float = stretch_keys.astype(jnp.float32)
    queries_float = stretch_queries.astype(jnp.float32)
    scaled = jnp.swapaxes(weight_end, 1, 2)[:, :, :, None] * value_float
    fresh_state = jnp.einsum("cjhp,cjn->chpn", scaled, keys_float, precision=highest)
    passing = (last_pos >= STRETCH).astype(jnp.float32)[:, None] * jnp.exp(
        log_decay[:, :, STRETCH - 1]
    )
    zero_state = jnp.zeros((local_heads, head_size, state_size), jnp.float32)
    unit_heads = jnp.ones((local_heads,), jnp.float32)
    local_enter = [zero_state]
    through_before = [unit_heads]
    for stretch_index in range(stretch_count):
        local_enter.append(
            passing[stretch_index][:, None, None] * local_enter[stretch_index]
            + fresh_state[stretch_index]
        )
        through_before.append(through_before[stretch_index] * passing[stretch_index])
    incoming = entering(
        (through_before[stretch_count], local_enter[stretch_count]),
        "ctx",
        chain_join,
        (unit_heads, zero_state),
        False,
    )[1]
    entering_state = jnp.stack(
        [
            through_before[stretch_index][:, None, None] * incoming + local_enter[stretch_index]
            for stretch_index in range(stretch_count)
        ]
    )
    carry_in = (stretch_pos >= places[None, :] + 1).astype(jnp.float32)[:, :, None] * jnp.exp(
        jnp.swapaxes(log_decay, 1, 2)
    )
    across_core = jnp.einsum("cin,chpn->cihp", queries_float, entering_state, precision=highest)
    across = carry_in[..., None] * across_core
    ssm_out = within + across + skip_gain[None, None, :, None] * value_float
    ssm_rows = ssm_out.reshape(row_count, local_inner)
    gate_act = jax.nn.silu(gate_pre)
    gated = ssm_rows * gate_act
    square_sum = lax.psum(jnp.sum(gated * gated, axis=-1), "tp")
    gated_scale = lax.rsqrt(square_sum / INNER + epsilon)[:, None]
    unit_gated = gated * gated_scale
    normed_out = (unit_gated * gated_gain[None, :] * valid_rows[:, None]).astype(jnp.bfloat16)
    branch_part = jnp.dot(normed_out, full_out, preferred_element_type=jnp.float32)
    branch = lax.psum(branch_part.astype(jnp.bfloat16), "tp").astype(jnp.float32)
    mixed_out = (tok_float + branch).astype(jnp.bfloat16)
    refetched = (
        lax.all_gather(inner_weight, ("fsdp", "ctx"), axis=1, tiled=True),
        lax.all_gather(state_weight, ("fsdp", "ctx"), axis=0, tiled=True),
        lax.all_gather(step_weight, ("fsdp", "ctx"), axis=0, tiled=True),
        lax.all_gather(norm_gain, ("fsdp", "ctx"), axis=0, tiled=True),
        lax.all_gather(out_weight, ("fsdp", "ctx"), axis=1, tiled=True),
    )
    full_inner, full_state, full_step, full_gain, full_out = refetched
    grad_normed_out = jnp.einsum(
        "rd,kd->rk", out_grad, full_out, preferred_element_type=jnp.float32
    )
    out_weight_grad = jnp.einsum(
        "rk,rd->kd", normed_out, out_grad, preferred_element_type=jnp.float32
    )
    gated_gain_grad = jnp.sum(grad_normed_out * unit_gated * valid_rows[:, None], axis=0)
    grad_unit = grad_normed_out * gated_gain[None, :] * valid_rows[:, None]
    row_dots = lax.psum(jnp.sum(grad_unit * gated, axis=-1), "tp")
    grad_gated = gated_scale * (
        grad_unit - gated * gated_scale * gated_scale * row_dots[:, None] / INNER
    )
    grad_ssm = (grad_gated * gate_act).astype(jnp.bfloat16)
    gate_sig = jax.nn.sigmoid(gate_pre)
    grad_gate = (grad_gated * ssm_rows * gate_sig * (1.0 + gate_pre * (1.0 - gate_sig))).astype(
        jnp.bfloat16
    )
    grad_stretches = grad_ssm.reshape(stretch_count, STRETCH, local_heads, head_size)
    grad_float = grad_stretches.astype(jnp.float32)
    skip_gain_grad = jnp.sum(grad_float * value_float, axis=(0, 1, 3))
    grad_values = skip_gain[None, None, :, None] * grad_float + jnp.einsum(
        "chij,cihp->cjhp", mixing, grad_stretches, preferred_element_type=jnp.float32
    )
    grad_mixing = jnp.einsum(
        "cihp,cjhp->chij", grad_stretches, stretch_values, preferred_element_type=jnp.float32
    )
    mixing_terms = grad_mixing * raw_mixing
    grad_logs = jnp.sum(mixing_terms, axis=3) - jnp.sum(mixing_terms, axis=2)
    grad_dt = jnp.sum(grad_mixing * gram_matrix[:, None] * decays, axis=2)
    grad_gram = jnp.sum(grad_mixing * decays * stretch_dt[:, :, None, :], axis=1).astype(
        jnp.bfloat16
    )
    grad_queries = jnp.einsum(
        "cij,cjn->cin", grad_gram, stretch_keys, preferred_element_type=jnp.float32
    )
    grad_keys = jnp.einsum(
        "cij,cin->cjn", grad_gram, stretch_queries, preferred_element_type=jnp.float32
    )
    grad_core = grad_float * carry_in[..., None]
    grad_queries = grad_queries + jnp.einsum(
        "cihp,chpn->cin", grad_core, entering_state, precision=highest
    )
    direct = jnp.einsum("cihp,cin->chpn", grad_core, queries_float, precision=highest)
    grad_logs = grad_logs + jnp.swapaxes(jnp.sum(grad_float * across, axis=3), 1, 2)
    back_local = [zero_state] * (stretch_count + 1)
    suffix = [unit_heads] * (stretch_count + 1)
    for stretch_index in range(stretch_count - 1, -1, -1):
        back_local[stretch_index] = (
            direct[stretch_index]
            + passing[stretch_index][:, None, None] * back_local[stretch_index + 1]
        )
        suffix[stretch_index] = suffix[stretch_index + 1] * passing[stretch_index]
    outgoing = entering(
        (suffix[0], back_local[0]), "ctx", chain_join, (unit_heads, zero_state), True
    )[1]
    grad_leave = jnp.stack(
        [
            back_local[stretch_index] + suffix[stretch_index][:, None, None] * outgoing
            for stretch_index in range(1, stretch_count + 1)
        ]
    )
    last_grad = jnp.sum(grad_leave * entering_state, axis=(2, 3)) * passing
    grad_scaled = jnp.einsum("chpn,cjn->cjhp", grad_leave, keys_float, precision=highest)
    grad_values = grad_values + jnp.swapaxes(weight_end, 1, 2)[:, :, :, None] * grad_scaled
    grad_keys = grad_keys + jnp.einsum("chpn,cjhp->cjn", grad_leave, scaled, precision=highest)
    grad_weight_end = jnp.swapaxes(jnp.sum(grad_scaled * value_float, axis=3), 1, 2)
    end_terms = grad_weight_end * weight_end
    grad_dt = grad_dt + grad_weight_end * ending[:, None, :] * end_decay
    last_hot = (places == STRETCH - 1).astype(jnp.float32)
    grad_logs = (
        grad_logs
        - end_terms
        + (jnp.sum(end_terms, axis=2) + last_grad)[:, :, None] * last_hot[None, None, :]
    )
    grad_steps = jnp.flip(jnp.cumsum(jnp.flip(grad_logs, axis=2), axis=2), axis=2)
    grad_dt = grad_dt + grad_steps * decay_rate[None, :, None]
    log_rate_grad = jnp.sum(grad_steps * stretch_dt, axis=(0, 2)) * decay_rate
    grad_dt_rows = jnp.swapaxes(grad_dt, 1, 2).reshape(row_count, local_heads)
    grad_step_raw = (
        grad_dt_rows * valid_rows[:, None] * jax.nn.sigmoid(step_raw + step_bias[None, :])
    )
    step_bias_grad = jnp.sum(grad_step_raw, axis=0)
    grad_state_parts = (
        lax.psum(grad_keys.reshape(row_count, state_size).astype(jnp.bfloat16), "tp").astype(
            jnp.float32
        ),
        lax.psum(grad_queries.reshape(row_count, state_size).astype(jnp.bfloat16), "tp").astype(
            jnp.float32
        ),
    )
    grad_conv = jnp.concatenate(
        [grad_values.reshape(row_count, local_inner), grad_state_parts[0], grad_state_parts[1]],
        axis=1,
    )
    conv_sig = jax.nn.sigmoid(conv_pre)
    grad_pre = grad_conv * conv_sig * (1.0 + conv_pre * (1.0 - conv_sig))
    tap_grads = [None] * (CONV + 1)
    tap_grads[CONV] = jnp.sum(grad_pre, axis=0)
    grad_extended = jnp.zeros(extended.shape, jnp.float32)
    for offset in range(CONV):
        window = extended[carry_rows - offset : carry_rows - offset + row_count]
        masked = grad_pre * lag_masks[offset]
        tap_grads[CONV - 1 - offset] = jnp.sum(masked * window, axis=0)
        grad_extended = grad_extended + jnp.pad(
            masked * conv_taps[CONV - 1 - offset][None, :], ((carry_rows - offset, offset), (0, 0))
        )
    taps_grad = jnp.stack(tap_grads)
    returned = shifted(grad_extended[:carry_rows], "ctx", -1)
    grad_mixed = (
        grad_extended[carry_rows:] + jnp.pad(returned, ((row_count - carry_rows, 0), (0, 0)))
    ).astype(jnp.bfloat16)
    grad_inner_in = grad_mixed[:, :local_inner]
    grad_state_in = grad_mixed[:, local_inner:]
    partial_normed = jnp.einsum(
        "rk,dk->rd", grad_gate, full_inner[0], preferred_element_type=jnp.float32
    )
    partial_normed = partial_normed + jnp.einsum(
        "rk,dk->rd", grad_inner_in, full_inner[1], preferred_element_type=jnp.float32
    )
    partial_normed = partial_normed + jnp.dot(
        grad_step_raw, full_step.astype(jnp.float32).T, precision=highest
    )
    grad_normed = lax.psum(partial_normed.astype(jnp.bfloat16), "tp").astype(
        jnp.float32
    ) + jnp.einsum("rk,dk->rd", grad_state_in, full_state, preferred_element_type=jnp.float32)
    norm_gain_grad = jnp.sum(grad_normed * unit_rows, axis=0)
    grad_unit_rows = grad_normed * full_gain.astype(jnp.float32)[None, :]
    tokens_grad = scaling * (
        grad_unit_rows - unit_rows * jnp.mean(grad_unit_rows * unit_rows, axis=-1, keepdims=True)
    ) + out_grad.astype(jnp.float32)
    inner_weight_grad = jnp.stack(
        [
            jnp.einsum("rd,rk->dk", normed, grad_gate, preferred_element_type=jnp.float32),
            jnp.einsum("rd,rk->dk", normed, grad_inner_in, preferred_element_type=jnp.float32),
        ]
    )
    state_weight_grad = jnp.einsum(
        "rd,rk->dk", normed, grad_state_in, preferred_element_type=jnp.float32
    )
    step_weight_grad = jnp.dot(normed.astype(jnp.float32).T, grad_step_raw, precision=highest)
    summed = (
        lax.psum_scatter(
            inner_weight_grad.astype(jnp.bfloat16), ("fsdp", "ctx"), scatter_dimension=1, tiled=True
        ).astype(jnp.float32),
        lax.psum_scatter(
            state_weight_grad.astype(jnp.bfloat16), ("fsdp", "ctx"), scatter_dimension=0, tiled=True
        ).astype(jnp.float32),
        lax.psum_scatter(
            step_weight_grad.astype(jnp.bfloat16), ("fsdp", "ctx"), scatter_dimension=0, tiled=True
        ).astype(jnp.float32),
        lax.psum_scatter(
            norm_gain_grad.astype(jnp.bfloat16), ("fsdp", "ctx"), scatter_dimension=0, tiled=True
        ).astype(jnp.float32),
        lax.psum_scatter(
            out_weight_grad.astype(jnp.bfloat16), ("fsdp", "ctx"), scatter_dimension=1, tiled=True
        ).astype(jnp.float32),
    )
    small_sums = lax.psum(
        (
            taps_grad[:, :local_inner],
            taps_grad[:, local_inner:],
            step_bias_grad,
            log_rate_grad,
            skip_gain_grad,
            gated_gain_grad,
        ),
        ("fsdp", "ctx"),
    )
    return (
        mixed_out,
        tokens_grad,
        summed[3],
        summed[0],
        summed[1],
        summed[2],
        small_sums[0],
        small_sums[1],
        small_sums[2],
        small_sums[3],
        small_sums[4],
        small_sums[5],
        summed[4],
    )


def solution(mesh):
    return jax.shard_map(
        per_device,
        mesh=mesh,
        in_specs=(
            P(("fsdp", "ctx"), None),
            P(("fsdp", "ctx")),
            P(None, ("fsdp", "ctx"), "tp"),
            P(("fsdp", "ctx"), None),
            P(("fsdp", "ctx"), "tp"),
            P(None, "tp"),
            P(),
            P("tp"),
            P("tp"),
            P("tp"),
            P("tp"),
            P("tp", ("fsdp", "ctx")),
            P(("fsdp", "ctx"), None),
            P(("fsdp", "ctx")),
        ),
        out_specs=(
            P(("fsdp", "ctx"), None),
            P(("fsdp", "ctx"), None),
            P(("fsdp", "ctx")),
            P(None, ("fsdp", "ctx"), "tp"),
            P(("fsdp", "ctx"), None),
            P(("fsdp", "ctx"), "tp"),
            P(None, "tp"),
            P(),
            P("tp"),
            P("tp"),
            P("tp"),
            P("tp"),
            P("tp", ("fsdp", "ctx")),
        ),
        check_vma=False,
    )
```

profile of v0, /device:TPU:0, one launch (start us, length us, event | category | flops | bytes accessed | tf_op | source)
XLA Modules:
  0.0 793.1 jit_solution(8936453519855385804)
XLA Ops:
  14.4 10.2 %all-gather = bf16[8,1,128]{2,1,0:T(2,128)(2,1)S(1)} all-gather(bf16[1,1,128]{2,1,0:T(2,128)(2,1)S(1)} %bitcast.400), channel_id=1, replica_groups=mesh['fsdp'=4,'ctx'=2,'tp'=4] {'fsdp','ctx'}, dimensions={0}, use_global_device_ids=true | all-gather | bytes 2304 | tf_op jit(solution)/shard_map/all_gather | solution.py:68
  24.7 8.9 %all_gather.39 = bf16[1024,8]{0,1:T(8,128)(2,1)S(1)} all-gather(bf16[128,8]{0,1:T(8,128)(2,1)S(1)} %copy-done.113), channel_id=1, replica_groups=mesh['fsdp'=4,'ctx'=2,'tp'=4] {'fsdp','ctx'}, dimensions={0}, use_global_device_ids=true | all-gather | bytes 18432 | tf_op jit(solution)/shard_map/all_gather | solution.py:67
  46.4 9.5 %all_gather.38 = bf16[1024,256]{1,0:T(8,128)(2,1)S(1)} all-gather(bf16[128,256]{1,0:T(8,128)(2,1)S(1)} %copy-done.59), channel_id=1, replica_groups=mesh['fsdp'=4,'ctx'=2,'tp'=4] {'fsdp','ctx'}, dimensions={0}, use_global_device_ids=true | all-gather | bytes 589824 | tf_op jit(solution)/shard_map/all_gather | solution.py:66
  61.7 4.9 convolution_convert_fusion.1
  77.9 7.6 multiply_convert_fusion
  122.3 6.4 fusion.26
  134.2 6.6 multiply_reduce_fusion.9
  140.8 12.1 %psum.84 = f32[2048]{0:T(1024)S(1)} all-reduce(f32[2048]{0:T(1024)S(1)} %get-tuple-element.205), channel_id=1, replica_groups=mesh['fsdp'=4,'ctx'=2,'tp'=4] {'tp'}, use_global_device_ids=true, to_apply=%region_6.7 | all-reduce | flops 2048 | bytes 16384 | tf_op jit(solution)/shard_map/psum | solution.py:170
  153.0 9.3 %multiply_reduce_fusion.6 = (f32[512]{0:T(512)}, f32[2048]{0:T(1024)S(1)}, f32[2048,512]{0,1:T(8,128)}) fusion(f32[2048,512]{0,1:T(8,128)} %get-tuple-element.206, f32[2048]{0:T(1024)S(1)} %get-tuple-element.234, f32[2048]{0:T(1024)S(1)} %add_rsqrt_fusion, f32[512]{0:T(512)S(1)} %copy-done.107, bf16[2048,1024]{1,0:T(8,128)(2,1)} %param.30, ...), kind=kOutput, calls=%fused_computation.62 | convolution fusion | flops 2155869696 | bytes 13660160 | tf_op jit(solution)/shard_map/rd,kd->rk/dot_general | solution.py:185
  162.3 8.7 %psum.86 = f32[2048]{0:T(1024)S(1)} all-reduce(f32[2048]{0:T(1024)S(1)} %get-tuple-element.154), channel_id=1, replica_groups=mesh['fsdp'=4,'ctx'=2,'tp'=4] {'tp'}, use_global_device_ids=true, to_apply=%region_9.10 | all-reduce | flops 2048 | bytes 16384 | tf_op jit(solution)/shard_map/psum | solution.py:193
  171.0 9.4 %multiply_reduce_fusion.7 = (f32[512]{0:T(512)}, bf16[2048,512]{0,1:T(8,128)(2,1)S(1)}, bf16[2048,512]{0,1:T(8,128)(2,1)}) fusion(bf16[2048,768]{0,1:T(8,128)(2,1)S(1)} %get-tuple-element.221, f32[2048,512]{0,1:T(8,128)} %get-tuple-element.258, f32[2048]{0:T(1024)S(1)} %psum.86, f32[2048,512]{0,1:T(8,128)} %get-tuple-element.206, ...), kind=kLoop, calls=%fused_computation.63 | loop fusion | flops 26213888 | bytes 23097344 | tf_op jit(solution)/shard_map/reduce_sum | solution.py:204
  182.1 8.0 %fusion.46 = f32[8,256,128]{2,1,0:T(8,128)} fusion(f32[8,8,64,128]{3,2,1,0:T(8,128)S(1)} %copy-done.16, f32[8,256,8]{1,2,0:T(8,128)S(1)} %copy-done.38, bf16[8,256,8,64]{1,0,3,2:T(8,128)(2,1)S(1)} %bitcast.362), kind=kOutput, calls=%fused_computation.92 | convolution fusion | flops 1612709888 | bytes 5308416 | tf_op jit(solution)/shard_map/cihp,chpn->cin/dot_general | solution.py:224
  190.0 14.6 %fusion.6 = (f32[8,8,256]{2,1,0:T(8,128)}, f32[8,8,256]{2,1,0:T(8,128)}, f32[8,8,256]{2,1,0:T(8,128)}, bf16[8,256,256]{2,1,0:T(8,128)(2,1)}) fusion(f32[8,8,256]{2,1,0:T(8,128)S(1)} %bitcast.386, f32[8,8,256]{2,1,0:T(8,128)S(1)} %copy-done.36, f32[8,256,256]{2,1,0:T(8,128)S(1)} %copy-done.32, pred[8,256,256]{2,1,0:T(8,128)(4,1)S(1)} %copy-done.45, ...), kind=kOutput, calls=%fused_computation.17 | convolution fusion | flops 595017728 | bytes 8192000 | tf_op jit(solution)/shard_map/cihp,cjhp->chij/dot_general | solution.py:208
  211.7 7.9 fusion.47
  231.2 10.4 %fusion.29 = f32[8,256,8,64]{1,3,2,0:T(8,128)} fusion(f32[8,256,8,64]{1,3,2,0:T(8,128)} %get-tuple-element.261, f32[8,8,256]{2,1,0:T(8,128)S(1)} %bitcast.387, f32[8,8,256]{2,1,0:T(8,128)S(1)} %copy-done.37, f32[8,256,256]{2,1,0:T(8,128)} %copy-done.31, pred[8,256,256]{2,1,0:T(8,128)(4,1)} %compare_and_fusion, f32[8]{0:T(128)} %param.27, ...), kind=kOutput, calls=%fused_computation.59 | convolution fusion | flops 567279616 | bytes 13303840 | tf_op jit(solution)/shard_map/chij,cihp->cjhp/dot_general | solution.py:205
  252.8 6.0 convolution_convert_fusion.3
  258.9 5.7 fusion.48
  272.8 25.5 %all-reduce.14.cloned.1.call-done = (bf16[2048,128]{0,1:T(8,128)(2,1)}, bf16[2048,128]{0,1:T(8,128)(2,1)}) async-done(((bf16[2048,128]{0,1:T(8,128)(2,1)}, bf16[2048,128]{0,1:T(8,128)(2,1)}), (bf16[2048,128]{0,1:T(8,128)(2,1)}, bf16[2048,128]{0,1:T(8,128)(2,1)})) %all-reduce.14.cloned.1.call-update) | async-done | bytes 1048592 | tf_op jit(solution)/shard_map/psum | solution.py:271
  300.6 19.6 %multiply_reduce_fusion.2 = (f32[768]{0:T(1024)S(1)}, f32[768]{0:T(1024)S(1)}, f32[768]{0:T(1024)S(1)}, f32[768]{0:T(1024)S(1)}, f32[768]{0:T(1024)S(1)}, /*index=5*/f32[2048,768]{0,1:T(8,128)}) fusion(f32[2051,768]{0,1:T(8,128)} %copy-done, f32[2048]{0:T(1024)S(1)} %copy-done.52, f32[2048]{0:T(1024)S(1)} %copy-done.50, f32[2048]{0:T(1024)S(1)} %get-tuple-element.235, ...), kind=kLoop, calls=%fused_computation.34 | loop fusion | flops 34599168 | bytes 44080128 | tf_op jit(solution)/shard_map/reduce_sum | solution.py:287
  320.2 5.9 broadcast_multiply_fusion
  328.6 9.4 %pad_add_fusion = f32[2051,768]{0,1:T(8,128)} fusion(f32[2048,768]{0,1:T(8,128)S(1)} %get-tuple-element.225, f32[2048,768]{0,1:T(8,128)S(1)} %get-tuple-element.226, f32[2048,768]{0,1:T(8,128)} %get-tuple-element.227, f32[2048,768]{0,1:T(8,128)S(1)} %get-tuple-element.224), kind=kLoop, calls=%fused_computation.29 | loop fusion | flops 4725504 | bytes 31466496 | tf_op jit(solution)/shard_map/add | solution.py:288
  344.6 4.8 fusion.49
  354.7 5.8 fusion.63
  360.6 4.6 convolution_convert_fusion
  365.2 8.4 %add_convert_fusion = bf16[2048,1024]{1,0:T(8,128)(2,1)} fusion(f32[2048,1024]{1,0:T(8,128)S(1)} %fusion.119, f32[2048,1024]{1,0:T(8,128)} %fusion.63, bf16[2048,768]{0,1:T(8,128)(2,1)S(1)} %fusion.16, bf16[2,1024,512]{2,1,0:T(8,128)(2,1)S(1)} %copy-done.42), kind=kOutput, calls=%fused_computation.28 | convolution fusion | flops 2153775104 | bytes 24117248 | tf_op jit(solution)/shard_map/rk,dk->rd/dot_general | solution.py:301
  377.2 26.4 %all-reduce.6 = (f32[5,512]{1,0:T(8,128)}, f32[5,256]{1,0:T(8,128)}, f32[8]{0:T(128)}, f32[8]{0:T(128)}, f32[8]{0:T(128)}, /*index=5*/f32[512]{0:T(512)}) all-reduce(f32[5,512]{1,0:T(8,128)S(1)} %slice.281, f32[5,256]{1,0:T(8,128)S(1)} %slice.282, ...), channel_id=1, replica_groups=mesh['fsdp'=4,'ctx'=2,'tp'=4] {'fsdp','ctx'}, use_global_device_ids=true, to_apply=%region_36.37 | all-reduce | flops 4376 | bytes 35008 | tf_op jit(solution)/shard_map/psum | solution.py:342
  405.4 6.4 reduce-scatter.11.cloned.1.call-done
  413.3 43.4 %reduce-scatter.9.cloned.1.call-done = bf16[2,128,512]{2,1,0:T(8,128)(2,1)} async-done(((bf16[2,1024,512]{2,1,0:T(8,128)(2,1)}), bf16[2,128,512]{2,1,0:T(8,128)(2,1)}) %reduce-scatter.9.cloned.1.call-update) | async-done | bytes 262160 | tf_op jit(solution)/shard_map/reduce_scatter | solution.py:326
  458.4 292.9 %all-reduce.12.cloned.1.call-done = (bf16[2048,1024]{1,0:T(8,128)(2,1)}, bf16[2048,1024]{1,0:T(8,128)(2,1)}) async-done(((bf16[2048,1024]{1,0:T(8,128)(2,1)}, bf16[2048,1024]{1,0:T(8,128)(2,1)}), (bf16[2048,1024]{1,0:T(8,128)(2,1)}, bf16[2048,1024]{1,0:T(8,128)(2,1)})) %all-reduce.12.cloned.1.call-update) | async-done | bytes 8388624 | tf_op jit(solution)/shard_map/psum | solution.py:175
  751.4 8.1 %fusion.13 = (bf16[1024]{0:T(1024)(128)(2,1)S(1)}, f32[2048]{0:T(1024)S(1)}, f32[2048,1024]{1,0:T(8,128)}) fusion(bf16[2048,1024]{1,0:T(8,128)(2,1)} %param.18, f32[2048]{0:T(1024)S(1)} %copy-done.58, f32[1024]{0:T(1024)S(1)} %bitcast.398, bf16[1024,256]{1,0:T(8,128)(2,1)} %copy-done.43, bf16[2048,768]{0,1:T(8,128)(2,1)S(1)} %fusion.16, ...), kind=kOutput, calls=%fused_computation.24 | convolution fusion | flops 1092613120 | bytes 18372608 | tf_op jit(solution)/shard_map/rk,dk->rd/dot_general | solution.py:309
  759.5 13.7 %all-reduce.5 = bf16[1024]{0:T(1024)(128)(2,1)S(1)} all-reduce(bf16[1024]{0:T(1024)(128)(2,1)S(1)} %get-tuple-element.151), channel_id=2, replica_groups=mesh['fsdp'=4,'ctx'=2,'tp'=4] {'fsdp','ctx'}, use_global_device_ids=true, to_apply=%region_27.28.clone | all-reduce | flops 1024 | bytes 4096
  773.7 12.4 %fusion.12 = (f32[2048,1024]{1,0:T(8,128)}, bf16[2048,1024]{1,0:T(8,128)(2,1)}) fusion(bf16[2048,1024]{1,0:T(8,128)(2,1)} %param.18, bf16[2048,1024]{1,0:T(8,128)(2,1)} %param.30, f32[2048,1024]{1,0:T(8,128)} %get-tuple-element.262, f32[2048]{0:T(1024)S(1)} %broadcast_multiply_fusion.1, f32[1024]{0:T(1024)S(1)} %bitcast.399, f32[2048]{0:T(1024)S(1)} %copy-done.58, ...), kind=kLoop, calls=%fused_computation.23 | loop fusion | flops 23068672 | bytes 33574912 | tf_op jit(solution)/shard_map/add | solution.py:312
  (420 shorter events, 143.1 us)
Async XLA Ops:
  7.2 17.5 %copy-start.113 = (bf16[128,8]{0,1:T(8,128)(2,1)S(1)}, bf16[128,8]{0,1:T(8,128)(2,1)}, u32[]{:S(2)}) copy-start(bf16[128,8]{0,1:T(8,128)(2,1)} %param.22) | copy-start | bytes 6148
  7.2 26.3 %copy-start.125 = (f32[8]{0:T(128)S(1)}, f32[8]{0:T(128)}, u32[]{:S(2)}) copy-start(f32[8]{0:T(128)} %param.26) | copy-start | bytes 100
  7.2 54.5 %all-gather.6.cloned.1.call-start = ((), (), s32[]{:S(2)}) async-start(), calls=%async_computation.4 | async-start | bytes 2359296 | tf_op jit(solution)/shard_map/all_gather | solution.py:65
  7.9 145.1 %all-gather.8.cloned.1.call-start = ((), (), s32[]{:S(2)}) async-start(), calls=%async_computation.5 | async-start | bytes 1179648 | tf_op jit(solution)/shard_map/all_gather | solution.py:69
  8.7 289.6 %all-reduce.14.cloned.1.call-start = ((), (), s32[]{:S(2)}) async-start(), calls=%async_computation.11 | async-start | bytes 2097152 | tf_op jit(solution)/shard_map/psum | solution.py:271
  10.7 22.8 %copy-start.4 = (bf16[2048,1024]{1,0:T(8,128)(2,1)S(1)}, bf16[2048,1024]{1,0:T(8,128)(2,1)}, u32[]{:S(2)}) copy-start(bf16[2048,1024]{1,0:T(8,128)(2,1)} %param.18) | copy-start | bytes 12582916
  10.9 33.5 %copy-start.100 = (f32[8]{0:T(128)}, f32[8]{0:T(128)S(1)}, u32[]{:S(2)}) copy-start(f32[8]{0:T(128)S(1)} %convert_reduce_fusion) | copy-start | bytes 100
  14.4 20.3 %copy-start.57 = (f32[2048]{0:T(1024)}, f32[2048]{0:T(1024)S(1)}, u32[]{:S(2)}) copy-start(f32[2048]{0:T(1024)S(1)} %add_rsqrt_fusion.1) | copy-start | bytes 24580
  44.2 16.1 %copy-start.35 = (f32[8,8,256]{2,1,0:T(8,128)}, f32[8,8,256]{2,1,0:T(8,128)S(1)}, u32[]{:S(2)}) copy-start(f32[8,8,256]{2,1,0:T(8,128)S(1)} %get-tuple-element.208) | copy-start | bytes 196612
  44.4 15.9 %copy-start.53 = (f32[8,8,1]{1,0,2:T(8,128)}, f32[8,8,1]{1,0,2:T(8,128)S(1)}, u32[]{:S(2)}) copy-start(f32[8,8,1]{1,0,2:T(8,128)S(1)} %copy.239) | copy-start | bytes 772
  66.7 8.4 %collective-permute-start = (bf16[3,768]{0,1:T(8,128)(2,1)S(1)}, bf16[3,768]{0,1:T(8,128)(2,1)}, u32[]{:S(2)}, u32[]{:S(2)}) collective-permute-start(bf16[3,768]{0,1:T(8,128)(2,1)S(1)} %pad_maximum_fusion.1), channel_id=1, source_target_pairs={{0,4},{1,5},{2,6},{3,7},{8,12},{9,13},{10,14},{11,15},{16,20},{17,... | collective-permute-start | bytes 13832 | tf_op jit(solution)/shard_map/ppermute | solution.py:18
  134.2 18.8 %copy-start.107 = (f32[512]{0:T(512)S(1)}, f32[512]{0:T(512)}, u32[]{:S(2)}) copy-start(f32[512]{0:T(512)} %param.28) | copy-start | bytes 6148
  153.0 18.0 %copy-start.73 = (f32[2048]{0:T(1024)}, f32[2048]{0:T(1024)S(1)}, u32[]{:S(2)}) copy-start(f32[2048]{0:T(1024)S(1)} %add_rsqrt_fusion) | copy-start | bytes 24580
  181.2 23.5 %copy-start.11 = (bf16[64,8,8,256]{3,2,1,0:T(8,128)(2,1)}, bf16[64,8,8,256]{3,2,1,0:T(8,128)(2,1)S(1)}, u32[]{:S(2)}) copy-start(bf16[64,8,8,256]{3,2,1,0:T(8,128)(2,1)S(1)} %copy.244) | copy-start | bytes 6291460
  231.1 16.1 %copy-start.56 = (f32[8,256]{1,0:T(8,128)S(1)}, f32[8,256]{1,0:T(8,128)}, u32[]{:S(2)}) copy-start(f32[8,256]{1,0:T(8,128)} %copy-done.55) | copy-start | bytes 24580
  231.1 16.1 %copy-start.60 = (f32[8,8,256]{2,1,0:T(8,128)S(1)}, f32[8,8,256]{2,1,0:T(8,128)}, u32[]{:S(2)}) copy-start(f32[8,8,256]{2,1,0:T(8,128)} %get-tuple-element.145) | copy-start | bytes 196612
  231.2 16.1 %copy-start.111 = (f32[8]{0:T(128)S(1)}, f32[8]{0:T(128)}, u32[]{:S(2)}) copy-start(f32[8]{0:T(128)} %copy-done.110) | copy-start | bytes 100
  231.2 16.7 %copy-start.46 = (f32[2048,8]{0,1:T(8,128)S(1)}, f32[2048,8]{0,1:T(8,128)}, u32[]{:S(2)}) copy-start(f32[2048,8]{0,1:T(8,128)} %get-tuple-element.257) | copy-start | bytes 196612
  247.2 128.5 %reduce-scatter.13.cloned.1.call-start = ((), (), s32[]{:S(2)}) async-start(), calls=%async_computation.8 | async-start | bytes 294912
  258.9 144.8 %reduce-scatter.15.cloned.1.call-start = ((), (), s32[]{:S(2)}) async-start(), calls=%async_computation.9 | async-start | bytes 1179648
  271.0 29.6 %copy-start.50 = (f32[2048]{0:T(1024)S(1)}, f32[2048]{0:T(1024)}, u32[]{:S(2)}) copy-start(f32[2048]{0:T(1024)} %get-tuple-element.236) | copy-start | bytes 24580
  271.0 29.6 %copy-start.52 = (f32[2048]{0:T(1024)S(1)}, f32[2048]{0:T(1024)}, u32[]{:S(2)}) copy-start(f32[2048]{0:T(1024)} %get-tuple-element.237) | copy-start | bytes 24580
  272.3 139.4 %reduce-scatter.11.cloned.1.call-start = ((), (), s32[]{:S(2)}) async-start(), calls=%async_computation.7 | async-start | bytes 589824 | tf_op jit(solution)/shard_map/reduce_scatter | solution.py:329
  300.6 19.6 %copy-start.64 = (f32[768]{0:T(1024)S(1)}, f32[768]{0:T(1024)}, u32[]{:S(2)}) copy-start(f32[768]{0:T(1024)} %get-tuple-element.157) | copy-start | bytes 9220
  300.6 19.6 %copy-start.66 = (f32[768]{0:T(1024)S(1)}, f32[768]{0:T(1024)}, u32[]{:S(2)}) copy-start(f32[768]{0:T(1024)} %get-tuple-element.158) | copy-start | bytes 9220
  300.6 19.6 %copy-start.68 = (f32[768]{0:T(1024)S(1)}, f32[768]{0:T(1024)}, u32[]{:S(2)}) copy-start(f32[768]{0:T(1024)} %get-tuple-element.159) | copy-start | bytes 9220
  300.6 19.6 %copy-start.70 = (f32[768]{0:T(1024)S(1)}, f32[768]{0:T(1024)}, u32[]{:S(2)}) copy-start(f32[768]{0:T(1024)} %get-tuple-element.160) | copy-start | bytes 9220
  327.3 10.7 %collective-permute-start.1 = (f32[3,768]{0,1:T(8,128)S(1)}, f32[3,768]{0,1:T(8,128)S(1)}, u32[]{:S(2)}, u32[]{:S(2)}) collective-permute-start(f32[3,768]{0,1:T(8,128)S(1)} %pad_add_fusion.1), channel_id=1, source_target_pairs={{4,0},{5,1},{6,2},{7,3},{12,8},{13,9},{14,10},{15,11},{20,16},{21,... | collective-permute-start | bytes 27656 | tf_op jit(solution)/shard_map/ppermute | solution.py:18
  344.5 112.1 %reduce-scatter.9.cloned.1.call-start = ((), (), s32[]{:S(2)}) async-start(), calls=%async_computation.6 | async-start | bytes 2359296 | tf_op jit(solution)/shard_map/reduce_scatter | solution.py:326
  350.9 400.5 %all-reduce.12.cloned.1.call-start = ((), (), s32[]{:S(2)}) async-start(), calls=%async_computation.10 | async-start | bytes 16777216 | tf_op jit(solution)/shard_map/psum | solution.py:175
  373.5 377.8 %copy-start.58 = (f32[2048]{0:T(1024)S(1)}, f32[2048]{0:T(1024)}, u32[]{:S(2)}) copy-start(f32[2048]{0:T(1024)} %copy-done.57) | copy-start | bytes 24580
  373.5 377.8 %copy-start.72 = (f32[8,1,128]{2,1,0:T(1,128)S(1)}, f32[8,1,128]{2,1,0:T(1,128)}, u32[]{:S(2)}) copy-start(f32[8,1,128]{2,1,0:T(1,128)} %copy-done.71) | copy-start | bytes 12292
  (107 other events, 525.3 us)
Sparse Core Ops, SparseCore 0:
  9.9 30.5 all-gather.5
  42.5 24.5 all-gather.7
  247.3 50.8 all-reduce.13
  302.0 32.9 reduce-scatter.12
  338.0 36.0 reduce-scatter.14
  377.6 34.1 reduce-scatter.10
  415.4 41.1 reduce-scatter.8
  459.8 291.5 all-reduce.11
where the time goes:
time: 801 us; the launch traced here: 793 us
  waiting for transfers between devices  370 us (46%)
  matrix products  142 us (18%)
  other arithmetic  116 us (14%)
  blocking collectives  97.3 us (12%)
  local copies, waits for them, and re-layouts  45.4 us (6%)
  between operations  16.8 us (2%)
    psum x1, waiting for transfers between devices, per_device(): lax.psum(branch_part.astype(jnp.bfloat16), 'tp').astype(jnp.float32)  293 us
    reduce_scatter x1, waiting for transfers between devices, per_device(): lax.psum_scatter(inner_weight_grad.astype(jnp.bfloat16), ('fsdp', 'ctx'),...  43.4 us
    psum x1, blocking collectives, per_device(): lax.psum((taps_grad[:, :local_inner], taps_grad[:, local_inner:], step_bi...  26.4 us
    psum x1, waiting for transfers between devices, per_device(): lax.psum(grad_queries.reshape(row_count, state_size).astype(jnp.bfloat16)...  25.5 us
    unnamed x274, local copies, waits for them, and re-layouts  24.1 us
    reduce_sum x1, other arithmetic, per_device(): tap_grads[CONV - 1 - offset] = jnp.sum(masked * window, axis=0)  19.6 us
    another operation x6, other arithmetic  16.8 us
  transfers between devices with their start and end apart: 10, of which 4 were waited for; matrix products, arithmetic and copies ran while one was open for 25% of the time, Pallas kernels for 0%

commit v1 on v0

v1 whole, which is shorter than its diff:
```python
import functools

import jax
import jax.numpy as jnp
from jax import lax
from jax.experimental import pallas as pl
from jax.experimental.pallas import tpu as pltpu
from jax.sharding import PartitionSpec as P

CONV = 4
STRETCH = 256
INNER = 2048
LANES = 128
HALO = 16
NEVER = -1e30
VMEM_BYTES = 60 * 1024 * 1024

epsilon = 1e-05
bf16 = jnp.bfloat16
f32 = jnp.float32


def swap_ctx(x):
    return lax.ppermute(x, "ctx", [(0, 1), (1, 0)])


def swap_fsdp(x, k):
    return lax.ppermute(x, "fsdp", [(i, i ^ k) for i in range(4)])


def swap_tp(x, k):
    return lax.ppermute(x, "tp", [(i, i ^ k) for i in range(4)])


def row_shares():
    return 2 if small_mesh() and lax.axis_size("tp") == 4 else 1


def shift_part(x, by):
    tp, shares = lax.axis_size("tp"), row_shares()
    parts, group = lax.axis_size("ctx") * shares, tp // shares

    def device(part, k):
        return part // shares * tp + part % shares * group + k

    pairs = [
        (device(part, k), device(part + by, k))
        for part in range(parts)
        if 0 <= part + by < parts
        for k in range(group)
    ]
    return lax.ppermute(x, ("ctx", "tp"), pairs)


def small_mesh():
    return lax.axis_size("fsdp") == 4 and lax.axis_size("ctx") == 2


def gather_near(x):
    if not small_mesh():
        return [lax.all_gather(x, ("fsdp", "ctx"), axis=0, tiled=True)]
    return [x] + [swap_fsdp(x, k) for k in (1, 2, 3)]


def gather_stacks(near):
    stack = jnp.stack(near)
    return [stack, swap_ctx(stack)] if small_mesh() else [stack]


def gather_place(size):
    if not small_mesh():
        return jnp.zeros((1,), jnp.int32)
    me = lax.axis_index("fsdp")
    core = lax.axis_index("ctx")
    place = [(me ^ k) * 2 + core for k in range(4)] + [(me ^ k) * 2 + 1 - core for k in range(4)]
    return (jnp.stack(place) * size).astype(jnp.int32)


def scatter_rows(x):
    if not small_mesh():
        x = x.reshape(-1, x.shape[-1])
        return lax.psum_scatter(x, ("fsdp", "ctx"), scatter_dimension=0, tiled=True).astype(f32)
    me = lax.axis_index("fsdp")
    core = lax.axis_index("ctx")
    theirs = swap_ctx(lax.dynamic_index_in_dim(x, 1 - core, 0, False))
    mine = lax.dynamic_index_in_dim(x, core, 0, False)
    summed = (mine.astype(f32) + theirs.astype(f32)).astype(bf16)
    total = lax.dynamic_index_in_dim(summed, me, 0, False).astype(f32)
    for k in (1, 2, 3):
        total = total + swap_fsdp(lax.dynamic_index_in_dim(summed, me ^ k, 0, False), k).astype(f32)
    return total


def sum_rows_group(x):
    if not small_mesh():
        return lax.psum(x, ("fsdp", "ctx"))
    x = x + swap_ctx(x)
    x = x + swap_fsdp(x, 1)
    return x + swap_fsdp(x, 2)


def sum_tp_small(x):
    if lax.axis_size("tp") != 4:
        return lax.psum(x, "tp").astype(f32)
    pair = (x.astype(f32) + swap_tp(x, 1).astype(f32)).astype(x.dtype)
    return pair.astype(f32) + swap_tp(pair, 2).astype(f32)


def tied(x, *others):
    return lax.optimization_barrier((x,) + others)[0]


def nn(a, b):
    return jnp.dot(a, b, preferred_element_type=f32)


def nt(a, b):
    return lax.dot_general(a, b, (((1,), (1,)), ((), ())), preferred_element_type=f32)


def tn(a, b):
    return lax.dot_general(a, b, (((0,), (0,)), ((), ())), preferred_element_type=f32)


def two_terms(x):
    high = x.astype(bf16)
    return high, (x - high.astype(f32)).astype(bf16)


def dot_pair(x, choice):
    high, low = two_terms(x)
    return nn(high, choice) + nn(low, choice)


def dot_triple(choice, x):
    high = x.astype(bf16)
    rest = x - high.astype(f32)
    middle, low = two_terms(rest)
    return nn(choice, high) + nn(choice, middle) + nn(choice, low)


def iota(shape, axis):
    return lax.broadcasted_iota(jnp.int32, shape, axis)


def head_choice(channels, head_size):
    return (iota((LANES, channels), 1) // head_size == iota((LANES, channels), 0)).astype(bf16)


def head_choice_t(channels, head_size):
    return (iota((channels, LANES), 0) // head_size == iota((channels, LANES), 1)).astype(bf16)


def head_column(row, choice_t):
    return jnp.sum(choice_t.astype(f32) * row, axis=1, keepdims=True)


def column(rows):
    if rows.shape[0] == 1:
        return jnp.broadcast_to(rows, (LANES, STRETCH)).T
    return jnp.concatenate([rows, jnp.zeros((LANES - rows.shape[0], STRETCH), f32)], axis=0).T


def row_norm(rows):
    scaling = lax.rsqrt(jnp.mean(rows * rows, axis=-1, keepdims=True) + epsilon)
    return scaling, rows * scaling


def softplus(v):
    return jnp.maximum(v, 0.0) + jnp.log1p(jnp.exp(-jnp.abs(v)))


def pair_sel(x, part, head_size):
    return jnp.where(iota(x.shape, 1) // head_size == part, x, jnp.zeros_like(x))


def mask_matrix(pos):
    wide = jnp.concatenate([pos] * (STRETCH // LANES), axis=1)
    ahead = (iota((STRETCH, STRETCH), 0) - iota((STRETCH, STRETCH), 1)).astype(f32)
    return jnp.where((ahead >= 0.0) & (ahead <= wide), 0.0, NEVER)


def carry_factor(pos, decay):
    places = iota((STRETCH, LANES), 0).astype(f32)
    return jnp.where(pos >= places + 1.0, jnp.exp(decay), 0.0)


def passing_row(pos, decay):
    last = slice(STRETCH - 1, STRETCH)
    return jnp.where(pos[last] >= float(STRETCH), jnp.exp(decay[last]), 0.0)


def pack_state(ref, state, through, own_heads):
    channels = state.shape[0]
    ref[:channels, :] = state.astype(bf16)
    row, col = iota((LANES, LANES), 0), iota((LANES, LANES), 1)
    turn = (row < 2 * own_heads) & (
        jnp.where(row < own_heads, row + own_heads, row - own_heads) == col
    )
    low = jnp.broadcast_to(through, (8, LANES))
    turned = dot_pair(low, turn.astype(bf16))
    ref[channels:, :] = jnp.concatenate([low, turned], axis=0).astype(bf16)


def join_states(refs, choice_t, groups):
    channels = choice_t.shape[0]
    half = channels // 2
    total = None
    for distance in range(len(refs), 0, -1):
        ref = refs[distance - 1]
        state = ref[:channels, :].astype(f32)
        through = ref[channels:, :].astype(f32)
        if groups == 2 and distance % 2 == 1:
            state = jnp.concatenate([state[half:], state[:half]], axis=0)
            through = through[8:9]
        else:
            through = through[0:1]
        total = state if total is None else state + head_column(through, choice_t) * total
    return total


def end_factor(pos, decay):
    last = slice(STRETCH - 1, STRETCH)
    places = iota((STRETCH, LANES), 0).astype(f32)
    return jnp.where(places >= STRETCH - 1.0 - pos[last], jnp.exp(decay[last] - decay), 0.0)


def steps_of(step_pre, pos, heads):
    lanes = iota((STRETCH, LANES), 1)
    return jnp.where((lanes < heads) & (pos >= 0.0), softplus(step_pre), 0.0)


def conv_of(mx_ref, taps_ref, pos):
    total = taps_ref[CONV : CONV + 1, :] + taps_ref[CONV - 1 : CONV, :] * mx_ref[8 : 8 + STRETCH, :]
    for s in range(1, CONV):
        window = mx_ref[8 - s : 8 - s + STRETCH, :] * (pos[:, :1] >= float(s)).astype(f32)
        total = total + taps_ref[CONV - 1 - s : CONV - s, :] * window
    return total


def place_stacks(place_ref, stacks, write):
    number = 0
    for stack in stacks:
        size = stack.shape[1]
        for k in range(stack.shape[0]):
            write(pl.ds(pl.multiple_of(place_ref[number], size), size), stack[k])
            number += 1


def forward_kernel(dims, count, groups, place_ref, *refs):
    own_stacks, refs = refs[:count], refs[count:]
    more_stacks, refs = refs[: count * (groups - 1)], refs[count * (groups - 1) :]
    pos_ref, tok_ref, halo_ref, taps_ref, bias_ref, rate_ref, skip_ref = refs[:7]
    gate_ref, mixed_ref, vkq_ref, ssm_ref, step_ref, decay_ref, enter_ref, last_ref = refs[7:15]
    edge_ref, gain_ref, w_ref, mx, state, through = refs[15:]
    heads, head_size, inner, states = dims
    width = inner + 2 * states
    at_mixed, at_misc = inner, inner + width
    c = pl.program_id(0)

    @pl.when(c == 0)
    def _():
        own = inner // groups

        def write_own(at, piece):
            w_ref[at, 0:own] = piece[:, 0:own]
            w_ref[at, at_mixed : at_mixed + own] = piece[:, own : 2 * own]
            w_ref[at, at_mixed + inner : at_misc] = piece[:, 2 * own : 2 * own + 2 * states]
            w_ref[at, at_misc:] = piece[:, 2 * own + 2 * states :]

        def write_more(at, piece):
            w_ref[at, own:inner] = piece[:, 0:own]
            w_ref[at, at_mixed + own : at_mixed + inner] = piece[:, own : 2 * own]
            w_ref[at, at_misc:] = w_ref[at, at_misc:] + piece[:, 2 * own :]

        place_stacks(place_ref, own_stacks, write_own)
        place_stacks(place_ref, more_stacks, write_more)
        misc = w_ref[:, at_misc:].astype(f32).T
        gain_ref[...] = jnp.broadcast_to(misc[heads : heads + 1], gain_ref.shape)
        unit = row_norm(halo_ref[...].astype(f32))[1]
        low = (unit * gain_ref[0:1, :]).astype(bf16)
        edge = nn(low, w_ref[:, at_mixed:at_misc]).astype(bf16)
        edge_ref[...] = edge
        mx[0:8, :] = edge[HALO - 8 :].astype(f32)
        state[...] = jnp.zeros_like(state)
        through[...] = jnp.ones_like(through)

    @pl.when(c > 0)
    def _():
        mx[0:8, :] = mx[STRETCH : STRETCH + 8, :]

    pos = column(pos_ref[0].astype(f32))
    unit = row_norm(tok_ref[...].astype(f32))[1]
    normed = (unit * gain_ref[0:1, :]).astype(bf16)
    gate_ref[...] = nn(normed, w_ref[:, :at_mixed])
    mixed = nn(normed, w_ref[:, at_mixed:at_misc]).astype(bf16)
    mixed_ref[...] = mixed
    mx[8 : 8 + STRETCH, :] = mixed.astype(f32)
    step_pre = nn(normed, w_ref[:, at_misc:]) + bias_ref[...]
    step_ref[...] = step_pre
    conv = conv_of(mx, taps_ref, pos)
    vkq = (conv * jax.nn.sigmoid(conv)).astype(bf16)
    vkq_ref[...] = vkq
    values, keys, queries = vkq[:, :inner], vkq[:, inner : inner + states], vkq[:, inner + states :]
    dt = steps_of(step_pre, pos, heads)
    rate = -jnp.exp(rate_ref[...])
    tri = (iota((STRETCH, STRETCH), 1) <= iota((STRETCH, STRETCH), 0)).astype(bf16)
    decay = dot_triple(tri, dt * rate)
    decay_ref[...] = decay
    decay_t = decay.T
    mask = mask_matrix(pos)
    gram = nt(queries, keys)
    choice = head_choice(inner, head_size)
    value_f = values.astype(f32)
    dt_values = (value_f * dot_pair(dt, choice)).astype(bf16)
    per = LANES // head_size
    within = []
    for pair in range(inner // LANES):
        part = dt_values[:, pair * LANES : (pair + 1) * LANES]
        total = None
        for k in range(per):
            h = pair * per + k
            m = (gram * jnp.exp((decay[:, h : h + 1] - decay_t[h : h + 1, :]) + mask)).astype(bf16)
            term = nn(m, pair_sel(part, k, head_size))
            total = term if total is None else total + term
        within.append(total)
    within = jnp.concatenate(within, axis=1)
    entering = state[...]
    enter_ref[0] = entering
    across = nt(queries, entering.astype(bf16)) * dot_pair(carry_factor(pos, decay), choice)
    ssm_ref[...] = within + across + skip_ref[...] * value_f
    wend = end_factor(pos, decay) * dt
    fresh = tn((value_f * dot_pair(wend, choice)).astype(bf16), keys)
    passing = passing_row(pos, decay)
    through[...] = through[...] * passing
    state[...] = head_column(passing, head_choice_t(inner, head_size)) * entering + fresh

    @pl.when(c == pl.num_programs(0) - 1)
    def _():
        pack_state(last_ref, state[...], through[0:1, :], heads // groups)


def stats_kernel(dims, count, groups, hops, place_ref, *refs):
    stacks, refs = refs[:count], refs[count:]
    come_refs, refs = refs[:hops], refs[hops:]
    pos_ref, ssm_ref, gate_ref, q_ref, decay_ref, enter_ref, og_ref, gain_ref = refs[:8]
    full_ref, state_ref, gno_ref, stats_ref, branch_ref, out_ref, through, come = refs[8:]
    heads, head_size, inner, states = dims
    c = pl.program_id(0)

    @pl.when(c == 0)
    def _():
        def write(at, piece):
            out_ref[at, :] = piece

        place_stacks(place_ref, stacks, write)
        through[...] = jnp.ones_like(through)
        come[...] = join_states(come_refs, head_choice_t(inner, head_size), groups)

    pos = column(pos_ref[0].astype(f32))
    decay = decay_ref[...]
    coming = come[...]
    choice = head_choice(inner, head_size)
    before = through[0:1, :]
    state_ref[0] = (
        enter_ref[0] + head_column(before, head_choice_t(inner, head_size)) * coming
    ).astype(bf16)
    across = nt(q_ref[...], coming.astype(bf16))
    ssm = ssm_ref[...] + across * dot_pair(carry_factor(pos, decay) * before, choice)
    full_ref[...] = ssm
    through[...] = through[...] * passing_row(pos, decay)
    gate = gate_ref[...]
    gated = ssm * (gate * jax.nn.sigmoid(gate))
    gno = nn(og_ref[...], out_ref[...])
    gno_ref[...] = gno
    gain = gain_ref[...] * (pos[:, :1] >= 0.0).astype(f32)
    branch_ref[...] = nt((gated * gain).astype(bf16), out_ref[...]).astype(bf16)
    grad_unit = gno * gain
    squares = jnp.sum(gated * gated, axis=1, keepdims=True)
    dots = jnp.sum(grad_unit * gated, axis=1, keepdims=True)
    lanes = iota((STRETCH, LANES), 1)
    stats_ref[...] = jnp.where(lanes == 0, squares, dots).T[0:2]


def gate_back_kernel(
    dims, groups,
    pos_ref, stats_ref, ssm_ref, gate_ref, gno_ref, vkq_ref, decay_ref, gain_ref, skip_ref,
    gssm_ref, ggate_ref, low_ref, glog_ref, leave_ref, last_ref, sums_ref,
    back, through,
):
    heads, head_size, inner, states = dims
    step = pl.program_id(0)

    @pl.when(step == 0)
    def _():
        back[...] = jnp.zeros_like(back)
        through[...] = jnp.ones_like(through)
        sums_ref[...] = jnp.zeros_like(sums_ref)

    pos = column(pos_ref[0].astype(f32))
    valid = (pos[:, :1] >= 0.0).astype(f32)
    stats = column(stats_ref[...])
    scale = lax.rsqrt(stats[:, 0:1] / INNER + epsilon)
    dots = stats[:, 1:2]
    gate = gate_ref[...]
    ssm = ssm_ref[...]
    sig = jax.nn.sigmoid(gate)
    act = gate * sig
    gated = ssm * act
    unit = gated * scale
    gain = gain_ref[...]
    gno = gno_ref[...]
    low_ref[...] = (unit * gain * valid).astype(bf16)
    grad_unit = gno * gain * valid
    grad_gated = scale * (grad_unit - gated * (scale * scale * dots * (1.0 / INNER)))
    gssm = (grad_gated * act).astype(bf16)
    gssm_ref[...] = gssm
    ggate_ref[...] = (grad_gated * ssm * sig * (1.0 + gate * (1.0 - sig))).astype(bf16)
    g = gssm.astype(f32)
    value_f = vkq_ref[:, :inner].astype(f32)
    queries = vkq_ref[:, inner + states :]
    g_values = g * value_f
    choice = head_choice(inner, head_size)
    choice_t = head_choice_t(inner, head_size)
    glog_ref[...] = dot_pair(g * ssm - skip_ref[...] * g_values, choice_t)
    sums_ref[0:1, :] += jnp.sum(gno * unit * valid, axis=0, keepdims=True)
    sums_ref[1:2, :] += jnp.sum(g_values, axis=0, keepdims=True)
    decay = decay_ref[...]
    core = (g * dot_pair(carry_factor(pos, decay), choice)).astype(bf16)
    after = back[...]
    leave_ref[0] = after
    passing = passing_row(pos, decay)
    through[...] = through[...] * passing
    back[...] = tn(core, queries) + head_column(passing, choice_t) * after

    @pl.when(step == pl.num_programs(0) - 1)
    def _():
        pack_state(last_ref, back[...], through[0:1, :], heads // groups)


def scan_back_kernel(
    dims, first, blocks, groups, hops,
    pos_ref, tok_ref, w_ref, gain_ref, taps_ref, rate_ref, skip_ref, mixed_ref, before_ref,
    edge_ref, vkq_ref, gssm_ref, ggate_ref, glog_ref, step_ref, decay_ref, state_ref, leave_ref,
    gp_in, pp_in, suffix_in, gsum_in, tsum_in, hsum_in, *refs,
):
    go_refs, refs = refs[:hops], refs[hops:]
    part_ref, ret_ref, grads_ref, gp_out, pp_out, suffix, gsum_ref, tsum_ref, hsum_ref = refs[-14:-5]
    mx, gp, pp, edge, go = refs[-5:]
    heads, head_size, inner, states = dims
    width = inner + 2 * states
    at_mixed, at_misc = inner, inner + width
    step = pl.program_id(0)
    c = blocks - 1 - first - step

    @pl.when(step == 0)
    def _():
        for out, given in (
            (suffix, suffix_in), (gsum_ref, gsum_in), (tsum_ref, tsum_in), (hsum_ref, hsum_in)
        ):
            out[...] = given[...]
        go[...] = join_states(go_refs, head_choice_t(inner, head_size), groups)
        gp[STRETCH : STRETCH + 8, :] = gp_in[...]
        pp[STRETCH : STRETCH + 8, :] = pp_in[...]

    @pl.when(step > 0)
    def _():
        gp[STRETCH : STRETCH + 8, :] = gp[0:8, :]
        pp[STRETCH : STRETCH + 8, :] = pp[0:8, :]

    @pl.when(c == 0)
    def _():
        mx[0:8, :] = edge_ref[HALO - 8 :, :].astype(f32)

    @pl.when(c > 0)
    def _():
        mx[0:8, :] = before_ref[HALO - 8 :, :].astype(f32)

    pos = column(pos_ref[0].astype(f32))
    pp[0:STRETCH, :] = pos
    mx[8 : 8 + STRETCH, :] = mixed_ref[...].astype(f32)
    values = vkq_ref[:, :inner]
    keys = vkq_ref[:, inner : inner + states]
    queries = vkq_ref[:, inner + states :]
    value_f = values.astype(f32)
    gssm = gssm_ref[...]
    g = gssm.astype(f32)
    step_pre = step_ref[...]
    decay = decay_ref[...]
    decay_t = decay.T
    dt = steps_of(step_pre, pos, heads)
    rate = -jnp.exp(rate_ref[...])
    choice = head_choice(inner, head_size)
    choice_t = head_choice_t(inner, head_size)
    dt_wide = dot_pair(dt, choice)
    dt_values = (value_f * dt_wide).astype(bf16)
    mask = mask_matrix(pos)
    gram = nt(queries, keys)
    per = LANES // head_size
    grad_gram = None
    turned = []
    for pair in range(inner // LANES):
        lanes = slice(pair * LANES, (pair + 1) * LANES)
        total = None
        for k in range(per):
            h = pair * per + k
            spread = jnp.exp((decay[:, h : h + 1] - decay_t[h : h + 1, :]) + mask)
            own_g = pair_sel(gssm[:, lanes], k, head_size)
            term = tn((gram * spread).astype(bf16), own_g)
            total = term if total is None else total + term
            more = nt(own_g, dt_values[:, lanes]) * spread
            grad_gram = more if grad_gram is None else grad_gram + more
        turned.append(total)
    turned = jnp.concatenate(turned, axis=1)
    grad_gram = grad_gram.astype(bf16)
    entering = state_ref[0]
    after = suffix[0:1, :]
    leaving = leave_ref[0] + head_column(after, choice_t) * go[...]
    leaving_low = leaving.astype(bf16)
    passing = passing_row(pos, decay)
    suffix[...] = suffix[...] * passing
    far = end_factor(pos, decay)
    wend = far * dt
    wend_wide = dot_pair(wend, choice)
    keyed = nt(keys, leaving_low)
    core = (g * dot_pair(carry_factor(pos, decay), choice)).astype(bf16)
    grad_values = skip_ref[...] * g + dt_wide * turned + wend_wide * keyed
    grad_keys = tn(grad_gram, queries) + nn((value_f * wend_wide).astype(bf16), leaving_low)
    grad_queries = nn(grad_gram, keys) + nn(core, entering)
    within_dt = dot_pair(value_f * turned, choice_t)
    within_logs = dot_pair(dt_values.astype(f32) * turned, choice_t)
    grad_wend = dot_pair(value_f * keyed, choice_t)
    through = jnp.sum(leaving * entering.astype(f32), axis=1, keepdims=True)
    last_grad = passing * jnp.sum(through * choice_t.astype(f32), axis=0, keepdims=True)
    end_terms = grad_wend * wend
    grad_logs = glog_ref[...] - within_logs - end_terms
    at_last = iota((STRETCH, LANES), 0) == STRETCH - 1
    grad_logs = grad_logs + jnp.where(
        at_last, jnp.sum(end_terms, axis=0, keepdims=True) + last_grad, 0.0
    )
    tri = (iota((STRETCH, STRETCH), 1) >= iota((STRETCH, STRETCH), 0)).astype(bf16)
    grad_steps = dot_triple(tri, grad_logs)
    grad_dt = within_dt + grad_wend * far + grad_steps * rate
    lane_ok = (iota((STRETCH, LANES), 1) < heads) & (pos >= 0.0)
    grad_step = jnp.where(lane_ok, grad_dt * jax.nn.sigmoid(step_pre), 0.0)
    hsum_ref[0:1, :] += jnp.sum(grad_step, axis=0, keepdims=True)
    hsum_ref[1:2, :] += jnp.sum(grad_steps * dt, axis=0, keepdims=True) * rate

    conv = conv_of(mx, taps_ref, pos)
    sig = jax.nn.sigmoid(conv)
    grad_conv = jnp.concatenate([grad_values, grad_keys, grad_queries], axis=1)
    grad_pre = grad_conv * (sig * (1.0 + conv * (1.0 - sig)))
    gp[0:STRETCH, :] = grad_pre
    tsum_ref[CONV : CONV + 1, :] += jnp.sum(grad_pre, axis=0, keepdims=True)
    tsum_ref[CONV - 1 : CONV, :] += jnp.sum(
        grad_pre * mx[8 : 8 + STRETCH, :], axis=0, keepdims=True
    )
    grad_mixed = grad_pre * taps_ref[CONV - 1 : CONV, :]
    for s in range(1, CONV):
        inside = (pos[:, :1] >= float(s)).astype(f32)
        tsum_ref[CONV - 1 - s : CONV - s, :] += jnp.sum(
            grad_pre * inside * mx[8 - s : 8 - s + STRETCH, :], axis=0, keepdims=True
        )
        later = (pp[s : s + STRETCH, :][:, :1] >= float(s)).astype(f32)
        grad_mixed = grad_mixed + gp[s : s + STRETCH, :] * later * taps_ref[
            CONV - 1 - s : CONV - s, :
        ]
    grads = jnp.concatenate(
        [ggate_ref[...], grad_mixed.astype(bf16), grad_step.astype(bf16)], axis=1
    )
    partial = nt(grads, w_ref[...])
    unit = row_norm(tok_ref[...].astype(f32))[1]
    grads_ref[...] = grads[:, at_mixed:]
    gp_out[...] = gp[0:8, :]
    pp_out[...] = pp[0:8, :]
    part_ref[...] = partial.astype(bf16)
    gsum_ref[0:1, :] += jnp.sum(partial * unit, axis=0, keepdims=True)
    ret_ref[...] = jnp.zeros_like(ret_ref)

    @pl.when(c == 0)
    def _():
        edge[0:8, :] = jnp.zeros((8, width), f32)
        total = jnp.zeros((8, width), f32)
        for s in range(1, CONV):
            inside = (pos[0:8, :1] >= float(s)).astype(f32)
            edge[8:16, :] = gp[0:8, :] * inside
            total = total + edge[s : s + 8, :] * taps_ref[CONV - 1 - s : CONV - s, :]
        ret_ref[...] = total


def spread_rows(out_ref, total_ref, groups, cores):
    size = total_ref.shape[0] // (cores * groups)
    for at in range(cores * groups):
        out_ref[at % cores, at // cores] = total_ref[at * size : (at + 1) * size, :].astype(bf16)


def first_grad_kernel(
    dims, groups, cores, tok_ref, gain_ref, gate_ref, og_ref, low_ref, out_ref, total
):
    inner = dims[2]
    c = pl.program_id(0)

    @pl.when(c == 0)
    def _():
        total[...] = jnp.zeros_like(total)

    normed = (row_norm(tok_ref[...].astype(f32))[1] * gain_ref[0:1, :]).astype(bf16)
    total[:, :inner] += tn(normed, gate_ref[...])
    total[:, inner:] += tn(og_ref[...], low_ref[...])

    @pl.when(c == pl.num_programs(0) - 1)
    def _():
        spread_rows(out_ref, total, groups, cores)


def weight_grad_kernel(
    dims, groups, cores,
    tok_ref, gain_ref, grads_ref, extra_ref, gsum_ref, tail_ref,
    out_ref,
    total,
):
    heads, head_size, inner, states = dims
    width = inner + 2 * states
    c = pl.program_id(0)

    @pl.when(c == 0)
    def _():
        total[...] = jnp.zeros_like(total)

    unit = row_norm(tok_ref[...].astype(f32))[1]
    normed = (unit * gain_ref[0:1, :]).astype(bf16)
    total[...] += tn(normed, grads_ref[...])

    @pl.when(c == pl.num_programs(0) - 1)
    def _():
        total[:, :width] += tn(normed[STRETCH - HALO :], extra_ref[...])
        norm = gsum_ref[0:1, :] + jnp.sum(
            tail_ref[...] * unit[STRETCH - HALO :], axis=0, keepdims=True
        )
        norm = jnp.broadcast_to(norm, (LANES, norm.shape[1])).T
        misc = total[:, width:]
        total[:, width:] = jnp.where(iota(misc.shape, 1) == heads, norm, misc)
        spread_rows(out_ref, total, groups, cores)


def mixed_out_kernel(stats_ref, branch_ref, tok_ref, out_ref):
    scale = lax.rsqrt(column(stats_ref[...])[:, 0:1] / INNER + epsilon)
    out_ref[...] = (tok_ref[...].astype(f32) + scale * branch_ref[...].astype(f32)).astype(bf16)


def tokens_grad_kernel(grad_ref, tok_ref, og_ref, gain_ref, out_ref):
    scaling, unit = row_norm(tok_ref[...].astype(f32))
    grad = grad_ref[...].astype(f32) * gain_ref[0:1, :]
    mean = jnp.mean(grad * unit, axis=-1, keepdims=True)
    out_ref[...] = scaling * (grad - unit * mean) + og_ref[...].astype(f32)


def own_rows_kernel(mine_ref, came_ref, tok_ref, gain_ref, tail_ref, out_ref):
    scaling, unit = row_norm(tok_ref[...].astype(f32))
    grad = mine_ref[...].astype(f32) + came_ref[...].astype(f32)
    size, model = grad.shape
    tail = jnp.concatenate([jnp.zeros((size - HALO, model), f32), tail_ref[...]], axis=0)
    grad = grad + jnp.where(pl.program_id(0) == pl.num_programs(0) - 1, tail, 0.0)
    grad = grad * gain_ref[0:1, :]
    mean = jnp.mean(grad * unit, axis=-1, keepdims=True)
    out_ref[...] = (scaling * (grad - unit * mean)).astype(bf16)


def add_kernel(a_ref, b_ref, out_ref):
    out_ref[...] = a_ref[...].astype(f32) + b_ref[...].astype(f32)


def own_branch_kernel(stats_ref, mine_ref, came_ref, tok_ref, out_ref):
    scale = lax.rsqrt(column(stats_ref[...])[:, 0:1] / INNER + epsilon)
    branch = mine_ref[...].astype(f32) + came_ref[...].astype(f32)
    out_ref[...] = (tok_ref[...].astype(f32) + scale * branch).astype(bf16)


def per_device(
    tokens,
    norm_gain,
    inner_weight,
    state_weight,
    step_weight,
    inner_taps,
    state_taps,
    step_bias,
    log_rate,
    skip_gain,
    gated_gain,
    out_weight,
    out_grad,
    positions,
):
    shares = row_shares()
    share = lax.axis_index("tp") // (lax.axis_size("tp") // shares)
    all_rows, model = tokens.shape
    rows = all_rows // shares
    own_heads = step_bias.shape[0]
    own_inner = gated_gain.shape[0]
    head_size = own_inner // own_heads
    heads, inner = own_heads * shares, own_inner * shares
    states = state_weight.shape[1] // 2
    blocks = rows // STRETCH
    width = inner + 2 * states
    at_mixed, at_misc = inner, inner + width
    columns = at_misc + LANES
    dims = (heads, head_size, inner, states)
    parts = lax.axis_size("ctx") * shares

    def own_share(x, size):
        return x if shares == 1 else lax.dynamic_slice_in_dim(x, share * size, size)

    def joined(groups, begin, size):
        return [g[:, begin : begin + size] for g in groups]

    def steps_at(lane):
        return jnp.pad(step_weight, ((0, 0), (lane, LANES - lane - own_heads)))

    own_rows_of = norm_gain.shape[0]
    gain_lanes = jnp.concatenate(
        [
            jnp.zeros((own_rows_of, heads), bf16),
            norm_gain[:, None],
            jnp.zeros((own_rows_of, LANES - heads - 1), bf16),
        ],
        axis=1,
    )
    edge_rows = lax.ppermute(tokens[all_rows - HALO :], "ctx", [(0, 1)])
    all_tokens, all_grad = tokens, out_grad
    tokens, out_grad = own_share(tokens, rows), own_share(out_grad, rows)
    positions = own_share(positions, rows)
    halo_tokens = edge_rows
    if shares > 1:
        halo_tokens = jnp.where(share == 0, edge_rows, all_tokens[rows - HALO : rows])

    head_params = jnp.stack([step_bias, log_rate, skip_gain])
    small_own = jnp.concatenate(
        [
            jnp.pad(jnp.concatenate([inner_taps, gated_gain[None]]), ((0, 8 - CONV - 2), (0, 0))),
            jnp.pad(head_params, ((0, 5), (0, LANES - own_heads))),
        ],
        axis=1,
    )
    channels_in = [inner_weight[0], inner_weight[1]]
    near = gather_near(
        jnp.concatenate(channels_in + [state_weight, steps_at(0) + gain_lanes], axis=1)
    )
    stacks = gather_stacks(near)
    count = len(stacks)
    out_near = out_weight.T
    if shares > 1:
        more = swap_tp(jnp.concatenate(channels_in + [steps_at(own_heads)], axis=1), 2)
        near = gather_near(tied(more, tokens, out_grad, halo_tokens))
        out_more = swap_tp(tied(out_near, more), 2)
        small_more = swap_tp(tied(small_own, more), 2)
        near[-1] = tied(near[-1], out_more, small_more)
        stacks += gather_stacks(near)
        out_near = jnp.concatenate([out_near, out_more], axis=1)
    out_near = gather_near(tied(out_near, near[-1]))
    place = gather_place(own_rows_of)

    small_groups = [small_own] + ([small_more] if shares > 1 else [])
    channel_rows = jnp.concatenate(joined(small_groups, 0, own_inner), axis=1)
    head_rows = jnp.concatenate(joined(small_groups, own_inner, own_heads), axis=1)
    taps = jnp.concatenate(
        [channel_rows, jnp.pad(state_taps, ((0, 8 - CONV - 1), (0, 0)))], axis=1
    )
    gain_row = channel_rows[CONV + 1 : CONV + 2]
    skip_row = jnp.repeat(head_rows[2], head_size)[None, :]
    head_rows = jnp.pad(head_rows, ((0, 0), (0, LANES - heads)))
    bias_row, rate_row = head_rows[0:1], head_rows[1:2]
    pos_rows = positions.reshape(blocks, 1, STRETCH)

    def fixed(shape):
        return pl.BlockSpec(shape, lambda c: (0,) * len(shape))

    def by_rows(cols, order, at=0):
        return pl.BlockSpec((STRETCH, cols), lambda c: (order(c), at))

    def by_block(order):
        return pl.BlockSpec((1, inner, states), lambda c: (order(c), 0, 0))

    def pos_spec(order):
        return pl.BlockSpec((1, 1, STRETCH), lambda c: (order(c), 0, 0))

    def ahead(c):
        return c

    def reverse(c):
        return blocks - 1 - c

    def shape(*dims_of, dtype=f32):
        return jax.ShapeDtypeStruct(dims_of, dtype)

    light = pl.CostEstimate(flops=1024, bytes_accessed=1024, transcendentals=0)
    params = pltpu.CompilerParams(
        dimension_semantics=("arbitrary",), vmem_limit_bytes=VMEM_BYTES
    )

    scalars = pl.BlockSpec(memory_space=pltpu.SMEM)
    gate, mixed, vkq, ssm_local, step_pre, decay, enter, last_state, edge, model_gain, weight = (
        pl.pallas_call(
            functools.partial(forward_kernel, dims, count, shares),
            grid=(blocks,),
            in_specs=[
                scalars,
                *[fixed(a.shape) for a in stacks],
                pos_spec(ahead),
                by_rows(model, ahead),
                fixed((HALO, model)),
                fixed((8, width)),
                fixed((1, LANES)),
                fixed((1, LANES)),
                fixed((1, inner)),
            ],
            out_specs=[
                by_rows(inner, ahead),
                by_rows(width, ahead),
                by_rows(width, ahead),
                by_rows(inner, ahead),
                by_rows(LANES, ahead),
                by_rows(LANES, ahead),
                by_block(ahead),
                fixed((inner + HALO, states)),
                fixed((HALO, width)),
                fixed((8, model)),
                fixed((model, columns)),
            ],
            out_shape=[
                shape(rows, inner),
                shape(rows, width, dtype=bf16),
                shape(rows, width, dtype=bf16),
                shape(rows, inner),
                shape(rows, LANES),
                shape(rows, LANES),
                shape(blocks, inner, states),
                shape(inner + HALO, states, dtype=bf16),
                shape(HALO, width, dtype=bf16),
                shape(8, model),
                shape(model, columns, dtype=bf16),
            ],
            scratch_shapes=[
                pltpu.VMEM((STRETCH + 8, width), f32),
                pltpu.VMEM((inner, states), f32),
                pltpu.VMEM((8, LANES), f32),
            ],
            compiler_params=params,
            name="forward",
        )(
            place, *stacks, pos_rows, tokens, halo_tokens, taps, bias_row, rate_row, skip_row
        )
    )
    out_stacks = gather_stacks(out_near[:-1] + [tied(out_near[-1], last_state)])
    coming = [shift_part(last_state, by) for by in range(1, parts)]
    ssm, state, grad_out, stats, branch, out_t = pl.pallas_call(
        functools.partial(stats_kernel, dims, count, shares, parts - 1),
        grid=(blocks,),
        in_specs=[
            scalars,
            *[fixed(a.shape) for a in out_stacks],
            *[fixed((inner + HALO, states))] * (parts - 1),
            pos_spec(ahead),
            by_rows(inner, ahead),
            by_rows(inner, ahead),
            by_rows(states, ahead, (inner + states) // states),
            by_rows(LANES, ahead),
            by_block(ahead),
            by_rows(model, ahead),
            fixed((1, inner)),
        ],
        out_specs=[
            by_rows(inner, ahead),
            by_block(ahead),
            by_rows(inner, ahead),
            pl.BlockSpec((2, STRETCH), lambda c: (0, c)),
            by_rows(model, ahead),
            fixed((model, inner)),
        ],
        out_shape=[
            shape(rows, inner),
            shape(blocks, inner, states, dtype=bf16),
            shape(rows, inner),
            shape(2, rows),
            shape(rows, model, dtype=bf16),
            shape(model, inner, dtype=bf16),
        ],
        scratch_shapes=[pltpu.VMEM((8, LANES), f32), pltpu.VMEM((inner, states), f32)],
        compiler_params=params,
        name="stats",
    )(
        place, *out_stacks, *coming, pos_rows, ssm_local, gate, vkq, decay, enter, out_grad, gain_row
    )
    half = rows // 2
    member = lax.axis_index("tp") % 2

    def halves(x):
        sent = lax.dynamic_slice_in_dim(x, (1 - member) * half, half)
        return lax.dynamic_slice_in_dim(tied(x, sent), member * half, half), swap_tp(sent, 1)

    if shares > 1:
        own_tokens = lax.dynamic_slice_in_dim(tokens, member * half, half)
        stats = stats + swap_tp(stats, 1)
        own_branch = pl.pallas_call(
            own_branch_kernel,
            grid=(half // STRETCH,),
            in_specs=[pl.BlockSpec((2, STRETCH), lambda c: (0, c))]
            + [by_rows(model, ahead)] * 3,
            out_specs=by_rows(model, ahead),
            out_shape=shape(half, model, dtype=bf16),
            compiler_params=params,
            name="own_branch",
        )(
            lax.dynamic_slice_in_dim(stats, member * half, half, 1),
            *halves(tied(branch, stats)),
            own_tokens,
        )
    else:
        stats = sum_tp_small(stats)
        first_total = lax.psum(branch, "tp")
    grad_ssm, grad_gate, normed_out, grad_logs, leave, last_back, gate_sums = pl.pallas_call(
        functools.partial(gate_back_kernel, dims, shares),
        grid=(blocks,),
        in_specs=[
            pos_spec(reverse),
            pl.BlockSpec((2, STRETCH), lambda c: (0, reverse(c))),
            by_rows(inner, reverse),
            by_rows(inner, reverse),
            by_rows(inner, reverse),
            by_rows(width, reverse),
            by_rows(LANES, reverse),
            fixed((1, inner)),
            fixed((1, inner)),
        ],
        out_specs=[
            by_rows(inner, reverse),
            by_rows(inner, reverse),
            by_rows(inner, reverse),
            by_rows(LANES, reverse),
            by_block(reverse),
            fixed((inner + HALO, states)),
            fixed((8, inner)),
        ],
        out_shape=[
            shape(rows, inner, dtype=bf16),
            shape(rows, inner, dtype=bf16),
            shape(rows, inner, dtype=bf16),
            shape(rows, LANES),
            shape(blocks, inner, states),
            shape(inner + HALO, states, dtype=bf16),
            shape(8, inner),
        ],
        scratch_shapes=[pltpu.VMEM((inner, states), f32), pltpu.VMEM((8, LANES), f32)],
        compiler_params=params,
        cost_estimate=light,
        name="gate_back",
    )(pos_rows, stats, ssm, gate, grad_out, vkq, decay, gain_row, skip_row)
    going = [shift_part(last_back, -by) for by in range(1, parts)]
    if shares > 1:
        mixed_out = lax.all_gather(tied(own_branch, *going), "tp", axis=0, tiled=True)
        first_total = mixed_out[:8, :LANES]
    near_count, cores = (lax.axis_size("fsdp"), lax.axis_size("ctx")) if small_mesh() else (1, 1)

    def grad_shape(cols):
        return (cores, near_count, model // (cores * near_count), cols)

    first_grad = pl.pallas_call(
        functools.partial(first_grad_kernel, dims, near_count, cores),
        grid=(blocks,),
        in_specs=[
            by_rows(model, ahead),
            fixed((8, model)),
            by_rows(inner, ahead),
            by_rows(model, ahead),
            by_rows(inner, ahead),
        ],
        out_specs=fixed(grad_shape(2 * inner)),
        out_shape=shape(*grad_shape(2 * inner), dtype=bf16),
        scratch_shapes=[pltpu.VMEM((model, 2 * inner), f32)],
        compiler_params=params,
        cost_estimate=light,
        name="first_grad",
    )(tokens, model_gain, grad_gate, out_grad, normed_out)
    grad_gate = tied(grad_gate, first_grad)
    first_grad = scatter_rows(first_grad)
    per_halo = STRETCH // HALO

    def scan_piece(first, size, going, carried):
        def place_of(c):
            return blocks - 1 - first - c

        grads_before, *carried = carried
        carry_shapes = [a.shape for a in carried]
        aliases = {}
        in_specs = [
            pos_spec(place_of),
            by_rows(model, place_of),
            fixed((model, columns)),
            fixed((8, model)),
            fixed((8, width)),
            fixed((1, LANES)),
            fixed((1, inner)),
            by_rows(width, place_of),
            pl.BlockSpec(
                (HALO, width), lambda c: (jnp.maximum(place_of(c) * per_halo - 1, 0), 0)
            ),
            fixed((HALO, width)),
            by_rows(width, place_of),
            by_rows(inner, place_of),
            by_rows(inner, place_of),
            by_rows(LANES, place_of),
            by_rows(LANES, place_of),
            by_rows(LANES, place_of),
            by_block(place_of),
            by_block(place_of),
            *[fixed(a) for a in carry_shapes],
            *[fixed((inner + HALO, states))] * (parts - 1),
        ]
        operands = [
            pos_rows, tokens, weight, model_gain, taps, rate_row, skip_row, mixed, mixed, edge,
            vkq, grad_ssm, grad_gate, grad_logs, step_pre, decay, state, leave, *carried, *going,
        ]
        if grads_before is not None:
            aliases = {len(operands): 2}
            operands.append(grads_before)
            in_specs.append(pl.BlockSpec(memory_space=pl.ANY))
        return pl.pallas_call(
            functools.partial(scan_back_kernel, dims, first, blocks, shares, parts - 1),
            grid=(size,),
            in_specs=in_specs,
            out_specs=[
                pl.BlockSpec((STRETCH, model), lambda c: (size - 1 - c, 0)),
                fixed((8, width)),
                by_rows(columns - inner, place_of),
                *[fixed(a) for a in carry_shapes],
            ],
            out_shape=[
                shape(size * STRETCH, model, dtype=bf16),
                shape(8, width),
                shape(rows, columns - inner, dtype=bf16),
                *[shape(*a) for a in carry_shapes],
            ],
            input_output_aliases=aliases,
            scratch_shapes=[
                pltpu.VMEM((STRETCH + 8, width), f32),
                pltpu.VMEM((STRETCH + 8, width), f32),
                pltpu.VMEM((STRETCH + 8, LANES), f32),
                pltpu.VMEM((16, width), f32),
                pltpu.VMEM((inner, states), f32),
            ],
            compiler_params=params,
            cost_estimate=light,
        name="scan_back",
        )(*operands)

    carried = [
        None,
        jnp.zeros((8, width), f32),
        jnp.zeros((8, LANES), f32),
        jnp.ones((8, LANES), f32),
        jnp.zeros((8, model), f32),
        jnp.zeros((8, width), f32),
        jnp.zeros((8, LANES), f32),
    ]
    partial, returned, *carried = scan_piece(0, blocks, going, carried)
    grads, _, _, _, norm_sums, tap_sums, head_sums = carried

    small = jnp.concatenate([tap_sums.reshape(-1, LANES), gate_sums.reshape(-1, LANES), head_sums])
    if shares > 1:
        mine, came = halves(partial)
        small = tied(small, mine)
    small = sum_rows_group(small)
    extra = shift_part(returned, -1).astype(bf16)
    if shares > 1:
        extra = jnp.concatenate(
            [extra[:, own_inner:inner], extra[:, :own_inner], extra[:, inner:]], axis=1
        )
    extra = jnp.concatenate([jnp.zeros((HALO - 8, width), bf16), extra], axis=0)
    tail_part = nt(extra, weight[:, at_mixed:at_misc])

    if shares > 1:
        tail_low = tail_part.astype(bf16)
        tail_sum = tail_low.astype(f32) + swap_tp(tail_low, 1).astype(f32)
        tail_sum = jnp.where(member == 1, tail_sum, 0.0)
        own_rows = pl.pallas_call(
            own_rows_kernel,
            grid=(half // STRETCH,),
            in_specs=[by_rows(model, ahead)] * 3 + [fixed((8, model)), fixed((HALO, model))],
            out_specs=by_rows(model, ahead),
            out_shape=shape(half, model, dtype=bf16),
            compiler_params=params,
            name="own_rows",
        )(tied(mine, first_grad), came, own_tokens, model_gain, tail_sum)
        grads = tied(grads, own_rows, small, first_total)
        own_rows = tied(own_rows, first_total)
        second_total = lax.all_gather(own_rows, "tp", axis=0, tiled=True)
    else:
        partial = partial.at[rows - HALO :].add(tail_part.astype(bf16))
        partial = tied(partial, first_total)
        mixed_out = pl.pallas_call(
            mixed_out_kernel,
            grid=(blocks,),
            in_specs=[
                pl.BlockSpec((2, STRETCH), lambda c: (0, c)),
                by_rows(model, ahead),
                by_rows(model, ahead),
            ],
            out_specs=by_rows(model, ahead),
            out_shape=shape(rows, model, dtype=bf16),
            compiler_params=params,
            name="mixed_out",
        )(stats, first_total, tokens)
        tokens_grad = pl.pallas_call(
            tokens_grad_kernel,
            grid=(blocks,),
            in_specs=[by_rows(model, ahead)] * 3 + [fixed((8, model))],
            out_specs=by_rows(model, ahead),
            out_shape=shape(rows, model),
            compiler_params=params,
            name="tokens_grad",
        )(lax.psum(partial, "tp"), tokens, out_grad, model_gain)

    weight_grad = pl.pallas_call(
        functools.partial(weight_grad_kernel, dims, near_count, cores),
        grid=(blocks,),
        in_specs=[
            by_rows(model, ahead),
            fixed((8, model)),
            by_rows(columns - inner, ahead),
            fixed((HALO, width)),
            fixed((8, model)),
            fixed((HALO, model)),
        ],
        out_specs=fixed(grad_shape(columns - inner)),
        out_shape=shape(*grad_shape(columns - inner), dtype=bf16),
        scratch_shapes=[pltpu.VMEM((model, columns - inner), f32)],
        compiler_params=params,
        cost_estimate=light,
        name="weight_grad",
    )(tokens, model_gain, grads, extra, norm_sums, tail_part)
    late_grad = scatter_rows(weight_grad)
    at = 8 * width // LANES
    tap_total = small[:at].reshape(8, width)
    gate_total = small[at : at + 8 * inner // LANES].reshape(8, inner)
    head_total = small[at + 8 * inner // LANES :]
    shared = late_grad[:, inner:].astype(bf16)
    state_taps_grad = tap_total[: CONV + 1, inner:]
    rows_of = jnp.concatenate([tap_total[: CONV + 1, :inner], gate_total[:2]])
    channels_of = [first_grad[:, :inner], late_grad[:, :inner], first_grad[:, inner:]]
    steps_of_grad = late_grad[:, width:]
    groups = [g[:, :own_inner] for g in channels_of] + [steps_of_grad[:, :own_heads]]
    channel_total, head_total = rows_of[:, :own_inner], head_total[:2, :LANES]
    if shares > 1:
        sent = [g[:, own_inner:] for g in channels_of]
        sent.append(steps_of_grad[:, own_heads:])
        sent.append(jnp.zeros((steps_of_grad.shape[0], own_heads), f32))
        sent = jnp.concatenate(sent, axis=1).astype(bf16)
        few = jnp.concatenate(
            [
                jnp.pad(rows_of[:, own_inner:], ((0, 1), (0, 0))),
                jnp.pad(
                    head_total[:, own_heads : own_heads + LANES // 2], ((0, 6), (0, LANES // 2))
                ),
            ],
            axis=1,
        )
        pair = (shared.astype(f32) + swap_tp(shared, 1).astype(f32)).astype(bf16)
        taps_pair = state_taps_grad + swap_tp(state_taps_grad, 1)
        came, few = swap_tp(sent, 2).astype(f32), swap_tp(few, 2)
        groups = [
            g + came[:, k * own_inner : k * own_inner + g.shape[1]] for k, g in enumerate(groups)
        ]
        channel_total = channel_total + few[: CONV + 3, :own_inner]
        head_total = head_total[:, :own_heads] + few[:2, own_inner : own_inner + own_heads]
        shared = pair.astype(f32) + swap_tp(pair, 2).astype(f32)
        state_taps_grad = taps_pair + swap_tp(taps_pair, 2)
    else:
        shared = sum_tp_small(shared)
        state_taps_grad = sum_tp_small(state_taps_grad)
        head_total = head_total[:, :own_heads]
    state_weight_grad = shared[:, : 2 * states]
    norm_gain_grad = shared[:, 2 * states + heads]
    inner_weight_grad = jnp.stack(groups[:2])
    out_weight_grad = groups[2].T
    if shares > 1:
        second_total = tied(second_total, inner_weight_grad, out_weight_grad)
        tokens_grad = pl.pallas_call(
            add_kernel,
            grid=(all_rows // STRETCH,),
            in_specs=[by_rows(model, ahead)] * 2,
            out_specs=by_rows(model, ahead),
            out_shape=shape(all_rows, model),
            compiler_params=params,
            name="tokens_grad",
        )(second_total, all_grad)
    return (
        mixed_out,
        tokens_grad,
        norm_gain_grad,
        inner_weight_grad,
        state_weight_grad,
        groups[3],
        channel_total[: CONV + 1],
        state_taps_grad,
        head_total[0],
        head_total[1],
        jnp.sum(channel_total[CONV + 2].reshape(own_heads, head_size), axis=1),
        channel_total[CONV + 1],
        out_weight_grad,
    )


def solution(mesh):
    return jax.shard_map(
        per_device,
        mesh=mesh,
        in_specs=(
            P(("fsdp", "ctx"), None),
            P(("fsdp", "ctx")),
            P(None, ("fsdp", "ctx"), "tp"),
            P(("fsdp", "ctx"), None),
            P(("fsdp", "ctx"), "tp"),
            P(None, "tp"),
            P(),
            P("tp"),
            P("tp"),
            P("tp"),
            P("tp"),
            P("tp", ("fsdp", "ctx")),
            P(("fsdp", "ctx"), None),
            P(("fsdp", "ctx")),
        ),
        out_specs=(
            P(("fsdp", "ctx"), None),
            P(("fsdp", "ctx"), None),
            P(("fsdp", "ctx")),
            P(None, ("fsdp", "ctx"), "tp"),
            P(("fsdp", "ctx"), None),
            P(("fsdp", "ctx"), "tp"),
            P(None, "tp"),
            P(),
            P("tp"),
            P("tp"),
            P("tp"),
            P("tp"),
            P("tp", ("fsdp", "ctx")),
        ),
        check_vma=False,
    )
```

time: 801 us -> 408 us (0.51)
  waiting for transfers between devices: 370 us -> 127 us
  matrix products: 142 us -> 1.42 us
  Pallas kernels: 0 us -> 136 us
  blocking collectives: 97.3 us -> 0 us
  other arithmetic: 116 us -> 19.8 us
  starting transfers between devices: 5.16 us -> 59.1 us
    psum x2 -> x0, waiting for transfers between devices: 318 us -> none  [the longest x1 293 us: per_device(): lax.psum(branch_part.astype(jnp.bfloat16), 'tp').astype(jnp.float32)]
    dot_general x27 -> x1, matrix products: 142 us -> 1.42 us  [nt(): lax.dot_general(a, b, (((1,), (1,)), ((), ())), preferred_element_type=f32)]
    pallas_call x0 -> x9, Pallas kernels: none -> 136 us  [the longest x1 44.2 us: scan_piece(): pl.pallas_call(functools.partial(scan_back_kernel, dims, first, blocks, s...]
    ppermute x2 -> x44, waiting for transfers between devices: 0.01 us -> 127 us  [the longest x13 84.6 us: swap_tp(): return lax.ppermute(x, 'tp', [(i, i ^ k) for i in range(4)])]
    ppermute x2 -> x44, starting transfers between devices: 4.26 us -> 59 us  [the longest x13 24.6 us: swap_tp(): return lax.ppermute(x, 'tp', [(i, i ^ k) for i in range(4)])]
    reduce_scatter x2 -> x0, waiting for transfers between devices: 49.8 us -> none  [the longest x1 43.4 us: per_device(): lax.psum_scatter(inner_weight_grad.astype(jnp.bfloat16), ('fsdp', 'ctx'),...]
    psum x3 -> x0, blocking collectives: 47.2 us -> none  [the longest x1 26.4 us: per_device(): lax.psum((taps_grad[:, :local_inner], taps_grad[:, local_inner:], step_bi...]
    all_gather x7 -> x0, blocking collectives: 36.4 us -> none  [the longest x1 10.2 us: per_device(): lax.all_gather(norm_gain, ('fsdp', 'ctx'), axis=0, tiled=True)]
  transfers between devices with their start and end apart: 10 -> 46, of which waited for: 4 -> 21; matrix products, arithmetic and copies ran while one was open for 25% -> 12% of each run, Pallas kernels for 0% -> 28%
where the time goes in v1:
time: 408 us; the launch traced here: 400 us
  Pallas kernels  136 us (33%)
  waiting for transfers between devices  127 us (31%)
  starting transfers between devices  59.1 us (14%)
  local copies, waits for them, and re-layouts  41.7 us (10%)
  other arithmetic  19.8 us (5%)
  between operations  15.2 us (4%)
    ppermute x13, waiting for transfers between devices, swap_tp(): return lax.ppermute(x, 'tp', [(i, i ^ k) for i in range(4)])  84.6 us
    pallas_call x1, Pallas kernels, scan_piece(): pl.pallas_call(functools.partial(scan_back_kernel, dims, first, blocks, s...  44.2 us
    pallas_call x1, Pallas kernels, per_device(): pl.pallas_call(functools.partial(forward_kernel, dims, count, shares), gr...  27.7 us
    ppermute x13, starting transfers between devices, swap_tp(): return lax.ppermute(x, 'tp', [(i, i ^ k) for i in range(4)])  24.6 us
    ppermute x17, waiting for transfers between devices, swap_fsdp(): return lax.ppermute(x, 'fsdp', [(i, i ^ k) for i in range(4)])  23.2 us
    ppermute x17, starting transfers between devices, swap_fsdp(): return lax.ppermute(x, 'fsdp', [(i, i ^ k) for i in range(4)])  21.8 us
    ppermute x7, waiting for transfers between devices, shift_part(): return lax.ppermute(x, ('ctx', 'tp'), pairs)  17.9 us
    pallas_call x1, Pallas kernels, per_device(): pl.pallas_call(functools.partial(gate_back_kernel, dims, shares), grid=(b...  14.4 us
  transfers between devices with their start and end apart: 46, of which 21 were waited for; matrix products, arithmetic and copies ran while one was open for 12% of the time, Pallas kernels for 28%

profile of v1, /device:TPU:0, one launch (start us, length us, event | category | flops | bytes accessed | tf_op | source)
XLA Modules:
  0.0 400.5 jit_solution(10161216967745642398)
XLA Ops:
  10.9 3.0 collective-permute-start.8
  17.6 3.1 collective-permute-start
  20.6 3.2 constant_dynamic-slice_fusion.7.refs_5_.tok_ref
  26.9 6.3 %collective-permute-done = bf16[128,1152]{1,0:T(8,128)(2,1)} collective-permute-done((bf16[128,1152]{1,0:T(8,128)(2,1)S(1)}, bf16[128,1152]{1,0:T(8,128)(2,1)}, u32[]{:S(2)}, u32[]{:S(2)}) %collective-permute-start) | collective-permute-done | bytes 294944 | tf_op jit(solution)/shard_map/ppermute | solution.py:32
  37.6 2.9 collective-permute-start.1
  42.4 3.0 collective-permute-done.1
  45.5 3.3 collective-permute-done.12
  57.2 27.7 %forward.1 = (f32[1024,1024]{1,0:T(8,128)}, bf16[1024,1280]{1,0:T(8,128)(2,1)}, bf16[1024,1280]{1,0:T(8,128)(2,1)}, f32[1024,1024]{1,0:T(8,128)}, f32[1024,128]{...) custom-call(s32[8]{0:T(128)} %broadcast_multiply_fusion.place_ref, ...), custom_call_target="tpu_custom_call" | custom-call | tf_op jit(solution)/shard_map/forward/pallas_call | solution.py:803
  87.7 3.0 collective-permute-start.17
  94.2 3.1 collective-permute-done.18.refs_4_
  98.4 14.4 %stats.1 = (f32[1024,1024]{1,0:T(8,128)}, bf16[4,1024,128]{2,1,0:T(8,128)(2,1)}, f32[1024,1024]{1,0:T(8,128)}, f32[2,1024]{1,0:T(2,128)}, bf16[1024,1024]{1,0:T(8,128)(2,1)}, /*index=5*/bf16[1024,1024]{1,0:T(8,128)(2,1)}) custom-call(s32[8]{0:T(128)} %broadcast_multiply_fusion.place_ref, bf16[4,128,1024]{2,1,0:T(8,128)(2,1)} %copy-done.4, ...), custom_call_target="tpu_custom_call" | custom-call | tf_op jit(solution)/shard_map/stats/pallas_call | solution.py:856
  112.8 10.0 %collective-permute-start.19 = (f32[2,1024]{1,0:T(2,128)}, f32[2,1024]{1,0:T(2,128)S(1)}, u32[]{:S(2)}, u32[]{:S(2)}) collective-permute-start(f32[2,1024]{1,0:T(2,128)} %get-tuple-element.70), channel_id=1, source_target_pairs={{0,1},{1,0},{2,3},{3,2},{4,5},{5,4},{6,7},{7,6},{8,9},{9,8},{10,11... | collective-permute-start | bytes 24584 | tf_op jit(solution)/shard_map/ppermute | solution.py:32
  129.4 14.4 %gate_back.1 = (bf16[1024,1024]{1,0:T(8,128)(2,1)}, bf16[1024,1024]{1,0:T(8,128)(2,1)}, bf16[1024,1024]{1,0:T(8,128)(2,1)}, f32[1024,128]{1,0:T(8,128)}, f32[4,1...) custom-call(s32[4,1,256]{2,1,0:T(1,128)} %bitcast.88, f32[2,1024]{1,0:T(2,128)} %add.175.stats_ref, ...), custom_call_target="tpu_custom_call" | custom-call | flops 1024 | bytes 1024 | tf_op jit(solution)/shard_map/gate_back/pallas_call | solution.py:921
  155.5 3.1 own_branch.1
  158.6 4.2 %collective-permute-done.21.refs_0_ = bf16[1040,128]{1,0:T(8,128)(2,1)S(1)} collective-permute-done((bf16[1040,128]{1,0:T(8,128)(2,1)}, bf16[1040,128]{1,0:T(8,128)(2,1)S(1)}, u32[]{:S(2)}, u32[]{:S(2)}) %collective-permute-start.21) | collective-permute-done | bytes 266272 | tf_op jit(solution)/shard_map/ppermute | solution.py:52
  165.3 10.8 %first_grad.1 = bf16[2,4,128,2048]{3,2,1,0:T(8,128)(2,1)} custom-call(bf16[1024,1024]{1,0:T(8,128)(2,1)} %constant_dynamic-slice_fusion.7.refs_5_.tok_ref, f32[8,1024]{1,0:T(8,128)} %get-tuple-element.79.gain_ref, bf16[1024,1024]{1,0:T(8,128)(2,1)} %get-tuple-element.85.gate_ref.ggate_ref, bf16[1024,1024]{1,0:T(8,128)(2,1)} %constant_dynamic-slice_fusion.6.refs_11_.og_ref, ...), custom_call_target="tpu_custom_call" | custom-call | flops 1024 | bytes 1024 | tf_op jit(solution)/shard_map/first_grad/pallas_call | solution.py:967
  176.1 3.2 dynamic-slice_bitcast_fusion
  181.7 44.2 %scan_back.1 = (bf16[1024,1024]{1,0:T(8,128)(2,1)}, f32[8,1280]{1,0:T(8,128)}, bf16[1024,1408]{1,0:T(8,128)(2,1)}, f32[8,1280]{1,0:T(8,128)}, f32[8,128]{1,0:T(8...) custom-call(s32[4,1,256]{2,1,0:T(1,128)} %bitcast.89, ...), custom_call_target="tpu_custom_call" | custom-call | flops 1024 | bytes 1024 | tf_op jit(solution)/shard_map/scan_back/pallas_call | solution.py:1027
  229.6 6.7 %collective-permute-done.29 = bf16[8,1280]{1,0:T(8,128)(2,1)S(1)} collective-permute-done((bf16[8,1280]{1,0:T(8,128)(2,1)S(1)}, bf16[8,1280]{1,0:T(8,128)(2,1)S(1)}, u32[]{:S(2)}, u32[]{:S(2)}) %collective-permute-start.29) | collective-permute-done | bytes 20512 | tf_op jit(solution)/shard_map/ppermute | solution.py:52
  245.0 20.5 %collective-permute-done.30 = bf16[16,1024]{1,0:T(8,128)(2,1)S(1)} collective-permute-done((bf16[16,1024]{1,0:T(8,128)(2,1)S(1)}, bf16[16,1024]{1,0:T(8,128)(2,1)S(1)}, u32[]{:S(2)}, u32[]{:S(2)}) %collective-permute-start.30) | collective-permute-done | bytes 32800 | tf_op jit(solution)/shard_map/ppermute | solution.py:32
  267.5 3.5 own_rows.1
  274.1 2.9 collective-permute-done.32
  281.5 9.1 %weight_grad.1 = bf16[2,4,128,1408]{3,2,1,0:T(8,128)(2,1)} custom-call(bf16[1024,1024]{1,0:T(8,128)(2,1)} %constant_dynamic-slice_fusion.7.refs_5_.tok_ref, f32[8,1024]{1,0:T(8,128)} %get-tuple-element.79.gain_ref, bf16[1024,1408]{1,0:T(8,128)(2,1)} %get-tuple-element.100.grads_ref, bf16[16,1280]{1,0:T(8,128)(2,1)} %fusion.17.extra_ref, ...), custom_call_target="tpu_custom_call" | custom-call | flops 1024 | bytes 1024 | tf_op jit(solution)/shard_map/weight_grad/pallas_call | solution.py:1123
  290.6 2.7 dynamic-slice_bitcast_fusion.1
  297.3 2.6 collective-permute-start.41
  304.4 3.1 collective-permute-done.43
  314.1 7.3 %collective-permute-done.35 = bf16[128,1408]{1,0:T(8,128)(2,1)S(1)} collective-permute-done((bf16[128,1408]{1,0:T(8,128)(2,1)S(1)}, bf16[128,1408]{1,0:T(8,128)(2,1)S(1)}, u32[]{:S(2)}, u32[]{:S(2)}) %collective-permute-start.35) | collective-permute-done | bytes 360480 | tf_op jit(solution)/shard_map/ppermute | solution.py:28
  321.3 7.4 %collective-permute-done.36 = bf16[128,1408]{1,0:T(8,128)(2,1)S(1)} collective-permute-done((bf16[128,1408]{1,0:T(8,128)(2,1)S(1)}, bf16[128,1408]{1,0:T(8,128)(2,1)S(1)}, u32[]{:S(2)}, u32[]{:S(2)}) %collective-permute-start.36) | collective-permute-done | bytes 360480 | tf_op jit(solution)/shard_map/ppermute | solution.py:28
  330.7 8.6 %collective-permute-done.39 = bf16[128,384]{1,0:T(8,128)(2,1)S(1)} collective-permute-done((bf16[128,384]{1,0:T(8,128)(2,1)S(1)}, bf16[128,384]{1,0:T(8,128)(2,1)S(1)}, u32[]{:S(2)}, u32[]{:S(2)}) %collective-permute-start.39) | collective-permute-done | bytes 98336 | tf_op jit(solution)/shard_map/ppermute | solution.py:32
  340.8 34.9 %collective-permute-done.40 = bf16[128,384]{1,0:T(8,128)(2,1)S(1)} collective-permute-done((bf16[128,384]{1,0:T(8,128)(2,1)S(1)}, bf16[128,384]{1,0:T(8,128)(2,1)S(1)}, u32[]{:S(2)}, u32[]{:S(2)}) %collective-permute-start.40) | collective-permute-done | bytes 98336 | tf_op jit(solution)/shard_map/ppermute | solution.py:32
  379.6 9.0 %tokens_grad.1 = f32[2048,1024]{1,0:T(8,128)} custom-call(bf16[2048,1024]{1,0:T(8,128)(2,1)} %all-gather.5.cloned.1.call-done.a_ref, bf16[2048,1024]{1,0:T(8,128)(2,1)} %b_ref.1), custom_call_target="tpu_custom_call" | custom-call | tf_op jit(solution)/shard_map/tokens_grad/pallas_call | solution.py:1187
  388.6 4.6 %copy.40 = bf16[2048,1024]{1,0:T(8,128)(2,1)} copy(bf16[2048,1024]{1,0:T(8,128)(2,1)} %all-gather.3.cloned.1.call-done) | data formatting | bytes 8388608
  (235 shorter events, 99.2 us)
Async XLA Ops:
  7.2 263.9 %all-gather.3.cloned.1.call-start = ((), (), s32[]{:S(2)}) async-start(), calls=%async_computation | async-start | bytes 5242880 | tf_op jit(solution)/shard_map/all_gather | solution.py:960
  10.9 25.4 %collective-permute-start.8 = (bf16[128,1408]{1,0:T(8,128)(2,1)S(1)}, bf16[128,1408]{1,0:T(8,128)(2,1)S(1)}, u32[]{:S(2)}, u32[]{:S(2)}) collective-permute-start(bf16[128,1408]{1,0:T(8,128)(2,1)S(1)} %get-tuple-element.145), channel_id=1, source_target_pairs={{0,8},{8,0},{16,24},{24,16},{1,9},{9,1},{17,25},{25,17},{2,10},{10... | collective-permute-start | bytes 1081352 | tf_op jit(solution)/shard_map/ppermute | solution.py:28
  13.9 23.6 %collective-permute-start.9 = (bf16[128,1408]{1,0:T(8,128)(2,1)S(1)}, bf16[128,1408]{1,0:T(8,128)(2,1)S(1)}, u32[]{:S(2)}, u32[]{:S(2)}) collective-permute-start(bf16[128,1408]{1,0:T(8,128)(2,1)S(1)} %get-tuple-element.145), channel_id=1, source_target_pairs={{0,16},{8,24},{16,0},{24,8},{1,17},{9,25},{17,1},{25,9},{2,18},{10... | collective-permute-start | bytes 1081352 | tf_op jit(solution)/shard_map/ppermute | solution.py:28
  15.4 22.1 %collective-permute-start.10 = (bf16[128,1408]{1,0:T(8,128)(2,1)S(1)}, bf16[128,1408]{1,0:T(8,128)(2,1)S(1)}, u32[]{:S(2)}, u32[]{:S(2)}) collective-permute-start(bf16[128,1408]{1,0:T(8,128)(2,1)S(1)} %get-tuple-element.145), channel_id=1, source_target_pairs={{0,24},{8,16},{16,8},{24,0},{1,25},{9,17},{17,9},{25,1},{2,26},{10... | collective-permute-start | bytes 1081352 | tf_op jit(solution)/shard_map/ppermute | solution.py:28
  17.6 15.7 %collective-permute-start = (bf16[128,1152]{1,0:T(8,128)(2,1)S(1)}, bf16[128,1152]{1,0:T(8,128)(2,1)}, u32[]{:S(2)}, u32[]{:S(2)}) collective-permute-start(bf16[128,1152]{1,0:T(8,128)(2,1)S(1)} %fusion.9), channel_id=1, source_target_pairs={{0,2},{1,3},{2,0},{3,1},{4,6},{5,7},{6,4},{7,5},{8,10},{9,11},{10,... | collective-permute-start | bytes 884744 | tf_op jit(solution)/shard_map/ppermute | solution.py:32
  33.2 12.2 %collective-permute-start.3 = (bf16[128,1152]{1,0:T(8,128)(2,1)}, bf16[128,1152]{1,0:T(8,128)(2,1)}, u32[]{:S(2)}, u32[]{:S(2)}) collective-permute-start(bf16[128,1152]{1,0:T(8,128)(2,1)} %collective-permute-done), channel_id=1, source_target_pairs={{0,24},{8,16},{16,8},{24,0},{1,25},{9,17},{17,9},{25,1},{2,26},{10... | collective-permute-start | bytes 884744 | tf_op jit(solution)/shard_map/ppermute | solution.py:28
  35.7 13.0 %collective-permute-start.12 = (bf16[128,1152]{1,0:T(8,128)(2,1)}, bf16[128,1152]{1,0:T(8,128)(2,1)}, u32[]{:S(2)}, u32[]{:S(2)}) collective-permute-start(bf16[128,1152]{1,0:T(8,128)(2,1)} %collective-permute-done), channel_id=1, source_target_pairs={{0,8},{8,0},{16,24},{24,16},{1,9},{9,1},{17,25},{25,17},{2,10},{10... | collective-permute-start | bytes 884744 | tf_op jit(solution)/shard_map/ppermute | solution.py:28
  36.3 12.5 %collective-permute-start.13 = (bf16[128,1152]{1,0:T(8,128)(2,1)}, bf16[128,1152]{1,0:T(8,128)(2,1)}, u32[]{:S(2)}, u32[]{:S(2)}) collective-permute-start(bf16[128,1152]{1,0:T(8,128)(2,1)} %collective-permute-done), channel_id=1, source_target_pairs={{0,16},{8,24},{16,0},{24,8},{1,17},{9,25},{17,1},{25,9},{2,18},{10... | collective-permute-start | bytes 884744 | tf_op jit(solution)/shard_map/ppermute | solution.py:28
  42.4 14.8 %collective-permute-start.11 = (bf16[4,128,1408]{2,1,0:T(8,128)(2,1)S(1)}, bf16[4,128,1408]{2,1,0:T(8,128)(2,1)}, u32[]{:S(2)}, u32[]{:S(2)}) collective-permute-start(bf16[4,128,1408]{2,1,0:T(8,128)(2,1)S(1)} %pad_maximum_fusion.refs_0_), channel_id=1, source_target_pairs={{0,4},{4,0},{1,5},{5,1},{2,6},{6,2},{3,7},{7,3},{8,12},{12,8},{9,1... | collective-permute-start | bytes 4325384 | tf_op jit(solution)/shard_map/ppermute | solution.py:24
  51.8 33.2 %collective-permute-start.7 = (bf16[128,1024]{1,0:T(8,128)(2,1)S(1)}, bf16[128,1024]{1,0:T(8,128)(2,1)S(1)}, u32[]{:S(2)}, u32[]{:S(2)}) collective-permute-start(bf16[128,1024]{1,0:T(8,128)(2,1)S(1)} %pad_maximum_fusion.5), channel_id=1, source_target_pairs={{0,24},{8,16},{16,8},{24,0},{1,25},{9,17},{17,9},{25,1},{2,26},{10... | collective-permute-start | bytes 786440 | tf_op jit(solution)/shard_map/ppermute | solution.py:28
  54.2 30.8 %collective-permute-start.5 = (bf16[128,1024]{1,0:T(8,128)(2,1)S(1)}, bf16[128,1024]{1,0:T(8,128)(2,1)}, u32[]{:S(2)}, u32[]{:S(2)}) collective-permute-start(bf16[128,1024]{1,0:T(8,128)(2,1)S(1)} %pad_maximum_fusion.5), channel_id=1, source_target_pairs={{0,8},{8,0},{16,24},{24,16},{1,9},{9,1},{17,25},{25,17},{2,10},{10... | collective-permute-start | bytes 786440 | tf_op jit(solution)/shard_map/ppermute | solution.py:28
  54.7 30.3 %collective-permute-start.6 = (bf16[128,1024]{1,0:T(8,128)(2,1)S(1)}, bf16[128,1024]{1,0:T(8,128)(2,1)}, u32[]{:S(2)}, u32[]{:S(2)}) collective-permute-start(bf16[128,1024]{1,0:T(8,128)(2,1)S(1)} %pad_maximum_fusion.5), channel_id=1, source_target_pairs={{0,16},{8,24},{16,0},{24,8},{1,17},{9,25},{17,1},{25,9},{2,18},{10... | collective-permute-start | bytes 786440 | tf_op jit(solution)/shard_map/ppermute | solution.py:28
  86.2 11.1 %collective-permute-start.15 = (bf16[4,128,1024]{2,1,0:T(8,128)(2,1)S(1)}, bf16[4,128,1024]{2,1,0:T(8,128)(2,1)S(1)}, u32[]{:S(2)}, u32[]{:S(2)}) collective-permute-start(bf16[4,128,1024]{2,1,0:T(8,128)(2,1)S(1)} %pad_maximum_fusion.2.refs_0_), channel_id=1, source_target_pairs={{0,4},{4,0},{1,5},{5,1},{2,6},{6,2},{3,7},{7,3},{8,12},{12,8},{9,1... | collective-permute-start | bytes 3145736 | tf_op jit(solution)/shard_map/ppermute | solution.py:24
  112.8 11.9 %collective-permute-start.19 = (f32[2,1024]{1,0:T(2,128)}, f32[2,1024]{1,0:T(2,128)S(1)}, u32[]{:S(2)}, u32[]{:S(2)}) collective-permute-start(f32[2,1024]{1,0:T(2,128)} %get-tuple-element.70), channel_id=1, source_target_pairs={{0,1},{1,0},{2,3},{3,2},{4,5},{5,4},{6,7},{7,6},{8,9},{9,8},{10,11... | collective-permute-start | bytes 24584 | tf_op jit(solution)/shard_map/ppermute | solution.py:32
  127.3 27.2 %collective-permute-start.20 = (bf16[512,1024]{1,0:T(8,128)(2,1)S(1)}, bf16[512,1024]{1,0:T(8,128)(2,1)S(1)}, u32[]{:S(2)}, u32[]{:S(2)}) collective-permute-start(bf16[512,1024]{1,0:T(8,128)(2,1)S(1)} %constant_dynamic-slice_fusion.4), channel_id=1, source_target_pairs={{0,1},{1,0},{2,3},{3,2},{4,5},{5,4},{6,7},{7,6},{8,9},{9,8},{10,11... | collective-permute-start | bytes 3145736 | tf_op jit(solution)/shard_map/ppermute | solution.py:32
  143.8 19.0 %collective-permute-start.21 = (bf16[1040,128]{1,0:T(8,128)(2,1)}, bf16[1040,128]{1,0:T(8,128)(2,1)S(1)}, u32[]{:S(2)}, u32[]{:S(2)}) collective-permute-start(bf16[1040,128]{1,0:T(8,128)(2,1)} %get-tuple-element.76), channel_id=1, source_target_pairs={{2,0},{3,1},{4,2},{5,3},{6,4},{7,5},{10,8},{11,9},{12,10},{13,11},... | collective-permute-start | bytes 798728 | tf_op jit(solution)/shard_map/ppermute | solution.py:52
  145.2 17.6 %collective-permute-start.22 = (bf16[1040,128]{1,0:T(8,128)(2,1)}, bf16[1040,128]{1,0:T(8,128)(2,1)S(1)}, u32[]{:S(2)}, u32[]{:S(2)}) collective-permute-start(bf16[1040,128]{1,0:T(8,128)(2,1)} %get-tuple-element.76), channel_id=1, source_target_pairs={{4,0},{5,1},{6,2},{7,3},{12,8},{13,9},{14,10},{15,11},{20,16},{21,... | collective-permute-start | bytes 798728 | tf_op jit(solution)/shard_map/ppermute | solution.py:52
  146.5 18.7 %collective-permute-start.23 = (bf16[1040,128]{1,0:T(8,128)(2,1)}, bf16[1040,128]{1,0:T(8,128)(2,1)S(1)}, u32[]{:S(2)}, u32[]{:S(2)}) collective-permute-start(bf16[1040,128]{1,0:T(8,128)(2,1)} %get-tuple-element.76), channel_id=1, source_target_pairs={{6,0},{7,1},{14,8},{15,9},{22,16},{23,17},{30,24},{31,25}} | collective-permute-start | bytes 798728 | tf_op jit(solution)/shard_map/ppermute | solution.py:52
  165.2 214.4 %all-gather.5.cloned.1.call-start = ((), (), s32[]{:S(2)}) async-start(), calls=%async_computation.1 | async-start | bytes 5242880 | tf_op jit(solution)/shard_map/all_gather | solution.py:1096
  179.3 57.0 %collective-permute-start.24 = (bf16[4,128,2048]{2,1,0:T(8,128)(2,1)}, bf16[4,128,2048]{2,1,0:T(8,128)(2,1)S(1)}, u32[]{:S(2)}, u32[]{:S(2)}) collective-permute-start(bf16[4,128,2048]{2,1,0:T(8,128)(2,1)} %dynamic-slice_bitcast_fusion), channel_id=1, source_target_pairs={{0,4},{4,0},{1,5},{5,1},{2,6},{6,2},{3,7},{7,3},{8,12},{12,8},{9,1... | collective-permute-start | bytes 6291464 | tf_op jit(solution)/shard_map/ppermute | solution.py:24
  229.5 38.0 %collective-permute-start.28 = (bf16[512,1024]{1,0:T(8,128)(2,1)S(1)}, bf16[512,1024]{1,0:T(8,128)(2,1)}, u32[]{:S(2)}, u32[]{:S(2)}) collective-permute-start(bf16[512,1024]{1,0:T(8,128)(2,1)S(1)} %constant_dynamic-slice_fusion.1), channel_id=1, source_target_pairs={{0,1},{1,0},{2,3},{3,2},{4,5},{5,4},{6,7},{7,6},{8,9},{9,8},{10,11... | collective-permute-start | bytes 3145736 | tf_op jit(solution)/shard_map/ppermute | solution.py:32
  239.0 27.2 %collective-permute-start.25 = (bf16[128,2048]{1,0:T(8,128)(2,1)S(1)}, bf16[128,2048]{1,0:T(8,128)(2,1)S(1)}, u32[]{:S(2)}, u32[]{:S(2)}) collective-permute-start(bf16[128,2048]{1,0:T(8,128)(2,1)S(1)} %get-tuple-element.133), channel_id=1, source_target_pairs={{0,8},{8,0},{16,24},{24,16},{1,9},{9,1},{17,25},{25,17},{2,10},{10... | collective-permute-start | bytes 1572872 | tf_op jit(solution)/shard_map/ppermute | solution.py:28
  240.4 25.7 %collective-permute-start.26 = (bf16[128,2048]{1,0:T(8,128)(2,1)S(1)}, bf16[128,2048]{1,0:T(8,128)(2,1)S(1)}, u32[]{:S(2)}, u32[]{:S(2)}) collective-permute-start(bf16[128,2048]{1,0:T(8,128)(2,1)S(1)} %get-tuple-element.135), channel_id=1, source_target_pairs={{0,16},{8,24},{16,0},{24,8},{1,17},{9,25},{17,1},{25,9},{2,18},{10... | collective-permute-start | bytes 1572872 | tf_op jit(solution)/shard_map/ppermute | solution.py:28
  241.7 24.5 %collective-permute-start.27 = (bf16[128,2048]{1,0:T(8,128)(2,1)S(1)}, bf16[128,2048]{1,0:T(8,128)(2,1)S(1)}, u32[]{:S(2)}, u32[]{:S(2)}) collective-permute-start(bf16[128,2048]{1,0:T(8,128)(2,1)S(1)} %get-tuple-element.134), channel_id=1, source_target_pairs={{0,24},{8,16},{16,8},{24,0},{1,25},{9,17},{17,9},{25,1},{2,26},{10... | collective-permute-start | bytes 1572872 | tf_op jit(solution)/shard_map/ppermute | solution.py:28
  243.9 21.5 %collective-permute-start.30 = (bf16[16,1024]{1,0:T(8,128)(2,1)S(1)}, bf16[16,1024]{1,0:T(8,128)(2,1)S(1)}, u32[]{:S(2)}, u32[]{:S(2)}) collective-permute-start(bf16[16,1024]{1,0:T(8,128)(2,1)S(1)} %get-tuple-element.156), channel_id=1, source_target_pairs={{0,1},{1,0},{2,3},{3,2},{4,5},{5,4},{6,7},{7,6},{8,9},{9,8},{10,11... | collective-permute-start | bytes 98312 | tf_op jit(solution)/shard_map/ppermute | solution.py:32
  293.3 14.7 %collective-permute-start.34 = (bf16[4,128,1408]{2,1,0:T(8,128)(2,1)}, bf16[4,128,1408]{2,1,0:T(8,128)(2,1)}, u32[]{:S(2)}, u32[]{:S(2)}) collective-permute-start(bf16[4,128,1408]{2,1,0:T(8,128)(2,1)} %dynamic-slice_bitcast_fusion.1), channel_id=1, source_target_pairs={{0,4},{4,0},{1,5},{5,1},{2,6},{6,2},{3,7},{7,3},{8,12},{12,8},{9,1... | collective-permute-start | bytes 4325384 | tf_op jit(solution)/shard_map/ppermute | solution.py:24
  297.3 10.8 %collective-permute-start.41 = (f32[8,640]{1,0:T(8,128)S(1)}, f32[8,640]{1,0:T(8,128)S(1)}, u32[]{:S(2)}, u32[]{:S(2)}) collective-permute-start(f32[8,640]{1,0:T(8,128)S(1)} %select_maximum_fusion.1), channel_id=1, source_target_pairs={{0,2},{1,3},{2,0},{3,1},{4,6},{5,7},{6,4},{7,5},{8,10},{9,11},{10,... | collective-permute-start | bytes 61448 | tf_op jit(solution)/shard_map/ppermute | solution.py:32
  309.9 11.4 %collective-permute-start.35 = (bf16[128,1408]{1,0:T(8,128)(2,1)S(1)}, bf16[128,1408]{1,0:T(8,128)(2,1)S(1)}, u32[]{:S(2)}, u32[]{:S(2)}) collective-permute-start(bf16[128,1408]{1,0:T(8,128)(2,1)S(1)} %get-tuple-element.138), channel_id=1, source_target_pairs={{0,8},{8,0},{16,24},{24,16},{1,9},{9,1},{17,25},{25,17},{2,10},{10... | collective-permute-start | bytes 1081352 | tf_op jit(solution)/shard_map/ppermute | solution.py:28
  311.4 17.3 %collective-permute-start.36 = (bf16[128,1408]{1,0:T(8,128)(2,1)S(1)}, bf16[128,1408]{1,0:T(8,128)(2,1)S(1)}, u32[]{:S(2)}, u32[]{:S(2)}) collective-permute-start(bf16[128,1408]{1,0:T(8,128)(2,1)S(1)} %get-tuple-element.140), channel_id=1, source_target_pairs={{0,16},{8,24},{16,0},{24,8},{1,17},{9,25},{17,1},{25,9},{2,18},{10... | collective-permute-start | bytes 1081352 | tf_op jit(solution)/shard_map/ppermute | solution.py:28
  312.9 15.8 %collective-permute-start.37 = (bf16[128,1408]{1,0:T(8,128)(2,1)S(1)}, bf16[128,1408]{1,0:T(8,128)(2,1)S(1)}, u32[]{:S(2)}, u32[]{:S(2)}) collective-permute-start(bf16[128,1408]{1,0:T(8,128)(2,1)S(1)} %get-tuple-element.139), channel_id=1, source_target_pairs={{0,24},{8,16},{16,8},{24,0},{1,25},{9,17},{17,9},{25,1},{2,26},{10... | collective-permute-start | bytes 1081352 | tf_op jit(solution)/shard_map/ppermute | solution.py:28
  329.3 47.8 %collective-permute-start.38 = (bf16[128,1664]{1,0:T(8,128)(2,1)S(1)}, bf16[128,1664]{1,0:T(8,128)(2,1)S(1)}, u32[]{:S(2)}, u32[]{:S(2)}) collective-permute-start(bf16[128,1664]{1,0:T(8,128)(2,1)S(1)} %concatenate.59), channel_id=1, source_target_pairs={{0,2},{1,3},{2,0},{3,1},{4,6},{5,7},{6,4},{7,5},{8,10},{9,11},{10,... | collective-permute-start | bytes 1277960 | tf_op jit(solution)/shard_map/ppermute | solution.py:32
  339.3 36.4 %collective-permute-start.40 = (bf16[128,384]{1,0:T(8,128)(2,1)S(1)}, bf16[128,384]{1,0:T(8,128)(2,1)S(1)}, u32[]{:S(2)}, u32[]{:S(2)}) collective-permute-start(bf16[128,384]{1,0:T(8,128)(2,1)S(1)} %add_convert_fusion), channel_id=1, source_target_pairs={{0,2},{1,3},{2,0},{3,1},{4,6},{5,7},{6,4},{7,5},{8,10},{9,11},{10,... | collective-permute-start | bytes 294920 | tf_op jit(solution)/shard_map/ppermute | solution.py:32
  (46 other events, 359.6 us)
Sparse Core Ops, SparseCore 0:
  165.3 84.8 all-gather.2
  271.2 104.3 all-gather.4

commit v2 on v1

--- a/solution.py
+++ b/solution.py
@@ -251,8 +251,8 @@
     own_stacks, refs = refs[:count], refs[count:]
     more_stacks, refs = refs[: count * (groups - 1)], refs[count * (groups - 1) :]
     pos_ref, tok_ref, halo_ref, taps_ref, bias_ref, rate_ref, skip_ref = refs[:7]
-    gate_ref, mixed_ref, vkq_ref, ssm_ref, step_ref, decay_ref, enter_ref, last_ref = refs[7:15]
-    edge_ref, gain_ref, w_ref, mx, state, through = refs[15:]
+    mixed_ref, vkq_ref, ssm_ref, step_ref, decay_ref, enter_ref, last_ref = refs[7:14]
+    edge_ref, gain_ref, w_ref, mx, state, through = refs[14:]
     heads, head_size, inner, states = dims
     width = inner + 2 * states
     at_mixed, at_misc = inner, inner + width
@@ -292,7 +292,6 @@
     pos = column(pos_ref[0].astype(f32))
     unit = row_norm(tok_ref[...].astype(f32))[1]
     normed = (unit * gain_ref[0:1, :]).astype(bf16)
-    gate_ref[...] = nn(normed, w_ref[:, :at_mixed])
     mixed = nn(normed, w_ref[:, at_mixed:at_misc]).astype(bf16)
     mixed_ref[...] = mixed
     mx[8 : 8 + STRETCH, :] = mixed.astype(f32)
@@ -340,20 +339,31 @@
         pack_state(last_ref, state[...], through[0:1, :], heads // groups)
 
 
-def stats_kernel(dims, count, groups, hops, place_ref, *refs):
+def gates_kernel(count, place_ref, *refs):
     stacks, refs = refs[:count], refs[count:]
+    tok_ref, gain_ref, w_ref, og_ref, gate_ref, gno_ref, out_ref = refs
+
+    @pl.when(pl.program_id(0) == 0)
+    def _():
+        def write(at, piece):
+            out_ref[at, :] = piece
+
+        place_stacks(place_ref, stacks, write)
+
+    normed = (row_norm(tok_ref[...].astype(f32))[1] * gain_ref[0:1, :]).astype(bf16)
+    gate_ref[...] = nn(normed, w_ref[...])
+    gno_ref[...] = nn(og_ref[...], out_ref[...])
+
+
+def stats_kernel(dims, groups, hops, *refs):
     come_refs, refs = refs[:hops], refs[hops:]
-    pos_ref, ssm_ref, gate_ref, q_ref, decay_ref, enter_ref, og_ref, gain_ref = refs[:8]
-    full_ref, state_ref, gno_ref, stats_ref, branch_ref, out_ref, through, come = refs[8:]
+    pos_ref, ssm_ref, gate_ref, q_ref, decay_ref, enter_ref, gno_ref, out_ref, gain_ref = refs[:9]
+    full_ref, state_ref, stats_ref, branch_ref, through, come = refs[9:]
     heads, head_size, inner, states = dims
     c = pl.program_id(0)
 
     @pl.when(c == 0)
     def _():
-        def write(at, piece):
-            out_ref[at, :] = piece
-
-        place_stacks(place_ref, stacks, write)
         through[...] = jnp.ones_like(through)
         come[...] = join_states(come_refs, head_choice_t(inner, head_size), groups)
 
@@ -371,8 +381,7 @@
     through[...] = through[...] * passing_row(pos, decay)
     gate = gate_ref[...]
     gated = ssm * (gate * jax.nn.sigmoid(gate))
-    gno = nn(og_ref[...], out_ref[...])
-    gno_ref[...] = gno
+    gno = gno_ref[...]
     gain = gain_ref[...] * (pos[:, :1] >= 0.0).astype(f32)
     branch_ref[...] = nt((gated * gain).astype(bf16), out_ref[...]).astype(bf16)
     grad_unit = gno * gain
@@ -666,6 +675,10 @@
     out_ref[...] = (scaling * (grad - unit * mean)).astype(bf16)
 
 
+def copy_kernel(in_ref, out_ref):
+    out_ref[...] = in_ref[...]
+
+
 def add_kernel(a_ref, b_ref, out_ref):
     out_ref[...] = a_ref[...].astype(f32) + b_ref[...].astype(f32)
 
@@ -799,7 +812,7 @@
     )
 
     scalars = pl.BlockSpec(memory_space=pltpu.SMEM)
-    gate, mixed, vkq, ssm_local, step_pre, decay, enter, last_state, edge, model_gain, weight = (
+    mixed, vkq, ssm_local, step_pre, decay, enter, last_state, edge, model_gain, weight = (
         pl.pallas_call(
             functools.partial(forward_kernel, dims, count, shares),
             grid=(blocks,),
@@ -815,7 +828,6 @@
                 fixed((1, inner)),
             ],
             out_specs=[
-                by_rows(inner, ahead),
                 by_rows(width, ahead),
                 by_rows(width, ahead),
                 by_rows(inner, ahead),
@@ -828,7 +840,6 @@
                 fixed((model, columns)),
             ],
             out_shape=[
-                shape(rows, inner),
                 shape(rows, width, dtype=bf16),
                 shape(rows, width, dtype=bf16),
                 shape(rows, inner),
@@ -853,12 +864,26 @@
     )
     out_stacks = gather_stacks(out_near[:-1] + [tied(out_near[-1], last_state)])
     coming = [shift_part(last_state, by) for by in range(1, parts)]
-    ssm, state, grad_out, stats, branch, out_t = pl.pallas_call(
-        functools.partial(stats_kernel, dims, count, shares, parts - 1),
+    gate, grad_out, out_t = pl.pallas_call(
+        functools.partial(gates_kernel, count),
         grid=(blocks,),
         in_specs=[
             scalars,
             *[fixed(a.shape) for a in out_stacks],
+            by_rows(model, ahead),
+            fixed((8, model)),
+            pl.BlockSpec((model, inner), lambda c: (0, 0)),
+            by_rows(model, ahead),
+        ],
+        out_specs=[by_rows(inner, ahead), by_rows(inner, ahead), fixed((model, inner))],
+        out_shape=[shape(rows, inner), shape(rows, inner), shape(model, inner, dtype=bf16)],
+        compiler_params=params,
+        name="gates",
+    )(place, *out_stacks, tokens, model_gain, weight, out_grad)
+    ssm, state, stats, branch = pl.pallas_call(
+        functools.partial(stats_kernel, dims, shares, parts - 1),
+        grid=(blocks,),
+        in_specs=[
             *[fixed((inner + HALO, states))] * (parts - 1),
             pos_spec(ahead),
             by_rows(inner, ahead),
@@ -866,31 +891,26 @@
             by_rows(states, ahead, (inner + states) // states),
             by_rows(LANES, ahead),
             by_block(ahead),
-            by_rows(model, ahead),
+            by_rows(inner, ahead),
+            fixed((model, inner)),
             fixed((1, inner)),
         ],
         out_specs=[
             by_rows(inner, ahead),
             by_block(ahead),
-            by_rows(inner, ahead),
             pl.BlockSpec((2, STRETCH), lambda c: (0, c)),
             by_rows(model, ahead),
-            fixed((model, inner)),
         ],
         out_shape=[
             shape(rows, inner),
             shape(blocks, inner, states, dtype=bf16),
-            shape(rows, inner),
             shape(2, rows),
             shape(rows, model, dtype=bf16),
-            shape(model, inner, dtype=bf16),
         ],
         scratch_shapes=[pltpu.VMEM((8, LANES), f32), pltpu.VMEM((inner, states), f32)],
         compiler_params=params,
         name="stats",
-    )(
-        place, *out_stacks, *coming, pos_rows, ssm_local, gate, vkq, decay, enter, out_grad, gain_row
-    )
+    )(*coming, pos_rows, ssm_local, gate, vkq, decay, enter, grad_out, out_t, gain_row)
     half = rows // 2
     member = lax.axis_index("tp") % 2
 
@@ -957,32 +977,22 @@
     )(pos_rows, stats, ssm, gate, grad_out, vkq, decay, gain_row, skip_row)
     going = [shift_part(last_back, -by) for by in range(1, parts)]
     if shares > 1:
-        mixed_out = lax.all_gather(tied(own_branch, *going), "tp", axis=0, tiled=True)
-        first_total = mixed_out[:8, :LANES]
+        first_gather = lax.all_gather(tied(own_branch, *going), "tp", axis=0, tiled=True)
+        mixed_out = pl.pallas_call(
+            copy_kernel,
+            grid=(all_rows // STRETCH,),
+            in_specs=[by_rows(model, ahead)],
+            out_specs=by_rows(model, ahead),
+            out_shape=shape(all_rows, model, dtype=bf16),
+            compiler_params=params,
+            name="mixed_out",
+        )(first_gather)
+        first_total = first_gather[:8, :LANES]
     near_count, cores = (lax.axis_size("fsdp"), lax.axis_size("ctx")) if small_mesh() else (1, 1)
 
     def grad_shape(cols):
         return (cores, near_count, model // (cores * near_count), cols)
 
-    first_grad = pl.pallas_call(
-        functools.partial(first_grad_kernel, dims, near_count, cores),
-        grid=(blocks,),
-        in_specs=[
-            by_rows(model, ahead),
-            fixed((8, model)),
-            by_rows(inner, ahead),
-            by_rows(model, ahead),
-            by_rows(inner, ahead),
-        ],
-        out_specs=fixed(grad_shape(2 * inner)),
-        out_shape=shape(*grad_shape(2 * inner), dtype=bf16),
-        scratch_shapes=[pltpu.VMEM((model, 2 * inner), f32)],
-        compiler_params=params,
-        cost_estimate=light,
-        name="first_grad",
-    )(tokens, model_gain, grad_gate, out_grad, normed_out)
-    grad_gate = tied(grad_gate, first_grad)
-    first_grad = scatter_rows(first_grad)
     per_halo = STRETCH // HALO
 
     def scan_piece(first, size, going, carried):
@@ -1069,6 +1079,24 @@
     if shares > 1:
         mine, came = halves(partial)
         small = tied(small, mine)
+        normed_out = tied(normed_out, mine)
+    first_grad = pl.pallas_call(
+        functools.partial(first_grad_kernel, dims, near_count, cores),
+        grid=(blocks,),
+        in_specs=[
+            by_rows(model, ahead),
+            fixed((8, model)),
+            by_rows(inner, ahead),
+            by_rows(model, ahead),
+            by_rows(inner, ahead),
+        ],
+        out_specs=fixed(grad_shape(2 * inner)),
+        out_shape=shape(*grad_shape(2 * inner), dtype=bf16),
+        scratch_shapes=[pltpu.VMEM((model, 2 * inner), f32)],
+        compiler_params=params,
+        cost_estimate=light,
+        name="first_grad",
+    )(tokens, model_gain, grad_gate, out_grad, normed_out)
     small = sum_rows_group(small)
     extra = shift_part(returned, -1).astype(bf16)
     if shares > 1:
@@ -1091,7 +1119,7 @@
             compiler_params=params,
             name="own_rows",
         )(tied(mine, first_grad), came, own_tokens, model_gain, tail_sum)
-        grads = tied(grads, own_rows, small, first_total)
+        grads = tied(grads, own_rows, first_total)
         own_rows = tied(own_rows, first_total)
         second_total = lax.all_gather(own_rows, "tp", axis=0, tiled=True)
     else:
@@ -1138,6 +1166,18 @@
         cost_estimate=light,
         name="weight_grad",
     )(tokens, model_gain, grads, extra, norm_sums, tail_part)
+    first_grad = scatter_rows(first_grad)
+    if shares > 1:
+        second_total = tied(second_total, mixed_out[:8, :LANES])
+        tokens_grad = pl.pallas_call(
+            add_kernel,
+            grid=(all_rows // STRETCH,),
+            in_specs=[by_rows(model, ahead)] * 2,
+            out_specs=by_rows(model, ahead),
+            out_shape=shape(all_rows, model),
+            compiler_params=params,
+            name="tokens_grad",
+        )(second_total, all_grad)
     late_grad = scatter_rows(weight_grad)
     at = 8 * width // LANES
     tap_total = small[:at].reshape(8, width)
@@ -1172,7 +1212,8 @@
         ]
         channel_total = channel_total + few[: CONV + 3, :own_inner]
         head_total = head_total[:, :own_heads] + few[:2, own_inner : own_inner + own_heads]
-        shared = pair.astype(f32) + swap_tp(pair, 2).astype(f32)
+        pair_more = tied(swap_tp(pair, 2), tokens_grad[:8, :LANES])
+        shared = pair.astype(f32) + pair_more.astype(f32)
         state_taps_grad = taps_pair + swap_tp(taps_pair, 2)
     else:
         shared = sum_tp_small(shared)
@@ -1182,17 +1223,6 @@
     norm_gain_grad = shared[:, 2 * states + heads]
     inner_weight_grad = jnp.stack(groups[:2])
     out_weight_grad = groups[2].T
-    if shares > 1:
-        second_total = tied(second_total, inner_weight_grad, out_weight_grad)
-        tokens_grad = pl.pallas_call(
-            add_kernel,
-            grid=(all_rows // STRETCH,),
-            in_specs=[by_rows(model, ahead)] * 2,
-            out_specs=by_rows(model, ahead),
-            out_shape=shape(all_rows, model),
-            compiler_params=params,
-            name="tokens_grad",
-        )(second_total, all_grad)
     return (
         mixed_out,
         tokens_grad,

time: 408 us -> 399 us (0.978)
  waiting for transfers between devices: 127 us -> 85.9 us
  starting transfers between devices: 59.1 us -> 88.4 us
  Pallas kernels: 136 us -> 147 us
  local copies, waits for them, and re-layouts: 41.7 us -> 33.7 us
    ppermute x13, waiting for transfers between devices: 84.6 us -> 37.9 us  [swap_tp(): return lax.ppermute(x, 'tp', [(i, i ^ k) for i in range(4)])]
    ppermute x13, starting transfers between devices: 24.6 us -> 50.7 us  [swap_tp(): return lax.ppermute(x, 'tp', [(i, i ^ k) for i in range(4)])]
    ppermute x17, waiting for transfers between devices: 23.2 us -> 40.9 us  [swap_fsdp(): return lax.ppermute(x, 'fsdp', [(i, i ^ k) for i in range(4)])]
    pallas_call x1 -> x3, Pallas kernels: 14.4 us -> 28.9 us  [the longest x1 12.1 us: per_device(): pl.pallas_call(functools.partial(stats_kernel, dims, shares, parts - 1),...]
    ppermute x7, waiting for transfers between devices: 17.9 us -> 5.95 us  [shift_part(): return lax.ppermute(x, ('ctx', 'tp'), pairs)]
    unnamed x69 -> x62, local copies, waits for them, and re-layouts: 9.26 us -> 5.34 us
  transfers between devices with their start and end apart: 46 -> 46, of which waited for: 21 -> 19; matrix products, arithmetic and copies ran while one was open for 12% -> 11% of each run, Pallas kernels for 28% -> 32%
where the time goes in v2:
time: 399 us; the launch traced here: 392 us
  Pallas kernels  147 us (37%)
  starting transfers between devices  88.4 us (22%)
  waiting for transfers between devices  85.9 us (22%)
  local copies, waits for them, and re-layouts  33.7 us (8%)
  other arithmetic  17.6 us (4%)
  between operations  15.3 us (4%)
    ppermute x13, starting transfers between devices, swap_tp(): return lax.ppermute(x, 'tp', [(i, i ^ k) for i in range(4)])  50.7 us
    pallas_call x1, Pallas kernels, scan_piece(): pl.pallas_call(functools.partial(scan_back_kernel, dims, first, blocks, s...  44.2 us
    ppermute x17, waiting for transfers between devices, swap_fsdp(): return lax.ppermute(x, 'fsdp', [(i, i ^ k) for i in range(4)])  40.9 us
    ppermute x13, waiting for transfers between devices, swap_tp(): return lax.ppermute(x, 'tp', [(i, i ^ k) for i in range(4)])  37.9 us
    pallas_call x1, Pallas kernels, per_device(): pl.pallas_call(functools.partial(forward_kernel, dims, count, shares), gr...  25.2 us
    ppermute x17, starting transfers between devices, swap_fsdp(): return lax.ppermute(x, 'fsdp', [(i, i ^ k) for i in range(4)])  24 us
    pallas_call x1, Pallas kernels, per_device(): pl.pallas_call(functools.partial(gate_back_kernel, dims, shares), grid=(b...  14.3 us
    pallas_call x1, Pallas kernels, per_device(): pl.pallas_call(functools.partial(stats_kernel, dims, shares, parts - 1),...  12.1 us
  transfers between devices with their start and end apart: 46, of which 19 were waited for; matrix products, arithmetic and copies ran while one was open for 11% of the time, Pallas kernels for 32%

profile of v2, /device:TPU:0, one launch (start us, length us, event | category | flops | bytes accessed | tf_op | source)
XLA Modules:
  0.0 391.6 jit_solution(3520524797751239281)
XLA Ops:
  10.9 3.0 collective-permute-start
  17.6 3.1 collective-permute-start.4
  20.6 3.2 constant_dynamic-slice_fusion.7.refs_5_.refs_2_.tok_ref
  26.9 6.3 %collective-permute-done.4 = bf16[128,1152]{1,0:T(8,128)(2,1)} collective-permute-done((bf16[128,1152]{1,0:T(8,128)(2,1)S(1)}, bf16[128,1152]{1,0:T(8,128)(2,1)}, u32[]{:S(2)}, u32[]{:S(2)}) %collective-permute-start.4) | collective-permute-done | bytes 294944 | tf_op jit(solution)/shard_map/ppermute | solution.py:32
  42.4 3.0 collective-permute-done.9
  45.5 3.3 collective-permute-done.6
  57.2 25.2 %forward.1 = (bf16[1024,1280]{1,0:T(8,128)(2,1)}, bf16[1024,1280]{1,0:T(8,128)(2,1)}, f32[1024,1024]{1,0:T(8,128)}, f32[1024,128]{1,0:T(8,128)}, f32[1024,128]{1...) custom-call(s32[8]{0:T(128)} %broadcast_multiply_fusion.place_ref, ...), custom_call_target="tpu_custom_call" | custom-call | tf_op jit(solution)/shard_map/forward/pallas_call | solution.py:816
  85.2 3.0 collective-permute-start.13
  91.2 10.2 %gates.1 = (f32[1024,1024]{1,0:T(8,128)}, f32[1024,1024]{1,0:T(8,128)}, bf16[1024,1024]{1,0:T(8,128)(2,1)}) custom-call(s32[8]{0:T(128)} %broadcast_multiply_fusion.place_ref, bf16[4,128,1024]{2,1,0:T(8,128)(2,1)} %copy-done.4, bf16[4,128,1024]{2,1,0:T(8,128)(2,1)} %copy-done.8, bf16[1024,1024]{1,0:T(8,128)(2,1)} %constant_dynamic-slice_fusion.7.refs_5_.refs_2_.tok_ref, ...), custom_call_target="tpu_custom_call" | custom-call | tf_op jit(solution)/shard_map/gates/pallas_call | solution.py:867
  102.3 12.1 %stats.1 = (f32[1024,1024]{1,0:T(8,128)}, bf16[4,1024,128]{2,1,0:T(8,128)(2,1)}, f32[2,1024]{1,0:T(2,128)}, bf16[1024,1024]{1,0:T(8,128)(2,1)}) custom-call(bf16[1040,128]{1,0:T(8,128)(2,1)} %copy-done.9, bf16[1040,128]{1,0:T(8,128)(2,1)} %copy-done.10, bf16[1040,128]{1,0:T(8,128)(2,1)} %copy-done.11, s32[4,1,256]{2,1,0:T(1,128)} %bitcast.85, ...), custom_call_target="tpu_custom_call" | custom-call | tf_op jit(solution)/shard_map/stats/pallas_call | solution.py:883
  114.5 4.9 %collective-permute-start.19 = (f32[2,1024]{1,0:T(2,128)}, f32[2,1024]{1,0:T(2,128)S(1)}, u32[]{:S(2)}, u32[]{:S(2)}) collective-permute-start(f32[2,1024]{1,0:T(2,128)} %get-tuple-element.74), channel_id=1, source_target_pairs={{0,1},{1,0},{2,3},{3,2},{4,5},{5,4},{6,7},{7,6},{8,9},{9,8},{10,11... | collective-permute-start | bytes 24584 | tf_op jit(solution)/shard_map/ppermute | solution.py:32
  125.9 14.3 %gate_back.1 = (bf16[1024,1024]{1,0:T(8,128)(2,1)}, bf16[1024,1024]{1,0:T(8,128)(2,1)}, bf16[1024,1024]{1,0:T(8,128)(2,1)}, f32[1024,128]{1,0:T(8,128)}, f32[4,1...) custom-call(s32[4,1,256]{2,1,0:T(1,128)} %bitcast.86, f32[2,1024]{1,0:T(2,128)} %add.175.stats_ref, ...), custom_call_target="tpu_custom_call" | custom-call | flops 1024 | bytes 1024 | tf_op jit(solution)/shard_map/gate_back/pallas_call | solution.py:941
  152.2 3.0 own_branch.1
  155.3 4.3 %collective-permute-done.21.refs_0_ = bf16[1040,128]{1,0:T(8,128)(2,1)S(1)} collective-permute-done((bf16[1040,128]{1,0:T(8,128)(2,1)}, bf16[1040,128]{1,0:T(8,128)(2,1)S(1)}, u32[]{:S(2)}, u32[]{:S(2)}) %collective-permute-start.21) | collective-permute-done | bytes 266272 | tf_op jit(solution)/shard_map/ppermute | solution.py:52
  163.9 44.2 %scan_back.1 = (bf16[1024,1024]{1,0:T(8,128)(2,1)}, f32[8,1280]{1,0:T(8,128)}, bf16[1024,1408]{1,0:T(8,128)(2,1)}, f32[8,1280]{1,0:T(8,128)}, f32[8,128]{1,0:T(8...) custom-call(s32[4,1,256]{2,1,0:T(1,128)} %bitcast.87, ...), custom_call_target="tpu_custom_call" | custom-call | flops 1024 | bytes 1024 | tf_op jit(solution)/shard_map/scan_back/pallas_call | solution.py:1037
  213.1 10.5 %first_grad.1 = bf16[2,4,128,2048]{3,2,1,0:T(8,128)(2,1)} custom-call(bf16[1024,1024]{1,0:T(8,128)(2,1)} %constant_dynamic-slice_fusion.7.refs_5_.refs_2_.tok_ref, f32[8,1024]{1,0:T(8,128)} %get-tuple-element.66.refs_3_.gain_ref, bf16[1024,1024]{1,0:T(8,128)(2,1)} %get-tuple-element.84.ggate_ref.gate_ref, ...), custom_call_target="tpu_custom_call" | custom-call | flops 1024 | bytes 1024 | tf_op jit(solution)/shard_map/first_grad/pallas_call | solution.py:1083
  223.6 3.2 fusion.29
  226.7 33.2 %collective-permute-start.26 = (bf16[16,1024]{1,0:T(8,128)(2,1)S(1)}, bf16[16,1024]{1,0:T(8,128)(2,1)S(1)}, u32[]{:S(2)}, u32[]{:S(2)}) collective-permute-start(bf16[16,1024]{1,0:T(8,128)(2,1)S(1)} %get-tuple-element.156), channel_id=1, source_target_pairs={{0,1},{1,0},{2,3},{3,2},{4,5},{5,4},{6,7},{7,6},{8,9},{9,8},{10,11... | collective-permute-start | bytes 98312 | tf_op jit(solution)/shard_map/ppermute | solution.py:32
  259.9 3.2 dynamic-slice_bitcast_fusion
  264.0 3.3 own_rows.1
  270.3 3.0 collective-permute-done.39
  278.4 4.2 %collective-permute-done.42 = f32[5,256]{1,0:T(8,128)S(1)} collective-permute-done((f32[5,256]{1,0:T(8,128)S(1)}, f32[5,256]{1,0:T(8,128)S(1)}, u32[]{:S(2)}, u32[]{:S(2)}) %collective-permute-start.42) | collective-permute-done | bytes 5152 | tf_op jit(solution)/shard_map/ppermute | solution.py:32
  282.6 2.9 collective-permute-start.41
  288.4 9.0 %weight_grad.1 = bf16[2,4,128,1408]{3,2,1,0:T(8,128)(2,1)} custom-call(bf16[1024,1024]{1,0:T(8,128)(2,1)} %constant_dynamic-slice_fusion.7.refs_5_.refs_2_.tok_ref, f32[8,1024]{1,0:T(8,128)} %get-tuple-element.66.refs_3_.gain_ref, bf16[1024,1408]{1,0:T(8,128)(2,1)} %get-tuple-element.97.grads_ref, bf16[16,1280]{1,0:T(8,128)(2,1)} %fusion.17.extra_ref, ...), custom_call_target="tpu_custom_call" | custom-call | flops 1024 | bytes 1024 | tf_op jit(solution)/shard_map/weight_grad/pallas_call | solution.py:1151
  309.5 7.5 %collective-permute-done.34 = bf16[128,2048]{1,0:T(8,128)(2,1)S(1)} collective-permute-done((bf16[128,2048]{1,0:T(8,128)(2,1)S(1)}, bf16[128,2048]{1,0:T(8,128)(2,1)S(1)}, u32[]{:S(2)}, u32[]{:S(2)}) %collective-permute-start.34) | collective-permute-done | bytes 524320 | tf_op jit(solution)/shard_map/ppermute | solution.py:28
  319.7 10.4 %collective-permute-done.35 = bf16[128,2048]{1,0:T(8,128)(2,1)S(1)} collective-permute-done((bf16[128,2048]{1,0:T(8,128)(2,1)S(1)}, bf16[128,2048]{1,0:T(8,128)(2,1)S(1)}, u32[]{:S(2)}, u32[]{:S(2)}) %collective-permute-start.35) | collective-permute-done | bytes 524320 | tf_op jit(solution)/shard_map/ppermute | solution.py:28
  330.4 5.7 %collective-permute-done.28 = bf16[128,1408]{1,0:T(8,128)(2,1)S(1)} collective-permute-done((bf16[128,1408]{1,0:T(8,128)(2,1)S(1)}, bf16[128,1408]{1,0:T(8,128)(2,1)S(1)}, u32[]{:S(2)}, u32[]{:S(2)}) %collective-permute-start.28) | collective-permute-done | bytes 360480 | tf_op jit(solution)/shard_map/ppermute | solution.py:28
  336.0 8.6 %collective-permute-done.29 = bf16[128,1408]{1,0:T(8,128)(2,1)S(1)} collective-permute-done((bf16[128,1408]{1,0:T(8,128)(2,1)S(1)}, bf16[128,1408]{1,0:T(8,128)(2,1)S(1)}, u32[]{:S(2)}, u32[]{:S(2)}) %collective-permute-start.29) | collective-permute-done | bytes 360480 | tf_op jit(solution)/shard_map/ppermute | solution.py:28
  346.8 4.7 %collective-permute-done.31 = bf16[128,384]{1,0:T(8,128)(2,1)} collective-permute-done((bf16[128,384]{1,0:T(8,128)(2,1)}, bf16[128,384]{1,0:T(8,128)(2,1)}, u32[]{:S(2)}, u32[]{:S(2)}) %collective-permute-start.31) | collective-permute-done | bytes 98336 | tf_op jit(solution)/shard_map/ppermute | solution.py:32
  353.7 6.6 %mixed_out.1 = bf16[2048,1024]{1,0:T(8,128)(2,1)} custom-call(bf16[2048,1024]{1,0:T(8,128)(2,1)} %all-gather.3.cloned.1.call-done.in_ref), custom_call_target="tpu_custom_call" | custom-call | tf_op jit(solution)/shard_map/mixed_out/pallas_call | solution.py:981
  360.2 11.2 %collective-permute-done.32 = bf16[128,384]{1,0:T(8,128)(2,1)S(1)} collective-permute-done((bf16[128,384]{1,0:T(8,128)(2,1)S(1)}, bf16[128,384]{1,0:T(8,128)(2,1)S(1)}, u32[]{:S(2)}, u32[]{:S(2)}) %collective-permute-start.32) | collective-permute-done | bytes 98336 | tf_op jit(solution)/shard_map/ppermute | solution.py:32
  375.3 9.0 %tokens_grad.1 = f32[2048,1024]{1,0:T(8,128)} custom-call(bf16[2048,1024]{1,0:T(8,128)(2,1)} %all-gather.5.cloned.1.call-done.a_ref, bf16[2048,1024]{1,0:T(8,128)(2,1)} %b_ref.1), custom_call_target="tpu_custom_call" | custom-call | tf_op jit(solution)/shard_map/tokens_grad/pallas_call | solution.py:1172
  (229 shorter events, 97.0 us)
Async XLA Ops:
  7.2 260.2 %all-gather.3.cloned.1.call-start = ((), (), s32[]{:S(2)}) async-start(), calls=%async_computation | async-start | bytes 5242880 | tf_op jit(solution)/shard_map/all_gather | solution.py:980
  10.9 25.4 %collective-permute-start = (bf16[128,1408]{1,0:T(8,128)(2,1)S(1)}, bf16[128,1408]{1,0:T(8,128)(2,1)S(1)}, u32[]{:S(2)}, u32[]{:S(2)}) collective-permute-start(bf16[128,1408]{1,0:T(8,128)(2,1)S(1)} %get-tuple-element.145), channel_id=1, source_target_pairs={{0,8},{8,0},{16,24},{24,16},{1,9},{9,1},{17,25},{25,17},{2,10},{10... | collective-permute-start | bytes 1081352 | tf_op jit(solution)/shard_map/ppermute | solution.py:28
  13.9 23.6 %collective-permute-start.1 = (bf16[128,1408]{1,0:T(8,128)(2,1)S(1)}, bf16[128,1408]{1,0:T(8,128)(2,1)S(1)}, u32[]{:S(2)}, u32[]{:S(2)}) collective-permute-start(bf16[128,1408]{1,0:T(8,128)(2,1)S(1)} %get-tuple-element.145), channel_id=1, source_target_pairs={{0,16},{8,24},{16,0},{24,8},{1,17},{9,25},{17,1},{25,9},{2,18},{10... | collective-permute-start | bytes 1081352 | tf_op jit(solution)/shard_map/ppermute | solution.py:28
  15.4 22.1 %collective-permute-start.2 = (bf16[128,1408]{1,0:T(8,128)(2,1)S(1)}, bf16[128,1408]{1,0:T(8,128)(2,1)S(1)}, u32[]{:S(2)}, u32[]{:S(2)}) collective-permute-start(bf16[128,1408]{1,0:T(8,128)(2,1)S(1)} %get-tuple-element.145), channel_id=1, source_target_pairs={{0,24},{8,16},{16,8},{24,0},{1,25},{9,17},{17,9},{25,1},{2,26},{10... | collective-permute-start | bytes 1081352 | tf_op jit(solution)/shard_map/ppermute | solution.py:28
  17.6 15.7 %collective-permute-start.4 = (bf16[128,1152]{1,0:T(8,128)(2,1)S(1)}, bf16[128,1152]{1,0:T(8,128)(2,1)}, u32[]{:S(2)}, u32[]{:S(2)}) collective-permute-start(bf16[128,1152]{1,0:T(8,128)(2,1)S(1)} %fusion.9), channel_id=1, source_target_pairs={{0,2},{1,3},{2,0},{3,1},{4,6},{5,7},{6,4},{7,5},{8,10},{9,11},{10,... | collective-permute-start | bytes 884744 | tf_op jit(solution)/shard_map/ppermute | solution.py:32
  35.7 13.0 %collective-permute-start.6 = (bf16[128,1152]{1,0:T(8,128)(2,1)}, bf16[128,1152]{1,0:T(8,128)(2,1)}, u32[]{:S(2)}, u32[]{:S(2)}) collective-permute-start(bf16[128,1152]{1,0:T(8,128)(2,1)} %collective-permute-done.4), channel_id=1, source_target_pairs={{0,8},{8,0},{16,24},{24,16},{1,9},{9,1},{17,25},{25,17},{2,10},{10... | collective-permute-start | bytes 884744 | tf_op jit(solution)/shard_map/ppermute | solution.py:28
  36.3 12.5 %collective-permute-start.7 = (bf16[128,1152]{1,0:T(8,128)(2,1)}, bf16[128,1152]{1,0:T(8,128)(2,1)}, u32[]{:S(2)}, u32[]{:S(2)}) collective-permute-start(bf16[128,1152]{1,0:T(8,128)(2,1)} %collective-permute-done.4), channel_id=1, source_target_pairs={{0,16},{8,24},{16,0},{24,8},{1,17},{9,25},{17,1},{25,9},{2,18},{10... | collective-permute-start | bytes 884744 | tf_op jit(solution)/shard_map/ppermute | solution.py:28
  42.4 14.8 %collective-permute-start.3 = (bf16[4,128,1408]{2,1,0:T(8,128)(2,1)S(1)}, bf16[4,128,1408]{2,1,0:T(8,128)(2,1)}, u32[]{:S(2)}, u32[]{:S(2)}) collective-permute-start(bf16[4,128,1408]{2,1,0:T(8,128)(2,1)S(1)} %pad_maximum_fusion.refs_0_), channel_id=1, source_target_pairs={{0,4},{4,0},{1,5},{5,1},{2,6},{6,2},{3,7},{7,3},{8,12},{12,8},{9,1... | collective-permute-start | bytes 4325384 | tf_op jit(solution)/shard_map/ppermute | solution.py:24
  51.7 30.7 %collective-permute-start.17 = (bf16[128,1024]{1,0:T(8,128)(2,1)S(1)}, bf16[128,1024]{1,0:T(8,128)(2,1)S(1)}, u32[]{:S(2)}, u32[]{:S(2)}) collective-permute-start(bf16[128,1024]{1,0:T(8,128)(2,1)S(1)} %pad_maximum_fusion.5), channel_id=1, source_target_pairs={{0,24},{8,16},{16,8},{24,0},{1,25},{9,17},{17,9},{25,1},{2,26},{10... | collective-permute-start | bytes 786440 | tf_op jit(solution)/shard_map/ppermute | solution.py:28
  54.2 28.3 %collective-permute-start.15 = (bf16[128,1024]{1,0:T(8,128)(2,1)S(1)}, bf16[128,1024]{1,0:T(8,128)(2,1)}, u32[]{:S(2)}, u32[]{:S(2)}) collective-permute-start(bf16[128,1024]{1,0:T(8,128)(2,1)S(1)} %pad_maximum_fusion.5), channel_id=1, source_target_pairs={{0,8},{8,0},{16,24},{24,16},{1,9},{9,1},{17,25},{25,17},{2,10},{10... | collective-permute-start | bytes 786440 | tf_op jit(solution)/shard_map/ppermute | solution.py:28
  54.7 27.8 %collective-permute-start.16 = (bf16[128,1024]{1,0:T(8,128)(2,1)S(1)}, bf16[128,1024]{1,0:T(8,128)(2,1)}, u32[]{:S(2)}, u32[]{:S(2)}) collective-permute-start(bf16[128,1024]{1,0:T(8,128)(2,1)S(1)} %pad_maximum_fusion.5), channel_id=1, source_target_pairs={{0,16},{8,24},{16,0},{24,8},{1,17},{9,25},{17,1},{25,9},{2,18},{10... | collective-permute-start | bytes 786440 | tf_op jit(solution)/shard_map/ppermute | solution.py:28
  83.8 17.6 %collective-permute-start.12 = (bf16[1040,128]{1,0:T(8,128)(2,1)S(1)}, bf16[1040,128]{1,0:T(8,128)(2,1)S(1)}, u32[]{:S(2)}, u32[]{:S(2)}) collective-permute-start(bf16[1040,128]{1,0:T(8,128)(2,1)S(1)} %copy-done.28), channel_id=1, source_target_pairs={{0,2},{1,3},{2,4},{3,5},{4,6},{5,7},{8,10},{9,11},{10,12},{11,13},... | collective-permute-start | bytes 798728 | tf_op jit(solution)/shard_map/ppermute | solution.py:52
  85.2 16.3 %collective-permute-start.13 = (bf16[1040,128]{1,0:T(8,128)(2,1)S(1)}, bf16[1040,128]{1,0:T(8,128)(2,1)S(1)}, u32[]{:S(2)}, u32[]{:S(2)}) collective-permute-start(bf16[1040,128]{1,0:T(8,128)(2,1)S(1)} %copy-done.28), channel_id=1, source_target_pairs={{0,4},{1,5},{2,6},{3,7},{8,12},{9,13},{10,14},{11,15},{16,20},{17,... | collective-permute-start | bytes 798728 | tf_op jit(solution)/shard_map/ppermute | solution.py:52
  88.1 13.3 %collective-permute-start.14 = (bf16[1040,128]{1,0:T(8,128)(2,1)S(1)}, bf16[1040,128]{1,0:T(8,128)(2,1)S(1)}, u32[]{:S(2)}, u32[]{:S(2)}) collective-permute-start(bf16[1040,128]{1,0:T(8,128)(2,1)S(1)} %copy-done.28), channel_id=1, source_target_pairs={{0,6},{1,7},{8,14},{9,15},{16,22},{17,23},{24,30},{25,31}} | collective-permute-start | bytes 798728 | tf_op jit(solution)/shard_map/ppermute | solution.py:52
  123.8 27.4 %collective-permute-start.20 = (bf16[512,1024]{1,0:T(8,128)(2,1)S(1)}, bf16[512,1024]{1,0:T(8,128)(2,1)S(1)}, u32[]{:S(2)}, u32[]{:S(2)}) collective-permute-start(bf16[512,1024]{1,0:T(8,128)(2,1)S(1)} %constant_dynamic-slice_fusion.4), channel_id=1, source_target_pairs={{0,1},{1,0},{2,3},{3,2},{4,5},{5,4},{6,7},{7,6},{8,9},{9,8},{10,11... | collective-permute-start | bytes 3145736 | tf_op jit(solution)/shard_map/ppermute | solution.py:32
  140.2 19.3 %collective-permute-start.21 = (bf16[1040,128]{1,0:T(8,128)(2,1)}, bf16[1040,128]{1,0:T(8,128)(2,1)S(1)}, u32[]{:S(2)}, u32[]{:S(2)}) collective-permute-start(bf16[1040,128]{1,0:T(8,128)(2,1)} %get-tuple-element.79), channel_id=1, source_target_pairs={{2,0},{3,1},{4,2},{5,3},{6,4},{7,5},{10,8},{11,9},{12,10},{13,11},... | collective-permute-start | bytes 798728 | tf_op jit(solution)/shard_map/ppermute | solution.py:52
  141.7 17.9 %collective-permute-start.22 = (bf16[1040,128]{1,0:T(8,128)(2,1)}, bf16[1040,128]{1,0:T(8,128)(2,1)S(1)}, u32[]{:S(2)}, u32[]{:S(2)}) collective-permute-start(bf16[1040,128]{1,0:T(8,128)(2,1)} %get-tuple-element.79), channel_id=1, source_target_pairs={{4,0},{5,1},{6,2},{7,3},{12,8},{13,9},{14,10},{15,11},{20,16},{21,... | collective-permute-start | bytes 798728 | tf_op jit(solution)/shard_map/ppermute | solution.py:52
  143.0 18.2 %collective-permute-start.23 = (bf16[1040,128]{1,0:T(8,128)(2,1)}, bf16[1040,128]{1,0:T(8,128)(2,1)S(1)}, u32[]{:S(2)}, u32[]{:S(2)}) collective-permute-start(bf16[1040,128]{1,0:T(8,128)(2,1)} %get-tuple-element.79), channel_id=1, source_target_pairs={{6,0},{7,1},{14,8},{15,9},{22,16},{23,17},{30,24},{31,25}} | collective-permute-start | bytes 798728 | tf_op jit(solution)/shard_map/ppermute | solution.py:52
  161.2 214.1 %all-gather.5.cloned.1.call-start = ((), (), s32[]{:S(2)}) async-start(), calls=%async_computation.1 | async-start | bytes 5242880 | tf_op jit(solution)/shard_map/all_gather | solution.py:1124
  209.6 54.4 %collective-permute-start.24 = (bf16[512,1024]{1,0:T(8,128)(2,1)S(1)}, bf16[512,1024]{1,0:T(8,128)(2,1)}, u32[]{:S(2)}, u32[]{:S(2)}) collective-permute-start(bf16[512,1024]{1,0:T(8,128)(2,1)S(1)} %constant_dynamic-slice_fusion.1), channel_id=1, source_target_pairs={{0,1},{1,0},{2,3},{3,2},{4,5},{5,4},{6,7},{7,6},{8,9},{9,8},{10,11... | collective-permute-start | bytes 3145736 | tf_op jit(solution)/shard_map/ppermute | solution.py:32
  210.4 13.1 %collective-permute-start.25 = (bf16[8,1280]{1,0:T(8,128)(2,1)S(1)}, bf16[8,1280]{1,0:T(8,128)(2,1)S(1)}, u32[]{:S(2)}, u32[]{:S(2)}) collective-permute-start(bf16[8,1280]{1,0:T(8,128)(2,1)S(1)} %convert.41), channel_id=1, source_target_pairs={{2,0},{3,1},{4,2},{5,3},{6,4},{7,5},{10,8},{11,9},{12,10},{13,11},... | collective-permute-start | bytes 61448 | tf_op jit(solution)/shard_map/ppermute | solution.py:52
  226.7 36.6 %collective-permute-start.26 = (bf16[16,1024]{1,0:T(8,128)(2,1)S(1)}, bf16[16,1024]{1,0:T(8,128)(2,1)S(1)}, u32[]{:S(2)}, u32[]{:S(2)}) collective-permute-start(bf16[16,1024]{1,0:T(8,128)(2,1)S(1)} %get-tuple-element.156), channel_id=1, source_target_pairs={{0,1},{1,0},{2,3},{3,2},{4,5},{5,4},{6,7},{7,6},{8,9},{9,8},{10,11... | collective-permute-start | bytes 98312 | tf_op jit(solution)/shard_map/ppermute | solution.py:32
  263.1 36.6 %collective-permute-start.33 = (bf16[4,128,2048]{2,1,0:T(8,128)(2,1)}, bf16[4,128,2048]{2,1,0:T(8,128)(2,1)S(1)}, u32[]{:S(2)}, u32[]{:S(2)}) collective-permute-start(bf16[4,128,2048]{2,1,0:T(8,128)(2,1)} %dynamic-slice_bitcast_fusion), channel_id=1, source_target_pairs={{0,4},{4,0},{1,5},{5,1},{2,6},{6,2},{3,7},{7,3},{8,12},{12,8},{9,1... | collective-permute-start | bytes 6291464 | tf_op jit(solution)/shard_map/ppermute | solution.py:24
  282.6 16.4 %collective-permute-start.41 = (f32[8,640]{1,0:T(8,128)S(1)}, f32[8,640]{1,0:T(8,128)S(1)}, u32[]{:S(2)}, u32[]{:S(2)}) collective-permute-start(f32[8,640]{1,0:T(8,128)S(1)} %select_maximum_fusion.1), channel_id=1, source_target_pairs={{0,2},{1,3},{2,0},{3,1},{4,6},{5,7},{6,4},{7,5},{8,10},{9,11},{10,... | collective-permute-start | bytes 61448 | tf_op jit(solution)/shard_map/ppermute | solution.py:32
  302.2 14.8 %collective-permute-start.34 = (bf16[128,2048]{1,0:T(8,128)(2,1)S(1)}, bf16[128,2048]{1,0:T(8,128)(2,1)S(1)}, u32[]{:S(2)}, u32[]{:S(2)}) collective-permute-start(bf16[128,2048]{1,0:T(8,128)(2,1)S(1)} %get-tuple-element.133), channel_id=1, source_target_pairs={{0,8},{8,0},{16,24},{24,16},{1,9},{9,1},{17,25},{25,17},{2,10},{10... | collective-permute-start | bytes 1572872 | tf_op jit(solution)/shard_map/ppermute | solution.py:28
  304.0 26.0 %collective-permute-start.35 = (bf16[128,2048]{1,0:T(8,128)(2,1)S(1)}, bf16[128,2048]{1,0:T(8,128)(2,1)S(1)}, u32[]{:S(2)}, u32[]{:S(2)}) collective-permute-start(bf16[128,2048]{1,0:T(8,128)(2,1)S(1)} %get-tuple-element.135), channel_id=1, source_target_pairs={{0,16},{8,24},{16,0},{24,8},{1,17},{9,25},{17,1},{25,9},{2,18},{10... | collective-permute-start | bytes 1572872 | tf_op jit(solution)/shard_map/ppermute | solution.py:28
  305.5 24.5 %collective-permute-start.36 = (bf16[128,2048]{1,0:T(8,128)(2,1)S(1)}, bf16[128,2048]{1,0:T(8,128)(2,1)S(1)}, u32[]{:S(2)}, u32[]{:S(2)}) collective-permute-start(bf16[128,2048]{1,0:T(8,128)(2,1)S(1)} %get-tuple-element.134), channel_id=1, source_target_pairs={{0,24},{8,16},{16,8},{24,0},{1,25},{9,17},{17,9},{25,1},{2,26},{10... | collective-permute-start | bytes 1572872 | tf_op jit(solution)/shard_map/ppermute | solution.py:28
  306.3 29.8 %collective-permute-start.28 = (bf16[128,1408]{1,0:T(8,128)(2,1)S(1)}, bf16[128,1408]{1,0:T(8,128)(2,1)S(1)}, u32[]{:S(2)}, u32[]{:S(2)}) collective-permute-start(bf16[128,1408]{1,0:T(8,128)(2,1)S(1)} %get-tuple-element.138), channel_id=1, source_target_pairs={{0,8},{8,0},{16,24},{24,16},{1,9},{9,1},{17,25},{25,17},{2,10},{10... | collective-permute-start | bytes 1081352 | tf_op jit(solution)/shard_map/ppermute | solution.py:28
  308.0 36.7 %collective-permute-start.29 = (bf16[128,1408]{1,0:T(8,128)(2,1)S(1)}, bf16[128,1408]{1,0:T(8,128)(2,1)S(1)}, u32[]{:S(2)}, u32[]{:S(2)}) collective-permute-start(bf16[128,1408]{1,0:T(8,128)(2,1)S(1)} %get-tuple-element.140), channel_id=1, source_target_pairs={{0,16},{8,24},{16,0},{24,8},{1,17},{9,25},{17,1},{25,9},{2,18},{10... | collective-permute-start | bytes 1081352 | tf_op jit(solution)/shard_map/ppermute | solution.py:28
  317.0 27.7 %collective-permute-start.30 = (bf16[128,1408]{1,0:T(8,128)(2,1)S(1)}, bf16[128,1408]{1,0:T(8,128)(2,1)S(1)}, u32[]{:S(2)}, u32[]{:S(2)}) collective-permute-start(bf16[128,1408]{1,0:T(8,128)(2,1)S(1)} %get-tuple-element.139), channel_id=1, source_target_pairs={{0,24},{8,16},{16,8},{24,0},{1,25},{9,17},{17,9},{25,1},{2,26},{10... | collective-permute-start | bytes 1081352 | tf_op jit(solution)/shard_map/ppermute | solution.py:28
  345.8 27.0 %collective-permute-start.37 = (bf16[128,1664]{1,0:T(8,128)(2,1)S(1)}, bf16[128,1664]{1,0:T(8,128)(2,1)S(1)}, u32[]{:S(2)}, u32[]{:S(2)}) collective-permute-start(bf16[128,1664]{1,0:T(8,128)(2,1)S(1)} %concatenate.58), channel_id=1, source_target_pairs={{0,2},{1,3},{2,0},{3,1},{4,6},{5,7},{6,4},{7,5},{8,10},{9,11},{10,... | collective-permute-start | bytes 1277960 | tf_op jit(solution)/shard_map/ppermute | solution.py:32
  352.3 19.1 %collective-permute-start.32 = (bf16[128,384]{1,0:T(8,128)(2,1)S(1)}, bf16[128,384]{1,0:T(8,128)(2,1)S(1)}, u32[]{:S(2)}, u32[]{:S(2)}) collective-permute-start(bf16[128,384]{1,0:T(8,128)(2,1)S(1)} %add_convert_fusion), channel_id=1, source_target_pairs={{0,2},{1,3},{2,0},{3,1},{4,6},{5,7},{6,4},{7,5},{8,10},{9,11},{10,... | collective-permute-start | bytes 294920 | tf_op jit(solution)/shard_map/ppermute | solution.py:32
  (43 other events, 234.0 us)
Sparse Core Ops, SparseCore 0:
  161.3 97.3 all-gather.2
  267.5 80.0 all-gather.4

commit v3 on v2

--- a/solution.py
+++ b/solution.py
@@ -650,6 +650,10 @@
         misc = total[:, width:]
         total[:, width:] = jnp.where(iota(misc.shape, 1) == heads, norm, misc)
         spread_rows(out_ref, total, groups, cores)
+
+
+def pair_kernel(mine_ref, came_ref, after_ref, out_ref):
+    out_ref[...] = (mine_ref[...].astype(f32) + came_ref[...].astype(f32)).astype(bf16)
 
 
 def mixed_out_kernel(stats_ref, branch_ref, tok_ref, out_ref):
@@ -1168,7 +1172,6 @@
     )(tokens, model_gain, grads, extra, norm_sums, tail_part)
     first_grad = scatter_rows(first_grad)
     if shares > 1:
-        second_total = tied(second_total, mixed_out[:8, :LANES])
         tokens_grad = pl.pallas_call(
             add_kernel,
             grid=(all_rows // STRETCH,),
@@ -1204,7 +1207,15 @@
             ],
             axis=1,
         )
-        pair = (shared.astype(f32) + swap_tp(shared, 1).astype(f32)).astype(bf16)
+        pair = pl.pallas_call(
+            pair_kernel,
+            grid=(1,),
+            in_specs=[fixed(shared.shape)] * 2 + [pl.BlockSpec(memory_space=pl.ANY)],
+            out_specs=fixed(shared.shape),
+            out_shape=shape(*shared.shape, dtype=bf16),
+            compiler_params=params,
+            name="pair",
+        )(shared, swap_tp(shared, 1), tokens_grad)
         taps_pair = state_taps_grad + swap_tp(state_taps_grad, 1)
         came, few = swap_tp(sent, 2).astype(f32), swap_tp(few, 2)
         groups = [
@@ -1212,8 +1223,7 @@
         ]
         channel_total = channel_total + few[: CONV + 3, :own_inner]
         head_total = head_total[:, :own_heads] + few[:2, own_inner : own_inner + own_heads]
-        pair_more = tied(swap_tp(pair, 2), tokens_grad[:8, :LANES])
-        shared = pair.astype(f32) + pair_more.astype(f32)
+        shared = pair.astype(f32) + swap_tp(pair, 2).astype(f32)
         state_taps_grad = taps_pair + swap_tp(taps_pair, 2)
     else:
         shared = sum_tp_small(shared)

time: 399 us -> 419 us (1.050)
  waiting for transfers between devices: 85.9 us -> 92.8 us
  starting transfers between devices: 88.4 us -> 94.8 us
    ppermute x13, starting transfers between devices: 50.7 us -> 57.6 us  [swap_tp(): return lax.ppermute(x, 'tp', [(i, i ^ k) for i in range(4)])]
    ppermute x7, waiting for transfers between devices: 5.95 us -> 12 us  [shift_part(): return lax.ppermute(x, ('ctx', 'tp'), pairs)]
  transfers between devices with their start and end apart: 46 -> 46, of which waited for: 19 -> 19; matrix products, arithmetic and copies ran while one was open for 11% -> 11% of each run, Pallas kernels for 32% -> 33%
where the time goes in v3:
time: 419 us; the launch traced here: 411 us
  Pallas kernels  149 us (36%)
  starting transfers between devices  94.8 us (23%)
  waiting for transfers between devices  92.8 us (22%)
  local copies, waits for them, and re-layouts  36.1 us (9%)
  other arithmetic  20.2 us (5%)
  between operations  15.3 us (4%)
    ppermute x13, starting transfers between devices, swap_tp(): return lax.ppermute(x, 'tp', [(i, i ^ k) for i in range(4)])  57.6 us
    pallas_call x1, Pallas kernels, scan_piece(): pl.pallas_call(functools.partial(scan_back_kernel, dims, first, blocks, s...  44.2 us
    ppermute x17, waiting for transfers between devices, swap_fsdp(): return lax.ppermute(x, 'fsdp', [(i, i ^ k) for i in range(4)])  40.6 us
    ppermute x13, waiting for transfers between devices, swap_tp(): return lax.ppermute(x, 'tp', [(i, i ^ k) for i in range(4)])  36.4 us
    pallas_call x1, Pallas kernels, per_device(): pl.pallas_call(functools.partial(forward_kernel, dims, count, shares), gr...  25.2 us
    ppermute x17, starting transfers between devices, swap_fsdp(): return lax.ppermute(x, 'fsdp', [(i, i ^ k) for i in range(4)])  23.5 us
    pallas_call x1, Pallas kernels, per_device(): pl.pallas_call(functools.partial(gate_back_kernel, dims, shares), grid=(b...  14.3 us
    pallas_call x1, Pallas kernels, per_device(): pl.pallas_call(functools.partial(stats_kernel, dims, shares, parts - 1),...  12.1 us
  transfers between devices with their start and end apart: 46, of which 19 were waited for; matrix products, arithmetic and copies ran while one was open for 11% of the time, Pallas kernels for 33%

profile of v3, /device:TPU:0, one launch (start us, length us, event | category | flops | bytes accessed | tf_op | source)
XLA Modules:
  0.0 411.4 jit_solution(8413395257097714147)
XLA Ops:
  10.9 3.0 collective-permute-start
  17.6 3.1 collective-permute-start.4
  20.6 3.2 constant_dynamic-slice_fusion.7.refs_5_.refs_2_.tok_ref
  26.9 6.3 %collective-permute-done.4 = bf16[128,1152]{1,0:T(8,128)(2,1)} collective-permute-done((bf16[128,1152]{1,0:T(8,128)(2,1)S(1)}, bf16[128,1152]{1,0:T(8,128)(2,1)}, u32[]{:S(2)}, u32[]{:S(2)}) %collective-permute-start.4) | collective-permute-done | bytes 294944 | tf_op jit(solution)/shard_map/ppermute | solution.py:32
  42.4 3.0 collective-permute-done.9
  45.5 3.3 collective-permute-done.6
  57.2 25.2 %forward.1 = (bf16[1024,1280]{1,0:T(8,128)(2,1)}, bf16[1024,1280]{1,0:T(8,128)(2,1)}, f32[1024,1024]{1,0:T(8,128)}, f32[1024,128]{1,0:T(8,128)}, f32[1024,128]{1...) custom-call(s32[8]{0:T(128)} %broadcast_multiply_fusion.place_ref, ...), custom_call_target="tpu_custom_call" | custom-call | tf_op jit(solution)/shard_map/forward/pallas_call | solution.py:820
  91.2 10.1 %gates.1 = (f32[1024,1024]{1,0:T(8,128)}, f32[1024,1024]{1,0:T(8,128)}, bf16[1024,1024]{1,0:T(8,128)(2,1)}) custom-call(s32[8]{0:T(128)} %broadcast_multiply_fusion.place_ref, bf16[4,128,1024]{2,1,0:T(8,128)(2,1)} %copy-done.4, bf16[4,128,1024]{2,1,0:T(8,128)(2,1)} %copy-done.8, bf16[1024,1024]{1,0:T(8,128)(2,1)} %constant_dynamic-slice_fusion.7.refs_5_.refs_2_.tok_ref, ...), custom_call_target="tpu_custom_call" | custom-call | tf_op jit(solution)/shard_map/gates/pallas_call | solution.py:871
  102.3 12.1 %stats.1 = (f32[1024,1024]{1,0:T(8,128)}, bf16[4,1024,128]{2,1,0:T(8,128)(2,1)}, f32[2,1024]{1,0:T(2,128)}, bf16[1024,1024]{1,0:T(8,128)(2,1)}) custom-call(bf16[1040,128]{1,0:T(8,128)(2,1)} %copy-done.11, bf16[1040,128]{1,0:T(8,128)(2,1)} %copy-done.12, bf16[1040,128]{1,0:T(8,128)(2,1)} %copy-done.13, s32[4,1,256]{2,1,0:T(1,128)} %bitcast.85, ...), custom_call_target="tpu_custom_call" | custom-call | tf_op jit(solution)/shard_map/stats/pallas_call | solution.py:887
  114.4 4.9 %collective-permute-start.19 = (f32[2,1024]{1,0:T(2,128)}, f32[2,1024]{1,0:T(2,128)S(1)}, u32[]{:S(2)}, u32[]{:S(2)}) collective-permute-start(f32[2,1024]{1,0:T(2,128)} %get-tuple-element.74), channel_id=1, source_target_pairs={{0,1},{1,0},{2,3},{3,2},{4,5},{5,4},{6,7},{7,6},{8,9},{9,8},{10,11... | collective-permute-start | bytes 24584 | tf_op jit(solution)/shard_map/ppermute | solution.py:32
  125.8 14.3 %gate_back.1 = (bf16[1024,1024]{1,0:T(8,128)(2,1)}, bf16[1024,1024]{1,0:T(8,128)(2,1)}, bf16[1024,1024]{1,0:T(8,128)(2,1)}, f32[1024,128]{1,0:T(8,128)}, f32[4,1...) custom-call(s32[4,1,256]{2,1,0:T(1,128)} %bitcast.86, f32[2,1024]{1,0:T(2,128)} %add.172.stats_ref, ...), custom_call_target="tpu_custom_call" | custom-call | flops 1024 | bytes 1024 | tf_op jit(solution)/shard_map/gate_back/pallas_call | solution.py:945
  152.1 3.1 own_branch.1
  155.2 4.4 %collective-permute-done.21.refs_0_ = bf16[1040,128]{1,0:T(8,128)(2,1)S(1)} collective-permute-done((bf16[1040,128]{1,0:T(8,128)(2,1)}, bf16[1040,128]{1,0:T(8,128)(2,1)S(1)}, u32[]{:S(2)}, u32[]{:S(2)}) %collective-permute-start.21) | collective-permute-done | bytes 266272 | tf_op jit(solution)/shard_map/ppermute | solution.py:52
  163.9 44.2 %scan_back.1 = (bf16[1024,1024]{1,0:T(8,128)(2,1)}, f32[8,1280]{1,0:T(8,128)}, bf16[1024,1408]{1,0:T(8,128)(2,1)}, f32[8,1280]{1,0:T(8,128)}, f32[8,128]{1,0:T(8...) custom-call(s32[4,1,256]{2,1,0:T(1,128)} %bitcast.87, ...), custom_call_target="tpu_custom_call" | custom-call | flops 1024 | bytes 1024 | tf_op jit(solution)/shard_map/scan_back/pallas_call | solution.py:1041
  211.3 6.1 %collective-permute-done.25 = bf16[8,1280]{1,0:T(8,128)(2,1)S(1)} collective-permute-done((bf16[8,1280]{1,0:T(8,128)(2,1)S(1)}, bf16[8,1280]{1,0:T(8,128)(2,1)S(1)}, u32[]{:S(2)}, u32[]{:S(2)}) %collective-permute-start.25) | collective-permute-done | bytes 20512 | tf_op jit(solution)/shard_map/ppermute | solution.py:52
  217.3 3.2 fusion.29
  220.5 39.6 %collective-permute-start.26 = (bf16[16,1024]{1,0:T(8,128)(2,1)S(1)}, bf16[16,1024]{1,0:T(8,128)(2,1)S(1)}, u32[]{:S(2)}, u32[]{:S(2)}) collective-permute-start(bf16[16,1024]{1,0:T(8,128)(2,1)S(1)} %get-tuple-element.156), channel_id=1, source_target_pairs={{0,1},{1,0},{2,3},{3,2},{4,5},{5,4},{6,7},{7,6},{8,9},{9,8},{10,11... | collective-permute-start | bytes 98312 | tf_op jit(solution)/shard_map/ppermute | solution.py:32
  261.2 10.5 %first_grad.1 = bf16[2,4,128,2048]{3,2,1,0:T(8,128)(2,1)} custom-call(bf16[1024,1024]{1,0:T(8,128)(2,1)} %constant_dynamic-slice_fusion.7.refs_5_.refs_2_.tok_ref, f32[8,1024]{1,0:T(8,128)} %get-tuple-element.66.refs_3_.gain_ref, bf16[1024,1024]{1,0:T(8,128)(2,1)} %get-tuple-element.84.ggate_ref.gate_ref, ...), custom_call_target="tpu_custom_call" | custom-call | flops 1024 | bytes 1024 | tf_op jit(solution)/shard_map/first_grad/pallas_call | solution.py:1087
  272.3 3.3 own_rows.1
  275.6 3.2 dynamic-slice_bitcast_fusion
  279.4 3.6 collective-permute-done.38
  284.6 3.0 collective-permute-done.39
  293.5 9.0 %weight_grad.1 = bf16[2,4,128,1408]{3,2,1,0:T(8,128)(2,1)} custom-call(bf16[1024,1024]{1,0:T(8,128)(2,1)} %constant_dynamic-slice_fusion.7.refs_5_.refs_2_.tok_ref, f32[8,1024]{1,0:T(8,128)} %get-tuple-element.66.refs_3_.gain_ref, bf16[1024,1408]{1,0:T(8,128)(2,1)} %get-tuple-element.97.grads_ref, bf16[16,1280]{1,0:T(8,128)(2,1)} %fusion.17.extra_ref, ...), custom_call_target="tpu_custom_call" | custom-call | flops 1024 | bytes 1024 | tf_op jit(solution)/shard_map/weight_grad/pallas_call | solution.py:1155
  308.7 4.7 %collective-permute-done.43 = f32[5,256]{1,0:T(8,128)} collective-permute-done((f32[5,256]{1,0:T(8,128)S(1)}, f32[5,256]{1,0:T(8,128)}, u32[]{:S(2)}, u32[]{:S(2)}) %collective-permute-start.43) | collective-permute-done | bytes 5152 | tf_op jit(solution)/shard_map/ppermute | solution.py:32
  327.0 7.8 %collective-permute-done.34 = bf16[128,2048]{1,0:T(8,128)(2,1)S(1)} collective-permute-done((bf16[128,2048]{1,0:T(8,128)(2,1)S(1)}, bf16[128,2048]{1,0:T(8,128)(2,1)S(1)}, u32[]{:S(2)}, u32[]{:S(2)}) %collective-permute-start.34) | collective-permute-done | bytes 524320 | tf_op jit(solution)/shard_map/ppermute | solution.py:28
  337.2 10.4 %collective-permute-done.35 = bf16[128,2048]{1,0:T(8,128)(2,1)S(1)} collective-permute-done((bf16[128,2048]{1,0:T(8,128)(2,1)S(1)}, bf16[128,2048]{1,0:T(8,128)(2,1)S(1)}, u32[]{:S(2)}, u32[]{:S(2)}) %collective-permute-start.35) | collective-permute-done | bytes 524320 | tf_op jit(solution)/shard_map/ppermute | solution.py:28
  348.0 5.9 %collective-permute-done.28 = bf16[128,1408]{1,0:T(8,128)(2,1)S(1)} collective-permute-done((bf16[128,1408]{1,0:T(8,128)(2,1)S(1)}, bf16[128,1408]{1,0:T(8,128)(2,1)S(1)}, u32[]{:S(2)}, u32[]{:S(2)}) %collective-permute-start.28) | collective-permute-done | bytes 360480 | tf_op jit(solution)/shard_map/ppermute | solution.py:28
  353.8 7.9 %collective-permute-done.29 = bf16[128,1408]{1,0:T(8,128)(2,1)S(1)} collective-permute-done((bf16[128,1408]{1,0:T(8,128)(2,1)S(1)}, bf16[128,1408]{1,0:T(8,128)(2,1)S(1)}, u32[]{:S(2)}, u32[]{:S(2)}) %collective-permute-start.29) | collective-permute-done | bytes 360480 | tf_op jit(solution)/shard_map/ppermute | solution.py:28
  363.4 6.6 %mixed_out.1 = bf16[2048,1024]{1,0:T(8,128)(2,1)} custom-call(bf16[2048,1024]{1,0:T(8,128)(2,1)} %all-gather.3.cloned.1.call-done.in_ref), custom_call_target="tpu_custom_call" | custom-call | tf_op jit(solution)/shard_map/mixed_out/pallas_call | solution.py:985
  371.9 9.4 %collective-permute-done.37 = bf16[128,1664]{1,0:T(8,128)(2,1)S(1)} collective-permute-done((bf16[128,1664]{1,0:T(8,128)(2,1)S(1)}, bf16[128,1664]{1,0:T(8,128)(2,1)S(1)}, u32[]{:S(2)}, u32[]{:S(2)}) %collective-permute-start.37) | collective-permute-done | bytes 426016 | tf_op jit(solution)/shard_map/ppermute | solution.py:32
  383.1 9.0 %tokens_grad.1.after_ref = f32[2048,1024]{1,0:T(8,128)} custom-call(bf16[2048,1024]{1,0:T(8,128)(2,1)} %all-gather.5.cloned.1.call-done.a_ref, bf16[2048,1024]{1,0:T(8,128)(2,1)} %b_ref.1), custom_call_target="tpu_custom_call" | custom-call | tf_op jit(solution)/shard_map/tokens_grad/pallas_call | solution.py:1175
  395.1 6.7 %collective-permute-done.32 = bf16[128,384]{1,0:T(8,128)(2,1)S(1)} collective-permute-done((bf16[128,384]{1,0:T(8,128)(2,1)}, bf16[128,384]{1,0:T(8,128)(2,1)S(1)}, u32[]{:S(2)}, u32[]{:S(2)}) %collective-permute-start.32) | collective-permute-done | bytes 98336 | tf_op jit(solution)/shard_map/ppermute | solution.py:32
  (241 shorter events, 105.9 us)
Async XLA Ops:
  7.2 268.4 %all-gather.3.cloned.1.call-start = ((), (), s32[]{:S(2)}) async-start(), calls=%async_computation | async-start | bytes 5242880 | tf_op jit(solution)/shard_map/all_gather | solution.py:984
  10.9 25.4 %collective-permute-start = (bf16[128,1408]{1,0:T(8,128)(2,1)S(1)}, bf16[128,1408]{1,0:T(8,128)(2,1)S(1)}, u32[]{:S(2)}, u32[]{:S(2)}) collective-permute-start(bf16[128,1408]{1,0:T(8,128)(2,1)S(1)} %get-tuple-element.145), channel_id=1, source_target_pairs={{0,8},{8,0},{16,24},{24,16},{1,9},{9,1},{17,25},{25,17},{2,10},{10... | collective-permute-start | bytes 1081352 | tf_op jit(solution)/shard_map/ppermute | solution.py:28
  13.9 23.6 %collective-permute-start.1 = (bf16[128,1408]{1,0:T(8,128)(2,1)S(1)}, bf16[128,1408]{1,0:T(8,128)(2,1)S(1)}, u32[]{:S(2)}, u32[]{:S(2)}) collective-permute-start(bf16[128,1408]{1,0:T(8,128)(2,1)S(1)} %get-tuple-element.145), channel_id=1, source_target_pairs={{0,16},{8,24},{16,0},{24,8},{1,17},{9,25},{17,1},{25,9},{2,18},{10... | collective-permute-start | bytes 1081352 | tf_op jit(solution)/shard_map/ppermute | solution.py:28
  15.4 22.1 %collective-permute-start.2 = (bf16[128,1408]{1,0:T(8,128)(2,1)S(1)}, bf16[128,1408]{1,0:T(8,128)(2,1)S(1)}, u32[]{:S(2)}, u32[]{:S(2)}) collective-permute-start(bf16[128,1408]{1,0:T(8,128)(2,1)S(1)} %get-tuple-element.145), channel_id=1, source_target_pairs={{0,24},{8,16},{16,8},{24,0},{1,25},{9,17},{17,9},{25,1},{2,26},{10... | collective-permute-start | bytes 1081352 | tf_op jit(solution)/shard_map/ppermute | solution.py:28
  17.6 15.7 %collective-permute-start.4 = (bf16[128,1152]{1,0:T(8,128)(2,1)S(1)}, bf16[128,1152]{1,0:T(8,128)(2,1)}, u32[]{:S(2)}, u32[]{:S(2)}) collective-permute-start(bf16[128,1152]{1,0:T(8,128)(2,1)S(1)} %fusion.9), channel_id=1, source_target_pairs={{0,2},{1,3},{2,0},{3,1},{4,6},{5,7},{6,4},{7,5},{8,10},{9,11},{10,... | collective-permute-start | bytes 884744 | tf_op jit(solution)/shard_map/ppermute | solution.py:32
  35.7 13.0 %collective-permute-start.6 = (bf16[128,1152]{1,0:T(8,128)(2,1)}, bf16[128,1152]{1,0:T(8,128)(2,1)}, u32[]{:S(2)}, u32[]{:S(2)}) collective-permute-start(bf16[128,1152]{1,0:T(8,128)(2,1)} %collective-permute-done.4), channel_id=1, source_target_pairs={{0,8},{8,0},{16,24},{24,16},{1,9},{9,1},{17,25},{25,17},{2,10},{10... | collective-permute-start | bytes 884744 | tf_op jit(solution)/shard_map/ppermute | solution.py:28
  36.3 12.5 %collective-permute-start.7 = (bf16[128,1152]{1,0:T(8,128)(2,1)}, bf16[128,1152]{1,0:T(8,128)(2,1)}, u32[]{:S(2)}, u32[]{:S(2)}) collective-permute-start(bf16[128,1152]{1,0:T(8,128)(2,1)} %collective-permute-done.4), channel_id=1, source_target_pairs={{0,16},{8,24},{16,0},{24,8},{1,17},{9,25},{17,1},{25,9},{2,18},{10... | collective-permute-start | bytes 884744 | tf_op jit(solution)/shard_map/ppermute | solution.py:28
  42.4 14.8 %collective-permute-start.3 = (bf16[4,128,1408]{2,1,0:T(8,128)(2,1)S(1)}, bf16[4,128,1408]{2,1,0:T(8,128)(2,1)}, u32[]{:S(2)}, u32[]{:S(2)}) collective-permute-start(bf16[4,128,1408]{2,1,0:T(8,128)(2,1)S(1)} %pad_maximum_fusion.refs_0_), channel_id=1, source_target_pairs={{0,4},{4,0},{1,5},{5,1},{2,6},{6,2},{3,7},{7,3},{8,12},{12,8},{9,1... | collective-permute-start | bytes 4325384 | tf_op jit(solution)/shard_map/ppermute | solution.py:24
  51.7 30.7 %collective-permute-start.17 = (bf16[128,1024]{1,0:T(8,128)(2,1)S(1)}, bf16[128,1024]{1,0:T(8,128)(2,1)S(1)}, u32[]{:S(2)}, u32[]{:S(2)}) collective-permute-start(bf16[128,1024]{1,0:T(8,128)(2,1)S(1)} %pad_maximum_fusion.5), channel_id=1, source_target_pairs={{0,24},{8,16},{16,8},{24,0},{1,25},{9,17},{17,9},{25,1},{2,26},{10... | collective-permute-start | bytes 786440 | tf_op jit(solution)/shard_map/ppermute | solution.py:28
  54.1 28.3 %collective-permute-start.15 = (bf16[128,1024]{1,0:T(8,128)(2,1)S(1)}, bf16[128,1024]{1,0:T(8,128)(2,1)}, u32[]{:S(2)}, u32[]{:S(2)}) collective-permute-start(bf16[128,1024]{1,0:T(8,128)(2,1)S(1)} %pad_maximum_fusion.5), channel_id=1, source_target_pairs={{0,8},{8,0},{16,24},{24,16},{1,9},{9,1},{17,25},{25,17},{2,10},{10... | collective-permute-start | bytes 786440 | tf_op jit(solution)/shard_map/ppermute | solution.py:28
  54.7 27.8 %collective-permute-start.16 = (bf16[128,1024]{1,0:T(8,128)(2,1)S(1)}, bf16[128,1024]{1,0:T(8,128)(2,1)}, u32[]{:S(2)}, u32[]{:S(2)}) collective-permute-start(bf16[128,1024]{1,0:T(8,128)(2,1)S(1)} %pad_maximum_fusion.5), channel_id=1, source_target_pairs={{0,16},{8,24},{16,0},{24,8},{1,17},{9,25},{17,1},{25,9},{2,18},{10... | collective-permute-start | bytes 786440 | tf_op jit(solution)/shard_map/ppermute | solution.py:28
  83.8 17.6 %collective-permute-start.12 = (bf16[1040,128]{1,0:T(8,128)(2,1)S(1)}, bf16[1040,128]{1,0:T(8,128)(2,1)S(1)}, u32[]{:S(2)}, u32[]{:S(2)}) collective-permute-start(bf16[1040,128]{1,0:T(8,128)(2,1)S(1)} %copy-done.34), channel_id=1, source_target_pairs={{0,2},{1,3},{2,4},{3,5},{4,6},{5,7},{8,10},{9,11},{10,12},{11,13},... | collective-permute-start | bytes 798728 | tf_op jit(solution)/shard_map/ppermute | solution.py:52
  85.2 16.2 %collective-permute-start.13 = (bf16[1040,128]{1,0:T(8,128)(2,1)S(1)}, bf16[1040,128]{1,0:T(8,128)(2,1)S(1)}, u32[]{:S(2)}, u32[]{:S(2)}) collective-permute-start(bf16[1040,128]{1,0:T(8,128)(2,1)S(1)} %copy-done.34), channel_id=1, source_target_pairs={{0,4},{1,5},{2,6},{3,7},{8,12},{9,13},{10,14},{11,15},{16,20},{17,... | collective-permute-start | bytes 798728 | tf_op jit(solution)/shard_map/ppermute | solution.py:52
  88.1 13.3 %collective-permute-start.14 = (bf16[1040,128]{1,0:T(8,128)(2,1)S(1)}, bf16[1040,128]{1,0:T(8,128)(2,1)S(1)}, u32[]{:S(2)}, u32[]{:S(2)}) collective-permute-start(bf16[1040,128]{1,0:T(8,128)(2,1)S(1)} %copy-done.34), channel_id=1, source_target_pairs={{0,6},{1,7},{8,14},{9,15},{16,22},{17,23},{24,30},{25,31}} | collective-permute-start | bytes 798728 | tf_op jit(solution)/shard_map/ppermute | solution.py:52
  123.8 27.4 %collective-permute-start.20 = (bf16[512,1024]{1,0:T(8,128)(2,1)S(1)}, bf16[512,1024]{1,0:T(8,128)(2,1)S(1)}, u32[]{:S(2)}, u32[]{:S(2)}) collective-permute-start(bf16[512,1024]{1,0:T(8,128)(2,1)S(1)} %constant_dynamic-slice_fusion.4), channel_id=1, source_target_pairs={{0,1},{1,0},{2,3},{3,2},{4,5},{5,4},{6,7},{7,6},{8,9},{9,8},{10,11... | collective-permute-start | bytes 3145736 | tf_op jit(solution)/shard_map/ppermute | solution.py:32
  140.2 19.4 %collective-permute-start.21 = (bf16[1040,128]{1,0:T(8,128)(2,1)}, bf16[1040,128]{1,0:T(8,128)(2,1)S(1)}, u32[]{:S(2)}, u32[]{:S(2)}) collective-permute-start(bf16[1040,128]{1,0:T(8,128)(2,1)} %get-tuple-element.79), channel_id=1, source_target_pairs={{2,0},{3,1},{4,2},{5,3},{6,4},{7,5},{10,8},{11,9},{12,10},{13,11},... | collective-permute-start | bytes 798728 | tf_op jit(solution)/shard_map/ppermute | solution.py:52
  141.6 18.0 %collective-permute-start.22 = (bf16[1040,128]{1,0:T(8,128)(2,1)}, bf16[1040,128]{1,0:T(8,128)(2,1)S(1)}, u32[]{:S(2)}, u32[]{:S(2)}) collective-permute-start(bf16[1040,128]{1,0:T(8,128)(2,1)} %get-tuple-element.79), channel_id=1, source_target_pairs={{4,0},{5,1},{6,2},{7,3},{12,8},{13,9},{14,10},{15,11},{20,16},{21,... | collective-permute-start | bytes 798728 | tf_op jit(solution)/shard_map/ppermute | solution.py:52
  142.9 18.3 %collective-permute-start.23 = (bf16[1040,128]{1,0:T(8,128)(2,1)}, bf16[1040,128]{1,0:T(8,128)(2,1)S(1)}, u32[]{:S(2)}, u32[]{:S(2)}) collective-permute-start(bf16[1040,128]{1,0:T(8,128)(2,1)} %get-tuple-element.79), channel_id=1, source_target_pairs={{6,0},{7,1},{14,8},{15,9},{22,16},{23,17},{30,24},{31,25}} | collective-permute-start | bytes 798728 | tf_op jit(solution)/shard_map/ppermute | solution.py:52
  161.2 221.9 %all-gather.5.cloned.1.call-start = ((), (), s32[]{:S(2)}) async-start(), calls=%async_computation.1 | async-start | bytes 5242880 | tf_op jit(solution)/shard_map/all_gather | solution.py:1128
  209.6 62.6 %collective-permute-start.24 = (bf16[512,1024]{1,0:T(8,128)(2,1)S(1)}, bf16[512,1024]{1,0:T(8,128)(2,1)}, u32[]{:S(2)}, u32[]{:S(2)}) collective-permute-start(bf16[512,1024]{1,0:T(8,128)(2,1)S(1)} %constant_dynamic-slice_fusion.1), channel_id=1, source_target_pairs={{0,1},{1,0},{2,3},{3,2},{4,5},{5,4},{6,7},{7,6},{8,9},{9,8},{10,11... | collective-permute-start | bytes 3145736 | tf_op jit(solution)/shard_map/ppermute | solution.py:32
  220.5 51.1 %collective-permute-start.26 = (bf16[16,1024]{1,0:T(8,128)(2,1)S(1)}, bf16[16,1024]{1,0:T(8,128)(2,1)S(1)}, u32[]{:S(2)}, u32[]{:S(2)}) collective-permute-start(bf16[16,1024]{1,0:T(8,128)(2,1)S(1)} %get-tuple-element.156), channel_id=1, source_target_pairs={{0,1},{1,0},{2,3},{3,2},{4,5},{5,4},{6,7},{7,6},{8,9},{9,8},{10,11... | collective-permute-start | bytes 98312 | tf_op jit(solution)/shard_map/ppermute | solution.py:32
  278.8 38.6 %collective-permute-start.33 = (bf16[4,128,2048]{2,1,0:T(8,128)(2,1)}, bf16[4,128,2048]{2,1,0:T(8,128)(2,1)S(1)}, u32[]{:S(2)}, u32[]{:S(2)}) collective-permute-start(bf16[4,128,2048]{2,1,0:T(8,128)(2,1)} %dynamic-slice_bitcast_fusion), channel_id=1, source_target_pairs={{0,4},{4,0},{1,5},{5,1},{2,6},{6,2},{3,7},{7,3},{8,12},{12,8},{9,1... | collective-permute-start | bytes 6291464 | tf_op jit(solution)/shard_map/ppermute | solution.py:24
  293.5 21.3 %collective-permute-start.41 = (f32[8,640]{1,0:T(8,128)}, f32[8,640]{1,0:T(8,128)}, u32[]{:S(2)}, u32[]{:S(2)}) collective-permute-start(f32[8,640]{1,0:T(8,128)} %select_maximum_fusion.1), channel_id=1, source_target_pairs={{0,2},{1,3},{2,0},{3,1},{4,6},{5,7},{6,4},{7,5},{8,10},{9,11},{10,... | collective-permute-start | bytes 61448 | tf_op jit(solution)/shard_map/ppermute | solution.py:32
  305.1 18.4 %collective-permute-start.27 = (bf16[4,128,1408]{2,1,0:T(8,128)(2,1)}, bf16[4,128,1408]{2,1,0:T(8,128)(2,1)S(1)}, u32[]{:S(2)}, u32[]{:S(2)}) collective-permute-start(bf16[4,128,1408]{2,1,0:T(8,128)(2,1)} %dynamic-slice_bitcast_fusion.1), channel_id=1, source_target_pairs={{0,4},{4,0},{1,5},{5,1},{2,6},{6,2},{3,7},{7,3},{8,12},{12,8},{9,1... | collective-permute-start | bytes 4325384 | tf_op jit(solution)/shard_map/ppermute | solution.py:24
  320.0 14.9 %collective-permute-start.34 = (bf16[128,2048]{1,0:T(8,128)(2,1)S(1)}, bf16[128,2048]{1,0:T(8,128)(2,1)S(1)}, u32[]{:S(2)}, u32[]{:S(2)}) collective-permute-start(bf16[128,2048]{1,0:T(8,128)(2,1)S(1)} %get-tuple-element.133), channel_id=1, source_target_pairs={{0,8},{8,0},{16,24},{24,16},{1,9},{9,1},{17,25},{25,17},{2,10},{10... | collective-permute-start | bytes 1572872 | tf_op jit(solution)/shard_map/ppermute | solution.py:28
  321.5 26.1 %collective-permute-start.35 = (bf16[128,2048]{1,0:T(8,128)(2,1)S(1)}, bf16[128,2048]{1,0:T(8,128)(2,1)S(1)}, u32[]{:S(2)}, u32[]{:S(2)}) collective-permute-start(bf16[128,2048]{1,0:T(8,128)(2,1)S(1)} %get-tuple-element.135), channel_id=1, source_target_pairs={{0,16},{8,24},{16,0},{24,8},{1,17},{9,25},{17,1},{25,9},{2,18},{10... | collective-permute-start | bytes 1572872 | tf_op jit(solution)/shard_map/ppermute | solution.py:28
  323.0 24.6 %collective-permute-start.36 = (bf16[128,2048]{1,0:T(8,128)(2,1)S(1)}, bf16[128,2048]{1,0:T(8,128)(2,1)S(1)}, u32[]{:S(2)}, u32[]{:S(2)}) collective-permute-start(bf16[128,2048]{1,0:T(8,128)(2,1)S(1)} %get-tuple-element.134), channel_id=1, source_target_pairs={{0,24},{8,16},{16,8},{24,0},{1,25},{9,17},{17,9},{25,1},{2,26},{10... | collective-permute-start | bytes 1572872 | tf_op jit(solution)/shard_map/ppermute | solution.py:28
  324.0 29.8 %collective-permute-start.28 = (bf16[128,1408]{1,0:T(8,128)(2,1)S(1)}, bf16[128,1408]{1,0:T(8,128)(2,1)S(1)}, u32[]{:S(2)}, u32[]{:S(2)}) collective-permute-start(bf16[128,1408]{1,0:T(8,128)(2,1)S(1)} %get-tuple-element.138), channel_id=1, source_target_pairs={{0,8},{8,0},{16,24},{24,16},{1,9},{9,1},{17,25},{25,17},{2,10},{10... | collective-permute-start | bytes 1081352 | tf_op jit(solution)/shard_map/ppermute | solution.py:28
  325.5 36.2 %collective-permute-start.29 = (bf16[128,1408]{1,0:T(8,128)(2,1)S(1)}, bf16[128,1408]{1,0:T(8,128)(2,1)S(1)}, u32[]{:S(2)}, u32[]{:S(2)}) collective-permute-start(bf16[128,1408]{1,0:T(8,128)(2,1)S(1)} %get-tuple-element.140), channel_id=1, source_target_pairs={{0,16},{8,24},{16,0},{24,8},{1,17},{9,25},{17,1},{25,9},{2,18},{10... | collective-permute-start | bytes 1081352 | tf_op jit(solution)/shard_map/ppermute | solution.py:28
  334.8 26.9 %collective-permute-start.30 = (bf16[128,1408]{1,0:T(8,128)(2,1)S(1)}, bf16[128,1408]{1,0:T(8,128)(2,1)S(1)}, u32[]{:S(2)}, u32[]{:S(2)}) collective-permute-start(bf16[128,1408]{1,0:T(8,128)(2,1)S(1)} %get-tuple-element.139), channel_id=1, source_target_pairs={{0,24},{8,16},{16,8},{24,0},{1,25},{9,17},{17,9},{25,1},{2,26},{10... | collective-permute-start | bytes 1081352 | tf_op jit(solution)/shard_map/ppermute | solution.py:28
  362.1 19.2 %collective-permute-start.37 = (bf16[128,1664]{1,0:T(8,128)(2,1)S(1)}, bf16[128,1664]{1,0:T(8,128)(2,1)S(1)}, u32[]{:S(2)}, u32[]{:S(2)}) collective-permute-start(bf16[128,1664]{1,0:T(8,128)(2,1)S(1)} %concatenate.58), channel_id=1, source_target_pairs={{0,2},{1,3},{2,0},{3,1},{4,6},{5,7},{6,4},{7,5},{8,10},{9,11},{10,... | collective-permute-start | bytes 1277960 | tf_op jit(solution)/shard_map/ppermute | solution.py:32
  370.0 22.0 %collective-permute-start.31 = (bf16[128,384]{1,0:T(8,128)(2,1)S(1)}, bf16[128,384]{1,0:T(8,128)(2,1)S(1)}, u32[]{:S(2)}, u32[]{:S(2)}) collective-permute-start(bf16[128,384]{1,0:T(8,128)(2,1)S(1)} %slice.218.mine_ref), channel_id=1, source_target_pairs={{0,1},{1,0},{2,3},{3,2},{4,5},{5,4},{6,7},{7,6},{8,9},{9,8},{10,11... | collective-permute-start | bytes 294920 | tf_op jit(solution)/shard_map/ppermute | solution.py:32
  (49 other events, 329.5 us)
Sparse Core Ops, SparseCore 0:
  161.3 97.3 all-gather.2
  275.7 80.0 all-gather.4
